TPU v7x, 512 devices: a whole 4x8x8 slice. The times are simulated.
512 devices in a mesh: blk: 32 (over y, x_lo, core), head: 16 (over z, x_hi).
Axes of the slice: x: 4 (x_hi: 2, x_lo: 2; x = x_hi * 2 + x_lo), y: 8, z: 8, core: 2. Of those that a mesh axis runs over, the one named last changes fastest.
Arguments:
- tokens: bfloat16 [8, 4096, 768], P(None, ('blk', 'head')), may hold values from -6 to 6
- chain_id: int32 [4096], P(('blk', 'head')), may hold values from 0 to 3, never falling along the last dimension, each value on 1 to 2048 neighbouring positions
- hotspots: int32 [16], replicated, may hold values from 0 to 4095
- chain_embed: bfloat16 [4, 768], replicated, may hold values from -6 to 6
- hot_embed: bfloat16 [768], replicated, may hold values from -6 to 6
- w_proj: bfloat16 [768, 3072], P(None, 'head'), may hold values from -0.21875 to 0.21875
- pair_bias: bfloat16 [16, 4096, 4096], P('head', 'blk'), may hold values from -400 to 400
- w_out: bfloat16 [768, 768], P('head'), may hold values from -0.21875 to 0.21875
Outputs:
- update: bfloat16 [8, 4096, 768], P(None, ('blk', 'head'))
Inputs may be any that keep to these rules, and one draw needn't show every extreme that they name: `chain_id`: chain ids never fall along the tokens; one chain has exactly 2048 tokens. `hotspots`: positions may repeat.
All inputs are finite; a program needn't handle non-finite values.
Results may differ from a plain program's by a relative error of at most 0.02.
Values may be sent and summed in bfloat16 or wider, within the bound.
No kernel may reach another device: no remote copies, remote signals or barrier semaphores. Data moves between devices by JAX's collectives and lax.ppermute only.
A program may use at most 64 MiB of HBM per device.

v0:
```python
import jax
import jax.numpy as jnp
from jax import lax
from jax.sharding import PartitionSpec as P

HD = 48


def attend_keys(state, queries, key_blk, value_blk, bias_blk):
    row_max, row_sum, weighted = state
    scores = jnp.einsum("sqhd,shdk->shqk", queries, key_blk, preferred_element_type=jnp.float32)
    scores = scores + bias_blk.astype(jnp.float32)[None]
    new_max = jnp.maximum(row_max, jnp.max(scores, axis=-1))
    rescale = jnp.exp(row_max - new_max)
    probs = jnp.exp(scores - new_max[..., None])
    row_sum = row_sum * rescale + jnp.sum(probs, axis=-1)
    partial_out = jnp.einsum(
        "shqk,shdk->shqd", probs.astype(jnp.bfloat16), value_blk, preferred_element_type=jnp.float32
    )
    weighted = weighted * rescale[..., None] + partial_out
    return (new_max, row_sum, weighted)


def body(tokens, chain_id, hotspots, chain_embed, hot_embed, w_proj, pair_bias, w_out):
    samples, tok_dev, width = tokens.shape
    groups = lax.axis_size("head")
    first_tok = (lax.axis_index("blk") * groups + lax.axis_index("head")) * tok_dev
    positions = first_tok + jnp.arange(tok_dev, dtype=jnp.int32)
    is_hot = jnp.any(positions[:, None] == hotspots[None, :], axis=1).astype(jnp.float32)
    onehot = (
        chain_id[:, None] == jnp.arange(chain_embed.shape[0], dtype=jnp.int32)[None, :]
    ).astype(jnp.float32)
    condition = jnp.sum(onehot[:, :, None] * chain_embed.astype(jnp.float32)[None], axis=1)
    condition = condition + is_hot[:, None] * hot_embed.astype(jnp.float32)[None, :]
    shifted = tokens.astype(jnp.float32) + condition[None]
    average = jnp.mean(shifted, axis=-1, keepdims=True)
    spread = jnp.mean((shifted - average) ** 2, axis=-1, keepdims=True)
    normed = ((shifted - average) * lax.rsqrt(spread + 1e-05)).astype(jnp.bfloat16)
    block_tokens = lax.all_gather(normed, "head", axis=1, tiled=True)
    tok_blk = block_tokens.shape[1]
    heads_here = w_proj.shape[1] // (4 * HD)
    proj = jnp.dot(
        block_tokens.reshape(samples * tok_blk, width), w_proj, preferred_element_type=jnp.float32
    )
    proj = proj.reshape(samples, tok_blk, heads_here, 4, HD)
    queries = (proj[:, :, :, 0] * (1.0 / HD**0.5)).astype(jnp.bfloat16)
    keys_t = jnp.transpose(proj[:, :, :, 1], (0, 2, 3, 1)).astype(jnp.bfloat16)
    values_t = jnp.transpose(proj[:, :, :, 2], (0, 2, 3, 1)).astype(jnp.bfloat16)
    gating = jax.nn.sigmoid(proj[:, :, :, 3])
    start_state = (
        jnp.full((samples, heads_here, tok_blk), -jnp.inf, jnp.float32),
        jnp.zeros((samples, heads_here, tok_blk), jnp.float32),
        jnp.zeros((samples, heads_here, tok_blk, HD), jnp.float32),
    )
    key_part = lax.all_gather(keys_t, "blk", axis=3, tiled=True)
    value_part = lax.all_gather(values_t, "blk", axis=3, tiled=True)
    key_rows = key_part.shape[3]
    block_size = 512
    count = key_rows // block_size
    key_blocks = jnp.moveaxis(key_part.reshape(samples, heads_here, HD, count, block_size), 3, 0)
    value_blocks = jnp.moveaxis(
        value_part.reshape(samples, heads_here, HD, count, block_size), 3, 0
    )
    bias_blocks = jnp.moveaxis(pair_bias.reshape(heads_here, tok_blk, count, block_size), 2, 0)

    def scan_body(inner, blocks_in):
        return (attend_keys(inner, queries, blocks_in[0], blocks_in[1], blocks_in[2]), None)

    final, unused = lax.scan(scan_body, start_state, (key_blocks, value_blocks, bias_blocks))
    row_max, row_sum, weighted = final
    attended = jnp.transpose(weighted / row_sum[..., None], (0, 2, 1, 3))
    gated = (attended * gating).astype(jnp.bfloat16).reshape(samples, tok_blk, heads_here * HD)
    summed = lax.psum_scatter(
        jnp.einsum("std,de->tse", gated, w_out, preferred_element_type=jnp.float32).astype(
            jnp.bfloat16
        ),
        "head",
        scatter_dimension=0,
        tiled=True,
    ).astype(jnp.float32)
    update = jnp.transpose(summed, (1, 0, 2))
    return update.astype(jnp.bfloat16)


def solution(mesh):
    in_specs = (
        P(None, ("blk", "head"), None),
        P(("blk", "head")),
        P(),
        P(),
        P(),
        P(None, "head"),
        P("head", "blk", None),
        P("head", None),
    )
    out_specs = P(None, ("blk", "head"), None)
    return jax.shard_map(body, mesh=mesh, in_specs=in_specs, out_specs=out_specs, check_vma=False)
```

profile of v0, /device:TPU:1, one launch (start us, length us, event | category | flops | bytes accessed | tf_op | source)
XLA Modules:
  0.0 505.8 jit_solution(421765054528312035)
XLA Ops:
  6.5 0.0 copy-start
  6.5 0.0 all-gather.4.cloned.1.call-start
  6.5 0.9 compare_reduce_fusion
  7.4 0.7 convert_element_type.81
  8.1 0.7 fusion.36
  8.8 0.7 convert_element_type.83
  9.5 0.1 multiply_reduce_fusion.1
  9.6 0.1 multiply_add_fusion
  9.6 1.0 fusion.29
  10.6 1.1 multiply_reduce_fusion
  11.8 1.6 multiply_convert_fusion
  13.4 0.0 all-gather.4.cloned.1.call-update
  13.4 0.0 all-gather.8.cloned.1.call-start
  13.5 90.5 %all-gather.4.cloned.1.call-done = bf16[8,128,768]{2,1,0:T(8,128)(2,1)} async-done(((bf16[8,8,768]{2,1,0:T(8,128)(2,1)}), bf16[8,128,768]{2,1,0:T(8,128)(2,1)}) %all-gather.4.cloned.1.call-update) | async-done | bytes 1572880 | tf_op jit(solution)/shard_map/all_gather | solution.py:39
  104.0 0.0 copy-done
  104.0 2.1 fusion.38
  106.1 0.8 slice_bitcast_fusion
  106.8 0.0 all-gather.8.cloned.1.call-update
  106.8 0.0 all-gather.6.cloned.1.call-start
  106.9 0.7 all-gather.6.cloned.1.call-update
  107.6 0.0 reduce-scatter.4.cloned.1.call-start
  107.7 1.3 copy.19
  109.0 69.4 %all-gather.8.cloned.1.call-done = bf16[8,1,48,4096]{3,2,0,1:T(8,128)(2,1)} async-done(((bf16[8,1,48,128]{3,2,0,1:T(8,128)(2,1)}), bf16[8,1,48,4096]{3,2,0,1:T(8,128)(2,1)}) %all-gather.8.cloned.1.call-update) | async-done | bytes 3145744 | tf_op jit(solution)/shard_map/all_gather | solution.py:56
  178.4 4.0 copy.30
  182.4 0.0 copy-done.1
  182.4 68.9 %all-gather.6.cloned.1.call-done = bf16[8,1,48,4096]{3,2,0,1:T(8,128)(2,1)} async-done(((bf16[8,1,48,128]{3,2,0,1:T(8,128)(2,1)}), bf16[8,1,48,4096]{3,2,0,1:T(8,128)(2,1)}) %all-gather.6.cloned.1.call-update) | async-done | bytes 3145744 | tf_op jit(solution)/shard_map/all_gather | solution.py:55
  251.3 4.1 copy.31
  255.3 35.5 %while.15 = (s32[]{:T(128)}, f32[8,1,128]{2,0,1:T(8,128)S(1)}, f32[8,1,128]{2,0,1:T(8,128)S(1)}, f32[8,1,128,48]{2,3,0,1:T(8,128)S(1)}, bf16[8,8,1,48,512]{4,3,1...) while((s32[]{:T(128)}, f32[8,1,128]{2,0,1:T(8,128)S(1)}, ...), condition=%wide.region_7.8_spmd.clone, body=%wide.region_4.7_spmd.clone.sunk | while | flops 105076736 | bytes 8815733 | solution.py:69
  255.3 1.0 bitcast_convert_fusion.2
  256.3 1.5 fusion.48
  257.8 1.6 fusion.51
  259.4 0.4 fusion.50
  259.8 0.9 bitcast_convert_fusion.2
  260.7 1.5 fusion.48
  262.3 1.5 fusion.51
  263.8 0.4 fusion.50
  264.2 0.9 bitcast_convert_fusion.2
  265.2 1.5 fusion.48
  266.7 1.5 fusion.51
  268.3 0.4 fusion.50
  268.7 0.9 bitcast_convert_fusion.2
  269.6 1.5 fusion.48
  271.1 1.5 fusion.51
  272.7 0.4 fusion.50
  273.1 0.9 bitcast_convert_fusion.2
  274.0 1.5 fusion.48
  275.6 1.5 fusion.51
  277.1 0.4 fusion.50
  277.5 0.9 bitcast_convert_fusion.2
  278.5 1.5 fusion.48
  280.0 1.6 fusion.51
  281.6 0.4 fusion.50
  282.0 0.9 bitcast_convert_fusion.2
  282.9 1.5 fusion.48
  284.4 1.6 fusion.51
  286.0 0.4 fusion.50
  286.4 0.9 bitcast_convert_fusion.2
  287.3 1.5 fusion.48
  288.9 1.5 fusion.51
  290.4 0.4 fusion.50
  290.8 1.6 fusion.18
  292.4 1.3 copy.27
  293.7 0.0 reduce-scatter.4.cloned.1.call-update
  293.8 205.5 %reduce-scatter.4.cloned.1.call-done = bf16[8,6144]{1,0:T(8,128)(2,1)} async-done(((bf16[128,6144]{1,0:T(8,128)(2,1)}), bf16[8,6144]{1,0:T(8,128)(2,1)}) %reduce-scatter.4.cloned.1.call-update) | async-done | bytes 98320
  (37 shorter events, 0.2 us)
Async XLA Ops:
  6.5 97.4 %copy-start = (bf16[768,192]{0,1:T(8,128)(2,1)S(1)}, bf16[768,192]{0,1:T(8,128)(2,1)}, u32[]{:S(2)}) copy-start(bf16[768,192]{0,1:T(8,128)(2,1)} %param.15) | copy-start | bytes 884740
  6.5 97.4 %all-gather.4.cloned.1.call-start = ((), (), s32[]{:S(2)}) async-start(), calls=%async_computation.1 | async-start | bytes 1671168 | tf_op jit(solution)/shard_map/all_gather | solution.py:39
  10.6 97.0 %copy-start.2 = (bf16[1,128,4096]{2,1,0:T(8,128)(2,1)S(1)}, bf16[1,128,4096]{2,1,0:T(8,128)(2,1)}, u32[]{:S(2)}) copy-start(bf16[1,128,4096]{2,1,0:T(8,128)(2,1)} %param.16) | copy-start | bytes 3145732
  13.4 164.9 %all-gather.8.cloned.1.call-start = ((), (), s32[]{:S(2)}) async-start(), calls=%async_computation.3 | async-start | bytes 3244032 | tf_op jit(solution)/shard_map/all_gather | solution.py:56
  106.1 76.4 %copy-start.1 = (f32[8,128,1,4,48]{1,4,3,0,2:T(8,128)}, f32[8,128,1,4,48]{1,4,3,0,2:T(8,128)S(1)}, u32[]{:S(2)}) copy-start(f32[8,128,1,4,48]{1,4,3,0,2:T(8,128)S(1)} %get-tuple-element.100) | copy-start | bytes 2359300
  106.8 144.4 %all-gather.6.cloned.1.call-start = ((), (), s32[]{:S(2)}) async-start(), calls=%async_computation.2 | async-start | bytes 3244032 | tf_op jit(solution)/shard_map/all_gather | solution.py:55
  107.6 391.7 %reduce-scatter.4.cloned.1.call-start = ((), (), s32[]{:S(2)}) async-start(), calls=%async_computation.4 | async-start | bytes 1671168
  255.3 35.5 %copy-start.3 = (bf16[48,768]{1,0:T(8,128)(2,1)S(1)}, bf16[48,768]{1,0:T(8,128)(2,1)}, u32[]{:S(2)}) copy-start(bf16[48,768]{1,0:T(8,128)(2,1)} %param.17) | copy-start | bytes 221188
Sparse Core Ops, SparseCore 0:
  13.6 90.3 all-gather.3
  107.0 71.3 all-gather.7
  180.5 70.7 all-gather.5
  293.9 205.3 reduce-scatter.3
where the time goes:
time: 511 us; the launch traced here: 506 us
  waiting for transfers between devices  435 us (85%)
  matrix products  28.2 us (6%)
  other arithmetic  17.4 us (3%)
  between operations  13.2 us (3%)
  local copies, waits for them, and re-layouts  11.5 us (2%)
    unnamed x5, waiting for transfers between devices  206 us
    all_gather x1, waiting for transfers between devices, body(): block_tokens = lax.all_gather(normed, 'head', axis=1, tiled=True)  90.5 us
    all_gather x1, waiting for transfers between devices, body(): value_part = lax.all_gather(values_t, 'blk', axis=3, tiled=True)  69.4 us
    all_gather x1, waiting for transfers between devices, body(): key_part = lax.all_gather(keys_t, 'blk', axis=3, tiled=True)  68.9 us
    dot_general x8, matrix products, attend_keys(): jnp.einsum('shqk,shdk->shqd', probs.astype(jnp.bfloat16), value_blk, pref...  12.4 us
    dot_general x8, matrix products, attend_keys(): jnp.einsum('sqhd,shdk->shqk', queries, key_blk, preferred_element_type=jn...  12.2 us
  transfers between devices with their start and end apart: 4, of which 4 were waited for; matrix products, arithmetic and copies ran while one was open for 1% of the time, Pallas kernels for 0%

commit v1 on v0

v1 whole, which is shorter than its diff:
```python
import functools

import jax
import jax.numpy as jnp
import numpy as np
from jax import lax
from jax.experimental import pallas as pl
from jax.experimental.pallas import tpu as pltpu
from jax.sharding import Mesh
from jax.sharding import PartitionSpec as P

HD = 48
AXES = ("y", "xlo", "core", "z", "xhi")
SIZES = (8, 2, 2, 8, 2)
HEADS = ("z", "xhi")
QUAD = ("xlo", "core")
F32, BF16 = jnp.float32, jnp.bfloat16
VMEM = 56 * 1024 * 1024


def params():
    return pltpu.CompilerParams(vmem_limit_bytes=VMEM)


def norm_kernel(first_ref, chain_ref, hot_ref, tok_ref, emb_ref, hemb_ref, out_ref):
    samples, tok_dev, width = tok_ref.shape
    first = first_ref[0]
    emb = emb_ref[...].astype(F32)
    hemb = hemb_ref[...].astype(F32)
    row_of = lax.broadcasted_iota(jnp.int32, (tok_dev, width), 0)
    cond = jnp.zeros((tok_dev, width), F32)
    for t in range(tok_dev):
        chain = chain_ref[t]
        row = jnp.zeros((1, width), F32)
        for c in range(emb_ref.shape[0]):
            row = row + jnp.where(chain == c, 1.0, 0.0) * emb[c : c + 1]
        hits = jnp.int32(0)
        for i in range(hot_ref.shape[0]):
            hits = hits + jnp.where(hot_ref[i] == first + t, 1, 0)
        row = row + jnp.where(hits > 0, 1.0, 0.0) * hemb
        cond = cond + jnp.where(row_of == t, row, 0.0)
    shifted = tok_ref[...].astype(F32) + cond[None]
    average = jnp.mean(shifted, axis=-1, keepdims=True)
    centred = shifted - average
    spread = jnp.mean(centred * centred, axis=-1, keepdims=True)
    normed = (centred * lax.rsqrt(spread + 1e-05)).reshape(samples * tok_dev, width).astype(BF16)
    for g in range(out_ref.shape[0]):
        out_ref[g] = normed


def proj_kernel(x_ref, wt_ref, q_ref, kv_ref, gate_ref):
    peers, rows, width = x_ref.shape
    samples = q_ref.shape[0]
    tok = rows // samples
    full = lax.dot_general(
        x_ref[...].reshape(peers * rows, width), wt_ref[...], (((1,), (1,)), ((), ())), preferred_element_type=F32
    ).reshape(peers, samples, tok, 4 * HD)
    for s in range(samples):
        one = full[:, s].reshape(peers * tok, 4 * HD)
        turned = jnp.transpose(one)
        q_ref[s] = (turned[:HD] * (1.0 / HD**0.5)).astype(BF16)
        kv_ref[s] = turned[HD : 3 * HD].astype(BF16)
        gate_ref[s] = jax.nn.sigmoid(turned[3 * HD :])


def attend_kernel(role_ref, q_ref, b0_ref, b1_ref, *refs):
    kv_refs, out_ref = refs[:-1], refs[-1]
    me, yy = role_ref[0], role_ref[1]
    keys = jnp.concatenate([r[0, :HD] for r in kv_refs], axis=1)
    vals = jnp.concatenate([r[0, HD:] for r in kv_refs], axis=1)
    shifts = (0, -1, 1, -2, 2, -3, 3, -4)
    lane = lax.broadcasted_iota(jnp.int32, (128, 128), 1)
    for role in range(4):
        src = b0_ref if role < 2 else b1_ref
        j = jnp.bitwise_xor(me, role)
        queries = jnp.transpose(q_ref[j, 0].astype(F32)).astype(BF16)
        scores = jnp.dot(queries, keys, preferred_element_type=F32)
        bias = [src[role % 2, lax.rem(yy + 8 + sh, 8)].astype(F32) for sh in shifts]
        scores = scores + jnp.concatenate(bias, axis=1)
        top = jnp.max(scores, axis=1, keepdims=True)
        probs = jnp.exp(scores - top)
        total = jnp.sum(probs, axis=1, keepdims=True)
        part = lax.dot_general(probs.astype(BF16), vals, (((1,), (1,)), ((), ())), preferred_element_type=F32)
        part = part / total
        lse = top + jnp.log(total)
        hi = lse.astype(BF16).astype(F32)
        mid = (lse - hi).astype(BF16).astype(F32)
        low = lse - hi - mid
        wide = jnp.concatenate([part, jnp.zeros((128, 128 - HD), F32)], axis=1)
        wide = jnp.where(lane == HD, hi, jnp.where(lane == HD + 1, mid, jnp.where(lane == HD + 2, low, wide)))
        out_ref[j, 0] = jnp.transpose(wide)[:64].astype(BF16)


def merge_kernel(p_ref, gate_ref, out_ref, wide_ref):
    parts, samples = p_ref.shape[:2]
    peers = out_ref.shape[0]
    for s in range(samples):
        rows = [p_ref[i, s].astype(F32) for i in range(parts)]
        lse = [r[HD : HD + 1] + r[HD + 1 : HD + 2] + r[HD + 2 : HD + 3] for r in rows]
        top = functools.reduce(jnp.maximum, lse)
        weight = [jnp.exp(v - top) for v in lse]
        mixed = sum(w * r[:HD] for w, r in zip(weight, rows)) / sum(weight) * gate_ref[s]
        wide = jnp.concatenate([mixed, jnp.zeros((128 - HD, 128), F32)], axis=0)
        turned = jnp.transpose(wide)
        tok = turned.shape[0] // peers
        wide_ref[:, s * tok : (s + 1) * tok] = turned.reshape(peers, tok, 128)
    out_ref[...] = wide_ref[:, :, :HD].astype(BF16)


def out_kernel(g_ref, w_ref, out_ref):
    heads = g_ref.shape[0]
    total = jnp.zeros(out_ref.shape, F32)
    for h in range(heads):
        total = total + jnp.dot(g_ref[h], w_ref[h], preferred_element_type=F32)
    out_ref[...] = total.astype(BF16)


def shift(x, axis, by):
    n = SIZES[AXES.index(axis)]
    return lax.ppermute(x, axis, [(i, (i + by) % n) for i in range(n)])


def half(x, dim, index):
    return lax.dynamic_index_in_dim(x, index, dim, keepdims=False)


def body(tokens, chain_id, hotspots, chain_embed, hot_embed, w_proj, pair_bias, w_out):
    samples, tok_dev, width = tokens.shape
    peers = lax.axis_size(HEADS)
    block = peers * tok_dev
    xlo, core, yy = lax.axis_index("xlo"), lax.axis_index("core"), lax.axis_index("y")
    first = (lax.axis_index(("y", "xlo", "core")) * peers + lax.axis_index(HEADS)) * tok_dev
    vm = pl.BlockSpec(memory_space=pltpu.VMEM)
    sm = pl.BlockSpec(memory_space=pltpu.SMEM)

    bias = pair_bias.reshape(block, 8, 2, 2, block)
    keep = jnp.transpose(half(bias, 3, core), (2, 1, 0, 3))
    away = jnp.transpose(half(bias, 3, 1 - core), (2, 1, 0, 3))
    pair = jnp.stack([keep, shift(away, "core", 1)], axis=1)
    bias0 = half(pair, 0, xlo)
    bias1 = shift(half(pair, 0, 1 - xlo), "xlo", 1)

    copies = pl.pallas_call(
        norm_kernel,
        out_shape=jax.ShapeDtypeStruct((peers, samples * tok_dev, width), BF16),
        in_specs=[sm, sm, sm, vm, vm, vm],
        out_specs=vm,
        compiler_params=params(),
    )(first[None], chain_id, hotspots, tokens, chain_embed, hot_embed[None])
    gathered = lax.all_to_all(copies, HEADS, split_axis=0, concat_axis=0, tiled=True)
    q_t, kv_t, gate_t = pl.pallas_call(
        proj_kernel,
        out_shape=(
            jax.ShapeDtypeStruct((samples, HD, block), BF16),
            jax.ShapeDtypeStruct((samples, 2 * HD, block), BF16),
            jax.ShapeDtypeStruct((samples, HD, block), F32),
        ),
        in_specs=[vm, vm],
        out_specs=(vm, vm, vm),
        compiler_params=params(),
    )(gathered, jnp.transpose(w_proj))

    w_mine, kv_t = lax.optimization_barrier((w_out, kv_t))
    w_full = lax.all_gather(w_mine, HEADS, axis=0)

    right, left, ring = kv_t, kv_t, [kv_t]
    for step in range(4):
        right = shift(right, "y", 1)
        ring.append(right)
        if step < 3:
            left = shift(left, "y", -1)
            ring.append(left)
    q_all = lax.all_gather(q_t, QUAD, axis=0)

    def per_sample(dims):
        return pl.BlockSpec((1,) + dims, lambda s, role: (s,) + (0,) * len(dims))

    def quad(dims):
        return pl.BlockSpec((4, 1) + dims, lambda s, role: (0, s) + (0,) * len(dims))

    whole = pl.BlockSpec((2, 8, block, block), lambda s, role: (0, 0, 0, 0))
    parts = pl.pallas_call(
        attend_kernel,
        out_shape=jax.ShapeDtypeStruct((4, samples, 64, block), BF16),
        grid_spec=pltpu.PrefetchScalarGridSpec(
            num_scalar_prefetch=1,
            grid=(samples,),
            in_specs=[quad((HD, block)), whole, whole] + [per_sample((2 * HD, block))] * 8,
            out_specs=quad((64, block)),
        ),
        compiler_params=params(),
    )(jnp.stack([xlo * 2 + core, yy]), q_all, bias0, bias1, *ring)
    mine = lax.all_to_all(parts, QUAD, split_axis=0, concat_axis=0, tiled=True)
    gated = pl.pallas_call(
        merge_kernel,
        out_shape=jax.ShapeDtypeStruct((peers, samples * tok_dev, HD), BF16),
        in_specs=[vm, vm],
        out_specs=vm,
        scratch_shapes=[pltpu.VMEM((peers, samples * tok_dev, 128), F32)],
        compiler_params=params(),
    )(mine, gate_t)
    heads = lax.all_to_all(gated, HEADS, split_axis=0, concat_axis=0, tiled=True)
    update = pl.pallas_call(
        out_kernel,
        out_shape=jax.ShapeDtypeStruct((samples * tok_dev, width), BF16),
        in_specs=[vm, vm],
        out_specs=vm,
        compiler_params=params(),
    )(heads, w_full)
    return update.reshape(samples, tok_dev, width)


def solution(mesh):
    fine = Mesh(np.asarray(mesh.devices).reshape(SIZES), AXES)
    blk = ("y", "xlo", "core")
    in_specs = (
        P(None, AXES, None),
        P(AXES),
        P(),
        P(),
        P(),
        P(None, HEADS),
        P(HEADS, blk, None),
        P(HEADS, None),
    )
    return jax.shard_map(body, mesh=fine, in_specs=in_specs, out_specs=P(None, AXES, None), check_vma=False)
```

time: 511 us -> 173 us (0.34)
  waiting for transfers between devices: 435 us -> 4.16 us
  blocking collectives: 0 us -> 87.4 us
  starting transfers between devices: 0.12 us -> 29.2 us
  matrix products: 28.2 us -> 0 us
  Pallas kernels: 0 us -> 25.2 us
  other arithmetic: 17.4 us -> 1.5 us
    all_gather x3 -> x1, waiting for transfers between devices: 229 us -> 0.01 us  [body(): w_full = lax.all_gather(w_mine, HEADS, axis=0)]
    unnamed x5 -> x1, waiting for transfers between devices: 206 us -> 0.02 us
    all_to_all x0 -> x3, blocking collectives: none -> 78.3 us  [the longest x1 53.1 us: body(): lax.all_to_all(copies, HEADS, split_axis=0, concat_axis=0, tiled=True)]
    ppermute x0 -> x9, starting transfers between devices: none -> 29.2 us  [shift(): return lax.ppermute(x, axis, [(i, (i + by) % n) for i in range(n)])]
    dot_general x18 -> x0, matrix products: 28.2 us -> none  [the longest x8 12.4 us: attend_keys(): jnp.einsum('shqk,shdk->shqd', probs.astype(jnp.bfloat16), value_blk, pref...]
    pallas_call x0 -> x5, Pallas kernels: none -> 25.2 us  [the longest x1 14.9 us: body(): pl.pallas_call(attend_kernel, out_shape=jax.ShapeDtypeStruct((4, samples,...]
    all_gather x0 -> x1, blocking collectives: none -> 9.11 us  [body(): q_all = lax.all_gather(q_t, QUAD, axis=0)]
    add x18 -> x0, other arithmetic: 7.61 us -> none  [the longest x8 7.44 us: attend_keys(): scores = scores + bias_blk.astype(jnp.float32)[None]]
  transfers between devices with their start and end apart: 4 -> 10, of which waited for: 4 -> 2; matrix products, arithmetic and copies ran while one was open for 1% -> 4% of each run, Pallas kernels for 0% -> 10%
where the time goes in v1:
time: 173 us; the launch traced here: 169 us
  blocking collectives  87.4 us (51%)
  starting transfers between devices  29.2 us (17%)
  Pallas kernels  25.2 us (15%)
  between operations  13.7 us (8%)
  local copies, waits for them, and re-layouts  8.08 us (5%)
  waiting for transfers between devices  4.16 us (2%)
    all_to_all x1, blocking collectives, body(): lax.all_to_all(copies, HEADS, split_axis=0, concat_axis=0, tiled=True)  53.1 us
    ppermute x9, starting transfers between devices, shift(): return lax.ppermute(x, axis, [(i, (i + by) % n) for i in range(n)])  29.2 us
    pallas_call x1, Pallas kernels, body(): pl.pallas_call(attend_kernel, out_shape=jax.ShapeDtypeStruct((4, samples,...  14.9 us
    all_to_all x1, blocking collectives, body(): lax.all_to_all(gated, HEADS, split_axis=0, concat_axis=0, tiled=True)  12.7 us
    all_to_all x1, blocking collectives, body(): mine = lax.all_to_all(parts, QUAD, split_axis=0, concat_axis=0, tiled=True)  12.5 us
    all_gather x1, blocking collectives, body(): q_all = lax.all_gather(q_t, QUAD, axis=0)  9.11 us
    ppermute x9, waiting for transfers between devices, shift(): return lax.ppermute(x, axis, [(i, (i + by) % n) for i in range(n)])  4.14 us
  transfers between devices with their start and end apart: 10, of which 2 were waited for; matrix products, arithmetic and copies ran while one was open for 4% of the time, Pallas kernels for 10%

profile of v1, /device:TPU:1, one launch (start us, length us, event | category | flops | bytes accessed | tf_op | source)
XLA Modules:
  0.0 169.2 jit_solution(10617812677402343372)
XLA Ops:
  6.5 0.0 all-gather.4.cloned.1.call-start
  6.5 1.3 broadcast_in_dim.7.hemb_ref
  7.8 2.6 %shard_map.82 = bf16[16,64,768]{2,1,0:T(8,128)(2,1)} custom-call(s32[1]{0:T(128)} %bitcast.2.first_ref, s32[8]{0:T(128)} %chain_ref.1, s32[16]{0:T(128)} %hot_ref.1, bf16[8,8,768]{2,1,0:T(8,128)(2,1)} %tok_ref.1, bf16[4,768]{1,0:T(4,128)(2,1)} %emb_ref.1, bf16[1,768]{1,0:T(2,128)(2,1)} %broadcast_in_dim.7.hemb_ref), custom_call_target="tpu_custom_call" | custom-call | tf_op jit(solution)/shard_map/pallas_call | solution.py:143
  10.4 53.1 %all_to_all.15.x_ref = bf16[16,64,768]{2,1,0:T(8,128)(2,1)} all-to-all(bf16[16,64,768]{2,1,0:T(8,128)(2,1)} %shard_map.82), channel_id=1, replica_groups=mesh['y'=8,'xlo'=2,'core'=2,'z'=8,'xhi'=2] {'z','xhi'}, dimensions={0} | all-to-all | bytes 3145728 | tf_op jit(solution)/shard_map/all_to_all | solution.py:150
  63.5 0.0 copy-start
  63.5 3.1 %shard_map.83 = (bf16[8,48,128]{2,1,0:T(8,128)(2,1)}, bf16[8,96,128]{2,1,0:T(8,128)(2,1)}, f32[8,48,128]{2,1,0:T(8,128)}) custom-call(bf16[16,64,768]{2,1,0:T(8,128)(2,1)} %all_to_all.15.x_ref, bf16[192,768]{1,0:T(8,128)(2,1)} %bitcast.33), custom_call_target="tpu_custom_call" | custom-call | tf_op jit(solution)/shard_map/pallas_call | solution.py:151
  66.6 0.0 all-gather.4.cloned.1.call-update
  66.6 0.0 copy-done
  66.7 0.8 reshape.6
  67.4 2.2 %constant_dynamic-slice_fusion = (bf16[128,8,2,1,128]{4,3,2,1,0:T(2,128)(2,1)S(1)}, bf16[128,8,2,1,128]{4,3,2,1,0:T(2,128)(2,1)S(1)}) fusion(bf16[128,8,2,2,128]{4,3,2,1,0:T(2,128)(2,1)S(1)} %reshape.6, s32[]{:T(128)S(6)} %select_n.15, s32[]{:T(128)S(6)} %select_n.14), kind=kLoop, calls=%fused_computation.10 | loop fusion | bytes 2097160 | tf_op jit(solution)/shard_map/jit(dynamic_index_in_dim)/dynamic_slice | solution.py:124
  69.6 0.0 copy-start.2
  69.6 0.3 copy.17
  70.0 4.4 %collective-permute-start = (bf16[2,8,128,128]{3,2,1,0:T(8,128)(2,1)S(1)}, bf16[2,8,128,128]{3,2,1,0:T(8,128)(2,1)S(1)}, u32[]{:S(2)}, u32[]{:S(2)}) collective-permute-start(bf16[2,8,128,128]{3,2,1,0:T(8,128)(2,1)S(1)} %bitcast.31), channel_id=1, source_target_pairs={{0,16},{16,0},{1,17},{17,1},{2,18},{18,2},{3,19},{19,3},{4,20},{20... | collective-permute-start | bytes 1572872 | tf_op jit(solution)/shard_map/ppermute | solution.py:120
  74.4 0.0 copy-done.2
  74.4 3.2 %collective-permute-start.2 = (bf16[8,96,128]{2,1,0:T(8,128)(2,1)S(1)}, bf16[8,96,128]{2,1,0:T(8,128)(2,1)S(1)}, u32[]{:S(2)}, u32[]{:S(2)}) collective-permute-start(bf16[8,96,128]{2,1,0:T(8,128)(2,1)S(1)} %copy-done.2), channel_id=1, source_target_pairs={{0,64},{64,128},{128,192},{192,256},{256,320},{320,384},{384,448},... | collective-permute-start | bytes 589832 | tf_op jit(solution)/shard_map/ppermute | solution.py:120
  77.6 0.0 copy-start.10
  77.6 0.3 copy.18
  78.0 3.8 %collective-permute-start.3 = (bf16[8,96,128]{2,1,0:T(8,128)(2,1)S(1)}, bf16[8,96,128]{2,1,0:T(8,128)(2,1)S(1)}, u32[]{:S(2)}, u32[]{:S(2)}) collective-permute-start(bf16[8,96,128]{2,1,0:T(8,128)(2,1)S(1)} %copy-done.2), channel_id=1, source_target_pairs={{0,448},{64,0},{128,64},{192,128},{256,192},{320,256},{384,320},{4... | collective-permute-start | bytes 589832 | tf_op jit(solution)/shard_map/ppermute | solution.py:120
  81.8 3.0 %collective-permute-done.2.refs_1_ = bf16[8,96,128]{2,1,0:T(8,128)(2,1)S(1)} collective-permute-done((bf16[8,96,128]{2,1,0:T(8,128)(2,1)S(1)}, bf16[8,96,128]{2,1,0:T(8,128)(2,1)S(1)}, u32[]{:S(2)}, u32[]{:S(2)}) %collective-permute-start.2) | collective-permute-done | bytes 196640 | tf_op jit(solution)/shard_map/ppermute | solution.py:120
  84.8 0.0 copy-start.3
  84.8 1.9 %collective-permute-start.4 = (bf16[8,96,128]{2,1,0:T(8,128)(2,1)S(1)}, bf16[8,96,128]{2,1,0:T(8,128)(2,1)S(1)}, u32[]{:S(2)}, u32[]{:S(2)}) collective-permute-start(bf16[8,96,128]{2,1,0:T(8,128)(2,1)S(1)} %collective-permute-done.2.refs_1_), channel_id=1, source_target_pairs={{0,64},{64,128},{128,192},{192,256},{256,320},{320,384},{384,448},... | collective-permute-start | bytes 589832 | tf_op jit(solution)/shard_map/ppermute | solution.py:120
  86.8 0.0 collective-permute-done
  86.8 0.9 fusion.1
  87.7 2.1 %collective-permute-start.1 = (bf16[2,8,128,128]{3,2,1,0:T(8,128)(2,1)S(1)}, bf16[2,8,128,128]{3,2,1,0:T(8,128)(2,1)S(1)}, u32[]{:S(2)}, u32[]{:S(2)}) collective-permute-start(bf16[2,8,128,128]{3,2,1,0:T(8,128)(2,1)S(1)} %get-tuple-element.15), channel_id=1, source_target_pairs={{0,32},{32,0},{1,33},{33,1},{2,34},{34,2},{3,35},{35,3},{4,36},{36... | collective-permute-start | bytes 1572872 | tf_op jit(solution)/shard_map/ppermute | solution.py:120
  89.8 0.0 collective-permute-done.3.refs_2_
  89.8 0.0 copy-start.4
  89.8 4.6 %collective-permute-start.5 = (bf16[8,96,128]{2,1,0:T(8,128)(2,1)S(1)}, bf16[8,96,128]{2,1,0:T(8,128)(2,1)S(1)}, u32[]{:S(2)}, u32[]{:S(2)}) collective-permute-start(bf16[8,96,128]{2,1,0:T(8,128)(2,1)S(1)} %collective-permute-done.3.refs_2_), channel_id=1, source_target_pairs={{0,448},{64,0},{128,64},{192,128},{256,192},{320,256},{384,320},{4... | collective-permute-start | bytes 589832 | tf_op jit(solution)/shard_map/ppermute | solution.py:120
  94.4 0.0 collective-permute-done.4.refs_3_
  94.4 0.0 copy-start.5
  94.4 1.9 %collective-permute-start.6 = (bf16[8,96,128]{2,1,0:T(8,128)(2,1)S(1)}, bf16[8,96,128]{2,1,0:T(8,128)(2,1)S(1)}, u32[]{:S(2)}, u32[]{:S(2)}) collective-permute-start(bf16[8,96,128]{2,1,0:T(8,128)(2,1)S(1)} %collective-permute-done.4.refs_3_), channel_id=1, source_target_pairs={{0,64},{64,128},{128,192},{192,256},{256,320},{320,384},{384,448},... | collective-permute-start | bytes 589832 | tf_op jit(solution)/shard_map/ppermute | solution.py:120
  96.4 1.1 collective-permute-done.5.refs_4_
  97.4 0.0 copy-start.6
  97.4 5.3 %collective-permute-start.7 = (bf16[8,96,128]{2,1,0:T(8,128)(2,1)S(1)}, bf16[8,96,128]{2,1,0:T(8,128)(2,1)S(1)}, u32[]{:S(2)}, u32[]{:S(2)}) collective-permute-start(bf16[8,96,128]{2,1,0:T(8,128)(2,1)S(1)} %collective-permute-done.5.refs_4_), channel_id=1, source_target_pairs={{0,448},{64,0},{128,64},{192,128},{256,192},{320,256},{384,320},{4... | collective-permute-start | bytes 589832 | tf_op jit(solution)/shard_map/ppermute | solution.py:120
  102.8 0.0 collective-permute-done.6.refs_5_
  102.8 0.0 copy-start.7
  102.8 1.9 %collective-permute-start.8 = (bf16[8,96,128]{2,1,0:T(8,128)(2,1)S(1)}, bf16[8,96,128]{2,1,0:T(8,128)(2,1)S(1)}, u32[]{:S(2)}, u32[]{:S(2)}) collective-permute-start(bf16[8,96,128]{2,1,0:T(8,128)(2,1)S(1)} %collective-permute-done.6.refs_5_), channel_id=1, source_target_pairs={{0,64},{64,128},{128,192},{192,256},{256,320},{320,384},{384,448},... | collective-permute-start | bytes 589832 | tf_op jit(solution)/shard_map/ppermute | solution.py:120
  104.7 0.6 pad_add_fusion.role_ref
  105.3 0.0 copy-done.10
  105.3 9.1 %all-gather = bf16[32,48,128]{2,1,0:T(8,128)(2,1)} all-gather(bf16[8,48,128]{2,1,0:T(8,128)(2,1)S(1)} %copy-done.10), channel_id=2, replica_groups=mesh['y'=8,'xlo'=2,'core'=2,'z'=8,'xhi'=2] {'xlo','core'}, dimensions={0}, use_global_device_ids=true | all-gather | bytes 491520 | tf_op jit(solution)/shard_map/all_gather | solution.py:173
  114.4 0.0 collective-permute-done.1.b1_ref
  114.4 0.0 copy-start.1
  114.4 0.0 collective-permute-done.7.refs_6_
  114.4 0.0 copy-start.8
  114.4 0.0 collective-permute-done.8.refs_7_
  114.4 0.0 copy-start.9
  114.5 0.0 copy-done.3
  114.5 0.0 copy-done.4
  114.5 0.0 copy-done.5
  114.5 0.0 copy-done.6
  114.5 0.0 copy-done.7
  114.5 0.7 copy-done.1
  115.2 0.1 copy-done.8
  115.3 0.1 copy-done.9
  115.4 14.9 %shard_map.84 = bf16[4,8,64,128]{3,2,1,0:T(8,128)(2,1)} custom-call(s32[2]{0:T(128)} %pad_add_fusion.role_ref, bf16[4,8,48,128]{3,2,1,0:T(8,128)(2,1)} %bitcast.27, bf16[2,8,128,128]{3,2,1,0:T(8,128)(2,1)} %get-tuple-element.16.b0_ref, bf16[2,8,128,128]{3,2,1,0:T(8,128)(2,1)} %copy-done.1, bf16[8,96,128]{2,1,0:T(8,128)(2,1)} %get-tuple-element.12.refs_0_, ...), custom_call_target="tpu_custom_call" | custom-call | tf_op jit(solution)/shard_map/pallas_call | solution.py:182
  130.3 12.5 %all_to_all.16.p_ref = bf16[4,8,64,128]{3,2,1,0:T(8,128)(2,1)} all-to-all(bf16[4,8,64,128]{3,2,1,0:T(8,128)(2,1)} %shard_map.84), channel_id=1, replica_groups=mesh['y'=8,'xlo'=2,'core'=2,'z'=8,'xhi'=2] {'xlo','core'}, dimensions={0} | all-to-all | bytes 1048576 | tf_op jit(solution)/shard_map/all_to_all | solution.py:193
  142.8 2.0 %shard_map.85 = bf16[16,64,48]{2,1,0:T(8,128)(2,1)} custom-call(bf16[4,8,64,128]{3,2,1,0:T(8,128)(2,1)} %all_to_all.16.p_ref, f32[8,48,128]{2,1,0:T(8,128)} %get-tuple-element.13.gate_ref), custom_call_target="tpu_custom_call" | custom-call | tf_op jit(solution)/shard_map/pallas_call | solution.py:194
  144.8 1.1 copy.13
  145.9 0.2 reshape.10
  146.1 12.7 %all_to_all.17 = bf16[16,2,1536]{2,1,0:T(2,128)(2,1)S(1)} all-to-all(bf16[16,2,1536]{2,1,0:T(2,128)(2,1)S(1)} %reshape.10), channel_id=1, replica_groups=mesh['y'=8,'xlo'=2,'core'=2,'z'=8,'xhi'=2] {'z','xhi'}, dimensions={0} | all-to-all | bytes 196608 | tf_op jit(solution)/shard_map/all_to_all | solution.py:202
  158.8 0.2 reshape.11
  158.9 0.9 copy.14.g_ref
  159.8 0.0 all-gather.4.cloned.1.call-done
  159.8 2.5 %shard_map.86 = bf16[64,768]{1,0:T(8,128)(2,1)} custom-call(bf16[16,64,48]{2,1,0:T(8,128)(2,1)} %copy.14.g_ref, bf16[16,48,768]{2,1,0:T(8,128)(2,1)} %bitcast.28), custom_call_target="tpu_custom_call" | custom-call | tf_op jit(solution)/shard_map/pallas_call | solution.py:203
Async XLA Ops:
  6.5 153.2 %all-gather.4.cloned.1.call-start = ((), (), s32[]{:S(2)}) async-start(), calls=%async_computation.3 | async-start | bytes 1253376 | tf_op jit(solution)/shard_map/all_gather | solution.py:164
  63.5 3.2 %copy-start = (bf16[1,128,4096]{2,1,0:T(8,128)(2,1)S(1)}, bf16[1,128,4096]{2,1,0:T(8,128)(2,1)}, u32[]{:S(2)}) copy-start(bf16[1,128,4096]{2,1,0:T(8,128)(2,1)} %param.14) | copy-start | bytes 3145732
  69.6 4.8 %copy-start.2 = (bf16[8,96,128]{2,1,0:T(8,128)(2,1)S(1)}, bf16[8,96,128]{2,1,0:T(8,128)(2,1)}, u32[]{:S(2)}) copy-start(bf16[8,96,128]{2,1,0:T(8,128)(2,1)} %get-tuple-element.12.refs_0_) | copy-start | bytes 589828
  70.0 16.8 %collective-permute-start = (bf16[2,8,128,128]{3,2,1,0:T(8,128)(2,1)S(1)}, bf16[2,8,128,128]{3,2,1,0:T(8,128)(2,1)S(1)}, u32[]{:S(2)}, u32[]{:S(2)}) collective-permute-start(bf16[2,8,128,128]{3,2,1,0:T(8,128)(2,1)S(1)} %bitcast.31), channel_id=1, source_target_pairs={{0,16},{16,0},{1,17},{17,1},{2,18},{18,2},{3,19},{19,3},{4,20},{20... | collective-permute-start | bytes 1572872 | tf_op jit(solution)/shard_map/ppermute | solution.py:120
  74.4 10.4 %collective-permute-start.2 = (bf16[8,96,128]{2,1,0:T(8,128)(2,1)S(1)}, bf16[8,96,128]{2,1,0:T(8,128)(2,1)S(1)}, u32[]{:S(2)}, u32[]{:S(2)}) collective-permute-start(bf16[8,96,128]{2,1,0:T(8,128)(2,1)S(1)} %copy-done.2), channel_id=1, source_target_pairs={{0,64},{64,128},{128,192},{192,256},{256,320},{320,384},{384,448},... | collective-permute-start | bytes 589832 | tf_op jit(solution)/shard_map/ppermute | solution.py:120
  77.6 27.7 %copy-start.10 = (bf16[8,48,128]{2,1,0:T(8,128)(2,1)S(1)}, bf16[8,48,128]{2,1,0:T(8,128)(2,1)}, u32[]{:S(2)}) copy-start(bf16[8,48,128]{2,1,0:T(8,128)(2,1)} %get-tuple-element.10) | copy-start | bytes 294916
  78.0 11.8 %collective-permute-start.3 = (bf16[8,96,128]{2,1,0:T(8,128)(2,1)S(1)}, bf16[8,96,128]{2,1,0:T(8,128)(2,1)S(1)}, u32[]{:S(2)}, u32[]{:S(2)}) collective-permute-start(bf16[8,96,128]{2,1,0:T(8,128)(2,1)S(1)} %copy-done.2), channel_id=1, source_target_pairs={{0,448},{64,0},{128,64},{192,128},{256,192},{320,256},{384,320},{4... | collective-permute-start | bytes 589832 | tf_op jit(solution)/shard_map/ppermute | solution.py:120
  84.8 29.6 %copy-start.3 = (bf16[8,96,128]{2,1,0:T(8,128)(2,1)}, bf16[8,96,128]{2,1,0:T(8,128)(2,1)S(1)}, u32[]{:S(2)}) copy-start(bf16[8,96,128]{2,1,0:T(8,128)(2,1)S(1)} %collective-permute-done.2.refs_1_) | copy-start | bytes 589828
  84.8 9.6 %collective-permute-start.4 = (bf16[8,96,128]{2,1,0:T(8,128)(2,1)S(1)}, bf16[8,96,128]{2,1,0:T(8,128)(2,1)S(1)}, u32[]{:S(2)}, u32[]{:S(2)}) collective-permute-start(bf16[8,96,128]{2,1,0:T(8,128)(2,1)S(1)} %collective-permute-done.2.refs_1_), channel_id=1, source_target_pairs={{0,64},{64,128},{128,192},{192,256},{256,320},{320,384},{384,448},... | collective-permute-start | bytes 589832 | tf_op jit(solution)/shard_map/ppermute | solution.py:120
  87.7 26.7 %collective-permute-start.1 = (bf16[2,8,128,128]{3,2,1,0:T(8,128)(2,1)S(1)}, bf16[2,8,128,128]{3,2,1,0:T(8,128)(2,1)S(1)}, u32[]{:S(2)}, u32[]{:S(2)}) collective-permute-start(bf16[2,8,128,128]{3,2,1,0:T(8,128)(2,1)S(1)} %get-tuple-element.15), channel_id=1, source_target_pairs={{0,32},{32,0},{1,33},{33,1},{2,34},{34,2},{3,35},{35,3},{4,36},{36... | collective-permute-start | bytes 1572872 | tf_op jit(solution)/shard_map/ppermute | solution.py:120
  89.8 24.6 %copy-start.4 = (bf16[8,96,128]{2,1,0:T(8,128)(2,1)}, bf16[8,96,128]{2,1,0:T(8,128)(2,1)S(1)}, u32[]{:S(2)}) copy-start(bf16[8,96,128]{2,1,0:T(8,128)(2,1)S(1)} %collective-permute-done.3.refs_2_) | copy-start | bytes 589828
  89.8 7.6 %collective-permute-start.5 = (bf16[8,96,128]{2,1,0:T(8,128)(2,1)S(1)}, bf16[8,96,128]{2,1,0:T(8,128)(2,1)S(1)}, u32[]{:S(2)}, u32[]{:S(2)}) collective-permute-start(bf16[8,96,128]{2,1,0:T(8,128)(2,1)S(1)} %collective-permute-done.3.refs_2_), channel_id=1, source_target_pairs={{0,448},{64,0},{128,64},{192,128},{256,192},{320,256},{384,320},{4... | collective-permute-start | bytes 589832 | tf_op jit(solution)/shard_map/ppermute | solution.py:120
  94.4 20.1 %copy-start.5 = (bf16[8,96,128]{2,1,0:T(8,128)(2,1)}, bf16[8,96,128]{2,1,0:T(8,128)(2,1)S(1)}, u32[]{:S(2)}) copy-start(bf16[8,96,128]{2,1,0:T(8,128)(2,1)S(1)} %collective-permute-done.4.refs_3_) | copy-start | bytes 589828
  94.4 8.3 %collective-permute-start.6 = (bf16[8,96,128]{2,1,0:T(8,128)(2,1)S(1)}, bf16[8,96,128]{2,1,0:T(8,128)(2,1)S(1)}, u32[]{:S(2)}, u32[]{:S(2)}) collective-permute-start(bf16[8,96,128]{2,1,0:T(8,128)(2,1)S(1)} %collective-permute-done.4.refs_3_), channel_id=1, source_target_pairs={{0,64},{64,128},{128,192},{192,256},{256,320},{320,384},{384,448},... | collective-permute-start | bytes 589832 | tf_op jit(solution)/shard_map/ppermute | solution.py:120
  97.4 17.0 %copy-start.6 = (bf16[8,96,128]{2,1,0:T(8,128)(2,1)}, bf16[8,96,128]{2,1,0:T(8,128)(2,1)S(1)}, u32[]{:S(2)}) copy-start(bf16[8,96,128]{2,1,0:T(8,128)(2,1)S(1)} %collective-permute-done.5.refs_4_) | copy-start | bytes 589828
  97.4 17.0 %collective-permute-start.7 = (bf16[8,96,128]{2,1,0:T(8,128)(2,1)S(1)}, bf16[8,96,128]{2,1,0:T(8,128)(2,1)S(1)}, u32[]{:S(2)}, u32[]{:S(2)}) collective-permute-start(bf16[8,96,128]{2,1,0:T(8,128)(2,1)S(1)} %collective-permute-done.5.refs_4_), channel_id=1, source_target_pairs={{0,448},{64,0},{128,64},{192,128},{256,192},{320,256},{384,320},{4... | collective-permute-start | bytes 589832 | tf_op jit(solution)/shard_map/ppermute | solution.py:120
  102.8 11.7 %copy-start.7 = (bf16[8,96,128]{2,1,0:T(8,128)(2,1)}, bf16[8,96,128]{2,1,0:T(8,128)(2,1)S(1)}, u32[]{:S(2)}) copy-start(bf16[8,96,128]{2,1,0:T(8,128)(2,1)S(1)} %collective-permute-done.6.refs_5_) | copy-start | bytes 589828
  102.8 11.7 %collective-permute-start.8 = (bf16[8,96,128]{2,1,0:T(8,128)(2,1)S(1)}, bf16[8,96,128]{2,1,0:T(8,128)(2,1)S(1)}, u32[]{:S(2)}, u32[]{:S(2)}) collective-permute-start(bf16[8,96,128]{2,1,0:T(8,128)(2,1)S(1)} %collective-permute-done.6.refs_5_), channel_id=1, source_target_pairs={{0,64},{64,128},{128,192},{192,256},{256,320},{320,384},{384,448},... | collective-permute-start | bytes 589832 | tf_op jit(solution)/shard_map/ppermute | solution.py:120
  114.4 0.8 copy-start.1
  114.4 0.9 copy-start.8
  114.4 0.9 copy-start.9
Sparse Core Ops, SparseCore 0:
  66.8 78.9 all-gather.3

commit v2 on v1

v2 whole, which is shorter than its diff:
```python
import functools

import jax
import jax.numpy as jnp
import numpy as np
from jax import lax
from jax.experimental import pallas as pl
from jax.experimental.pallas import tpu as pltpu
from jax.sharding import Mesh
from jax.sharding import PartitionSpec as P

HD = 48
AXES = ("y", "xlo", "core", "z", "xhi")
SIZES = (8, 2, 2, 8, 2)
HEADS = ("z", "xhi")
OCT = ("xlo", "core", "xhi")
F32, BF16 = jnp.float32, jnp.bfloat16
VMEM = 56 * 1024 * 1024
SHIFTS = (0, -1, 1, -2, 2, -3, 3, -4)


def params():
    return pltpu.CompilerParams(vmem_limit_bytes=VMEM)


def dot(a, b, da, db):
    return lax.dot_general(a, b, (((da,), (db,)), ((), ())), preferred_element_type=F32)


def norm_kernel(pos_ref, chain_ref, hot_ref, tok_ref, emb_ref, hemb_ref, out_ref):
    samples, tok_dev, width = tok_ref.shape
    first = pos_ref[0]
    emb = emb_ref[...].astype(F32)
    hemb = hemb_ref[...].astype(F32)
    row_of = lax.broadcasted_iota(jnp.int32, (tok_dev, width), 0)
    cond = jnp.zeros((tok_dev, width), F32)
    for t in range(tok_dev):
        chain = chain_ref[t]
        row = jnp.zeros((1, width), F32)
        for c in range(emb_ref.shape[0]):
            row = row + jnp.where(chain == c, 1.0, 0.0) * emb[c : c + 1]
        hits = jnp.int32(0)
        for i in range(hot_ref.shape[0]):
            hits = hits + jnp.where(hot_ref[i] == first + t, 1, 0)
        row = row + jnp.where(hits > 0, 1.0, 0.0) * hemb
        cond = cond + jnp.where(row_of == t, row, 0.0)
    shifted = tok_ref[...].astype(F32) + cond[None]
    average = jnp.mean(shifted, axis=-1, keepdims=True)
    centred = shifted - average
    spread = jnp.mean(centred * centred, axis=-1, keepdims=True)
    normed = (centred * lax.rsqrt(spread + 1e-05)).reshape(samples * tok_dev, width).astype(BF16)
    for g in range(out_ref.shape[0]):
        out_ref[g] = normed


def bias_kernel(pos_ref, b_ref, keep_ref, away_ref):
    xlo, core, xhi = pos_ref[1], pos_ref[2], pos_ref[3]
    row = lax.broadcasted_iota(jnp.int32, (128, 128), 0)
    col = lax.broadcasted_iota(jnp.int32, (128, 128), 1)
    z, t = (row % 64) // 8, row % 8
    from_q = (z * 2 + row // 64) * 8 + t
    from_k = (z * 2 + jnp.bitwise_xor(row // 64, xhi)) * 8 + t
    pick_q = jnp.where(col == from_q, 1.0, 0.0).astype(BF16)
    pick_k = jnp.where(col == from_k, 1.0, 0.0).astype(BF16)
    for b in range(32):
        y, xl, c = b // 4, (b // 2) % 2, b % 2
        tile = dot(pick_q, b_ref[0, :, b * 128 : (b + 1) * 128], 1, 0).astype(BF16)
        turned = dot(pick_k, tile, 1, 1).astype(BF16)
        role = jnp.bitwise_xor(xlo, xl)

        @pl.when(core == c)
        def _():
            keep_ref[role, y] = turned

        @pl.when(core != c)
        def _():
            away_ref[role, y] = turned


def proj_kernel(pos_ref, x_ref, own_ref, other_ref, q_ref, kv_own_ref, kv_other_ref, gate_ref):
    peers, rows, width = x_ref.shape
    pairs = kv_own_ref.shape[0]
    tok = rows // (2 * pairs)
    xhi = pos_ref[3]
    x = x_ref[...].reshape(peers * rows, width)
    for role, w_ref in enumerate((own_ref, other_ref)):
        kv_ref = (kv_own_ref, kv_other_ref)[role]
        full = dot(x, w_ref[: 4 * HD], 1, 1).reshape(peers, 2 * pairs, tok, 4 * HD)
        for p in range(pairs):
            two = jnp.concatenate([full[:, 2 * p + i].reshape(peers * tok, 4 * HD) for i in range(2)], axis=0)
            turned = jnp.transpose(two)
            queries = (turned[:HD] * (1.0 / HD**0.5)).astype(BF16)
            for d in range(4):
                q_ref[2 * d + jnp.bitwise_xor(xhi, role), p] = queries
            kv_ref[p] = turned[HD : 3 * HD].astype(BF16)
            gate_ref[jnp.bitwise_xor(xhi, role), p] = jax.nn.sigmoid(turned[3 * HD :])


def join(a, b):
    lane = lax.broadcasted_iota(jnp.int32, a.shape, 1)
    return jnp.where(lane < 64, a, pltpu.roll(b, 64, 1)), jnp.where(lane < 64, pltpu.roll(a, 64, 1), b)


def join_kernel(own_ref, other_ref, kv_ref):
    for p in range(own_ref.shape[0]):
        even, odd = join(own_ref[p].astype(F32), other_ref[p].astype(F32))
        kv_ref[2 * p] = even.astype(BF16)
        kv_ref[2 * p + 1] = odd.astype(BF16)


def join_q_kernel(pos_ref, q_ref, out_ref):
    me = pos_ref[1] * 2 + pos_ref[2]
    for role in range(4):
        d = 2 * jnp.bitwise_xor(me, role)
        for p in range(q_ref.shape[1]):
            even, odd = join(q_ref[d, p].astype(F32), q_ref[d + 1, p].astype(F32))
            out_ref[2 * p, :, role * 128 : (role + 1) * 128] = even.astype(BF16)
            out_ref[2 * p + 1, :, role * 128 : (role + 1) * 128] = odd.astype(BF16)


def attend_kernel(steps, first, last, pos_ref, q_ref, keep_ref, recv_ref, far_ref, *refs):
    count = sum(len(s) for s in steps)
    kv_refs, rest = refs[:count], refs[count:]
    me, yy = pos_ref[1] * 2 + pos_ref[2], pos_ref[0]
    acc = [None, None] if first else [rest[0][i] for i in range(2)]
    top = [None, None] if first else [rest[1][i, :1] for i in range(2)]
    at = 0
    for step in steps:
        bias = []
        for sh in step:
            y = lax.rem(yy + 8 + sh, 8)
            bias.append(
                jnp.concatenate([keep_ref[0, y], recv_ref[0, y], far_ref[0, y], far_ref[1, y]], axis=1).astype(F32)
            )
        bias = jnp.concatenate(bias, axis=0)
        blocks = kv_refs[at : at + len(step)]
        at += len(step)
        for i in range(2):
            keys = jnp.concatenate([jnp.transpose(r[i, :HD].astype(F32)).astype(BF16) for r in blocks], axis=0)
            vals = jnp.concatenate([r[i, HD:] for r in blocks], axis=1)
            vals = jnp.concatenate([vals, jnp.ones((16, vals.shape[1]), BF16)], axis=0)
            scores = jnp.dot(keys, q_ref[i], preferred_element_type=F32) + bias
            best = jnp.max(scores, axis=0, keepdims=True)
            if top[i] is not None:
                best = jnp.maximum(best, top[i])
            probs = jnp.exp(scores - best).astype(BF16)
            part = jnp.dot(vals, probs, preferred_element_type=F32)
            if top[i] is not None:
                part = part + acc[i] * jnp.exp(top[i] - best)
            acc[i], top[i] = part, best
    if not last:
        for i in range(2):
            rest[-2][i] = acc[i]
            rest[-1][i] = jnp.broadcast_to(top[i], (8, top[i].shape[1]))
        return
    out_ref = rest[-1]
    row = lax.broadcasted_iota(jnp.int32, (16, 128), 0)
    for role in range(4):
        d = 2 * jnp.bitwise_xor(me, role)
        tiles = []
        for i in range(2):
            mine = acc[i][:, role * 128 : (role + 1) * 128]
            total = mine[HD : HD + 1]
            lse = top[i][:, role * 128 : (role + 1) * 128] + jnp.log(total)
            hi = lse.astype(BF16).astype(F32)
            mid = (lse - hi).astype(BF16).astype(F32)
            low = lse - hi - mid
            tail = jnp.where(row == 0, hi, jnp.where(row == 1, mid, jnp.where(row == 2, low, 0.0)))
            tiles.append(jnp.concatenate([mine[:HD] / total, tail], axis=0))
        even, odd = join(tiles[0], tiles[1])
        out_ref[d, 0] = even.astype(BF16)
        out_ref[d + 1, 0] = odd.astype(BF16)


def merge_kernel(pos_ref, p_ref, gate_ref, w_own_ref, w_other_ref, out_ref):
    xhi = pos_ref[3]
    pairs = p_ref.shape[1]
    peers = out_ref.shape[0]
    for p in range(pairs):
        share = None
        for role, w_ref in enumerate((w_own_ref, w_other_ref)):
            h = jnp.bitwise_xor(xhi, role)
            rows = [p_ref[2 * i + h, p].astype(F32) for i in range(4)]
            lse = [r[HD : HD + 1] + r[HD + 1 : HD + 2] + r[HD + 2 : HD + 3] for r in rows]
            top = functools.reduce(jnp.maximum, lse)
            weight = [jnp.exp(v - top) for v in lse]
            mixed = sum(w * r[:HD] for w, r in zip(weight, rows)) / sum(weight) * gate_ref[h, p]
            gated = jnp.transpose(jnp.concatenate([mixed, jnp.zeros((80, 128), F32)], axis=0))[:, :HD].astype(BF16)
            term = jnp.dot(gated, w_ref[4 * HD :], preferred_element_type=F32)
            share = term if share is None else share + term
        tok = 64 // peers
        split = share.reshape(2, peers, tok, share.shape[1])
        for g in range(peers):
            both = jnp.concatenate([split[0, g], split[1, g]], axis=0)
            out_ref[g, 2 * tok * p : 2 * tok * (p + 1)] = both.astype(BF16)


def sum_kernel(x_ref, out_ref):
    total = x_ref[0].astype(F32)
    for g in range(1, x_ref.shape[0]):
        total = total + x_ref[g].astype(F32)
    out_ref[...] = total.astype(BF16)


def shift(x, axis, by):
    n = SIZES[AXES.index(axis)]
    return lax.ppermute(x, axis, [(i, (i + by) % n) for i in range(n)])


def body(tokens, chain_id, hotspots, chain_embed, hot_embed, w_proj, pair_bias, w_out):
    samples, tok_dev, width = tokens.shape
    pairs, peers = samples // 2, 8
    at = {a: lax.axis_index(a) for a in AXES}
    first = ((((at["y"] * 2 + at["xlo"]) * 2 + at["core"]) * 8 + at["z"]) * 2 + at["xhi"]) * tok_dev
    pos = jnp.stack([first, at["xlo"], at["core"], at["xhi"]])
    where = jnp.stack([at["y"], at["xlo"], at["core"], at["xhi"]])
    vm = pl.BlockSpec(memory_space=pltpu.VMEM)
    sm = pl.BlockSpec(memory_space=pltpu.SMEM)

    def call(kernel, specs, out, *args):
        shapes = [jax.ShapeDtypeStruct(s, t) for s, t in out]
        return pl.pallas_call(
            kernel, out_shape=shapes, in_specs=specs, out_specs=[vm] * len(out), compiler_params=params()
        )(*args)

    weights = jnp.concatenate([jnp.transpose(w_proj), w_out], axis=0)
    weights_other = shift(weights, "xhi", 1)
    keep, away = call(bias_kernel, [sm, vm], [((2, 8, 128, 128), BF16)] * 2, pos, pair_bias)
    recv = shift(away, "core", 1)
    far = shift(jnp.stack([keep[1], recv[1]]), "xlo", 1)

    (copies,) = call(
        norm_kernel,
        [sm, sm, sm, vm, vm, vm],
        [((peers, samples * tok_dev, width), BF16)],
        pos,
        chain_id,
        hotspots,
        tokens,
        chain_embed,
        hot_embed[None],
    )
    gathered = lax.all_to_all(copies, "z", split_axis=0, concat_axis=0, tiled=True)
    q_out, kv_own, kv_other, gate = call(
        proj_kernel,
        [sm, vm, vm, vm],
        [
            ((8, pairs, HD, 128), BF16),
            ((pairs, 2 * HD, 128), BF16),
            ((pairs, 2 * HD, 128), BF16),
            ((2, pairs, HD, 128), F32),
        ],
        pos,
        gathered,
        weights,
        weights_other,
    )
    kv_other = shift(kv_other, "xhi", 1)
    (kv,) = call(join_kernel, [vm, vm], [((samples, 2 * HD, 128), BF16)], kv_own, kv_other)
    right, left, ring = kv, kv, [kv]
    for step in range(4):
        right = shift(right, "y", 1)
        ring.append(right)
        if step < 3:
            left = shift(left, "y", -1)
            ring.append(left)
    q_in = lax.all_to_all(q_out, OCT, split_axis=0, concat_axis=0, tiled=True)
    (q_all,) = call(join_q_kernel, [sm, vm], [((samples, HD, 512), BF16)], pos, q_in)

    def two(*dims):
        return pl.BlockSpec((2,) + dims, lambda s, _: (s,) + (0,) * len(dims))

    whole = pl.BlockSpec((2, 8, 128, 128), lambda s, _: (0, 0, 0, 0))
    steps = (SHIFTS[0:2], SHIFTS[2:4], SHIFTS[4:6], SHIFTS[6:8])
    parts = pl.pallas_call(
        functools.partial(attend_kernel, steps, True, True),
        out_shape=jax.ShapeDtypeStruct((8, pairs, 64, 128), BF16),
        grid_spec=pltpu.PrefetchScalarGridSpec(
            num_scalar_prefetch=1,
            grid=(pairs,),
            in_specs=[two(HD, 512), whole, whole, whole] + [two(2 * HD, 128)] * 8,
            out_specs=pl.BlockSpec((8, 1, 64, 128), lambda s, _: (0, s, 0, 0)),
        ),
        compiler_params=params(),
    )(where, q_all, keep, recv, far, *ring)
    mine = lax.all_to_all(parts, OCT, split_axis=0, concat_axis=0, tiled=True)
    (shares,) = call(
        merge_kernel,
        [sm, vm, vm, vm, vm],
        [((peers, samples * tok_dev, width), BF16)],
        pos,
        mine,
        gate,
        weights,
        weights_other,
    )
    summands = lax.all_to_all(shares, "z", split_axis=0, concat_axis=0, tiled=True)
    (update,) = call(sum_kernel, [vm], [((samples * tok_dev, width), BF16)], summands)
    return update.reshape(samples, tok_dev, width)


def solution(mesh):
    fine = Mesh(np.asarray(mesh.devices).reshape(SIZES), AXES)
    blk = ("y", "xlo", "core")
    in_specs = (
        P(None, AXES, None),
        P(AXES),
        P(),
        P(),
        P(),
        P(None, HEADS),
        P(HEADS, blk, None),
        P(HEADS, None),
    )
    return jax.shard_map(body, mesh=fine, in_specs=in_specs, out_specs=P(None, AXES, None), check_vma=False)
```

time: 173 us -> 158 us (0.913); the launches traced: 169 us -> 157 us
  blocking collectives: 87.4 us -> 42.9 us
  starting transfers between devices: 29.2 us -> 55.6 us
  Pallas kernels: 25.2 us -> 39.7 us
  between operations: 13.7 us -> 0.32 us
  waiting for transfers between devices: 4.16 us -> 11.8 us
  local copies, waits for them, and re-layouts: 8.08 us -> 5.34 us
    all_to_all x3 -> x2, blocking collectives: 78.3 us -> 42.9 us  [the longest x1 27.8 us: body(): lax.all_to_all(shares, 'z', split_axis=0, concat_axis=0, tiled=True)]
    all_to_all x0 -> x2, starting transfers between devices: none -> 17.9 us  [the longest x1 11 us: body(): lax.all_to_all(copies, 'z', split_axis=0, concat_axis=0, tiled=True)]
    pallas_call x5 -> x8, Pallas kernels: 25.2 us -> 39.7 us  [the longest x7 25.6 us: call(): pl.pallas_call(kernel, out_shape=shapes, in_specs=specs, out_specs=[vm] *...]
    all_gather x1 -> x0, blocking collectives: 9.11 us -> none  [body(): q_all = lax.all_gather(q_t, QUAD, axis=0)]
    ppermute x9 -> x11, starting transfers between devices: 29.2 us -> 37.7 us  [shift(): return lax.ppermute(x, axis, [(i, (i + by) % n) for i in range(n)])]
    all_to_all x0 -> x2, waiting for transfers between devices: none -> 4.48 us  [the longest x1 3.93 us: body(): lax.all_to_all(copies, 'z', split_axis=0, concat_axis=0, tiled=True)]
    unnamed x24 -> x38, local copies, waits for them, and re-layouts: 1.25 us -> 4.72 us
    ppermute x9 -> x11, waiting for transfers between devices: 4.14 us -> 7.36 us  [shift(): return lax.ppermute(x, axis, [(i, (i + by) % n) for i in range(n)])]
  transfers between devices with their start and end apart: 10 -> 13, of which waited for: 2 -> 5; matrix products, arithmetic and copies ran while one was open for 4% -> 0% of each run, Pallas kernels for 10% -> 12%
where the time goes in v2:
time: 158 us; the launch traced here: 157 us
  starting transfers between devices  55.6 us (35%)
  blocking collectives  42.9 us (27%)
  Pallas kernels  39.7 us (25%)
  waiting for transfers between devices  11.8 us (7%)
  local copies, waits for them, and re-layouts  5.34 us (3%)
    ppermute x11, starting transfers between devices, shift(): return lax.ppermute(x, axis, [(i, (i + by) % n) for i in range(n)])  37.7 us
    all_to_all x1, blocking collectives, body(): lax.all_to_all(shares, 'z', split_axis=0, concat_axis=0, tiled=True)  27.8 us
    pallas_call x7, Pallas kernels, call(): pl.pallas_call(kernel, out_shape=shapes, in_specs=specs, out_specs=[vm] *...  25.6 us
    all_to_all x1, blocking collectives, body(): mine = lax.all_to_all(parts, OCT, split_axis=0, concat_axis=0, tiled=True)  15.1 us
    pallas_call x1, Pallas kernels, body(): pl.pallas_call(functools.partial(attend_kernel, steps, True, True), out_s...  14.1 us
    all_to_all x1, starting transfers between devices, body(): lax.all_to_all(copies, 'z', split_axis=0, concat_axis=0, tiled=True)  11 us
    ppermute x11, waiting for transfers between devices, shift(): return lax.ppermute(x, axis, [(i, (i + by) % n) for i in range(n)])  7.36 us
    all_to_all x1, starting transfers between devices, body(): q_in = lax.all_to_all(q_out, OCT, split_axis=0, concat_axis=0, tiled=True)  6.87 us
  transfers between devices with their start and end apart: 13, of which 5 were waited for; matrix products, arithmetic and copies ran while one was open for 0% of the time, Pallas kernels for 12%

profile of v2, /device:TPU:1, one launch (start us, length us, event | category | flops | bytes accessed | tf_op | source)
XLA Modules:
  0.0 157.0 jit_solution(7882920197382469377)
XLA Ops:
  0.0 0.7 copy-done.18
  0.7 0.6 broadcast_in_dim.3.hemb_ref
  1.3 0.7 add_add_fusion.pos_ref
  1.9 2.2 %shard_map.82 = bf16[8,64,768]{2,1,0:T(8,128)(2,1)} custom-call(s32[4]{0:T(128)} %add_add_fusion.pos_ref, s32[8]{0:T(128)} %chain_ref.1, s32[16]{0:T(128)} %hot_ref.1, bf16[8,8,768]{2,1,0:T(8,128)(2,1)} %tok_ref.1, bf16[4,768]{1,0:T(4,128)(2,1)} %emb_ref.1, bf16[1,768]{1,0:T(2,128)(2,1)} %broadcast_in_dim.3.hemb_ref), custom_call_target="tpu_custom_call" | custom-call | tf_op jit(solution)/shard_map/pallas_call | solution.py:222
  4.2 11.0 %all-to-all-start = ((bf16[8,64,768]{2,1,0:T(8,128)(2,1)}), bf16[8,64,768]{2,1,0:T(8,128)(2,1)S(1)}, u32[]{:S(2)}, u32[]{:S(2)}) async-start(bf16[8,64,768]{2,1,0:T(8,128)(2,1)} %shard_map.82), calls=%async_computation | async-start | bytes 1572864 | tf_op jit(solution)/shard_map/all_to_all | solution.py:243
  15.2 0.0 copy-done.8
  15.2 0.0 copy-done.17
  15.2 0.0 copy-start
  15.2 4.7 %collective-permute-start = (bf16[240,768]{1,0:T(8,128)(2,1)S(1)}, bf16[240,768]{1,0:T(8,128)(2,1)S(1)}, u32[]{:S(2)}, u32[]{:S(2)}) collective-permute-start(bf16[240,768]{1,0:T(8,128)(2,1)S(1)} %pad_maximum_fusion.1.own_ref.w_own_ref), channel_id=1, source_target_pairs={{0,1},{1,0},{2,3},{3,2},{4,5},{5,4},{6,7},{7,6},{8,9},{9,8},{10,11... | collective-permute-start | bytes 1105928 | tf_op jit(solution)/shard_map/ppermute | solution.py:207
  19.9 11.8 %shard_map.85 = (bf16[2,8,128,128]{3,2,1,0:T(8,128)(2,1)}, bf16[2,8,128,128]{3,2,1,0:T(8,128)(2,1)}) custom-call(s32[4]{0:T(128)} %add_add_fusion.pos_ref, bf16[1,128,4096]{2,1,0:T(8,128)(2,1)} %b_ref.1), custom_call_target="tpu_custom_call" | custom-call | tf_op jit(solution)/shard_map/pallas_call | solution.py:222
  31.6 0.0 copy-done
  31.7 3.1 %collective-permute-start.1 = (bf16[2,8,128,128]{3,2,1,0:T(8,128)(2,1)}, bf16[2,8,128,128]{3,2,1,0:T(8,128)(2,1)S(1)}, u32[]{:S(2)}, u32[]{:S(2)}) collective-permute-start(bf16[2,8,128,128]{3,2,1,0:T(8,128)(2,1)} %get-tuple-element.13), channel_id=1, source_target_pairs={{0,16},{16,0},{1,17},{17,1},{2,18},{18,2},{3,19},{19,3},{4,20},{20... | collective-permute-start | bytes 1572872 | tf_op jit(solution)/shard_map/ppermute | solution.py:207
  34.8 0.0 collective-permute-done.other_ref.w_other_ref
  34.8 0.0 copy-start.3
  34.8 3.9 %all-to-all-done.x_ref = bf16[8,64,768]{2,1,0:T(8,128)(2,1)S(1)} async-done(((bf16[8,64,768]{2,1,0:T(8,128)(2,1)}), bf16[8,64,768]{2,1,0:T(8,128)(2,1)S(1)}, u32[]{:S(2)}, u32[]{:S(2)}) %all-to-all-start) | async-done | bytes 786464 | tf_op jit(solution)/shard_map/all_to_all | solution.py:243
  38.7 0.0 copy-done.3
  38.7 0.9 copy-done.1
  39.6 3.1 %shard_map.83 = (bf16[8,4,48,128]{3,2,1,0:T(8,128)(2,1)}, bf16[4,96,128]{2,1,0:T(8,128)(2,1)}, bf16[4,96,128]{2,1,0:T(8,128)(2,1)}, f32[2,4,48,128]{3,2,1,0:T(8,128)}) custom-call(s32[4]{0:T(128)} %add_add_fusion.pos_ref, bf16[8,64,768]{2,1,0:T(8,128)(2,1)} %copy-done.1, bf16[240,768]{1,0:T(8,128)(2,1)} %copy-done, bf16[240,768]{1,0:T(8,128)(2,1)} %copy-done.3), custom_call_target="tpu_custom_call" | custom-call | tf_op jit(solution)/shard_map/pallas_call | solution.py:222
  42.8 4.6 %collective-permute-start.3 = (bf16[4,96,128]{2,1,0:T(8,128)(2,1)}, bf16[4,96,128]{2,1,0:T(8,128)(2,1)S(1)}, u32[]{:S(2)}, u32[]{:S(2)}) collective-permute-start(bf16[4,96,128]{2,1,0:T(8,128)(2,1)} %get-tuple-element.15), channel_id=1, source_target_pairs={{0,1},{1,0},{2,3},{3,2},{4,5},{5,4},{6,7},{7,6},{8,9},{9,8},{10,11... | collective-permute-start | bytes 294920 | tf_op jit(solution)/shard_map/ppermute | solution.py:207
  47.4 2.8 %collective-permute-done.3.other_ref = bf16[4,96,128]{2,1,0:T(8,128)(2,1)S(1)} collective-permute-done((bf16[4,96,128]{2,1,0:T(8,128)(2,1)}, bf16[4,96,128]{2,1,0:T(8,128)(2,1)S(1)}, u32[]{:S(2)}, u32[]{:S(2)}) %collective-permute-start.3) | collective-permute-done | bytes 98336 | tf_op jit(solution)/shard_map/ppermute | solution.py:207
  50.2 0.6 copy-done.16
  50.9 1.7 %shard_map.86.refs_0_ = bf16[8,96,128]{2,1,0:T(8,128)(2,1)} custom-call(bf16[4,96,128]{2,1,0:T(8,128)(2,1)} %get-tuple-element.14.own_ref, bf16[4,96,128]{2,1,0:T(8,128)(2,1)} %copy-done.16), custom_call_target="tpu_custom_call" | custom-call | tf_op jit(solution)/shard_map/pallas_call | solution.py:222
  52.6 3.2 %collective-permute-start.4 = (bf16[8,96,128]{2,1,0:T(8,128)(2,1)}, bf16[8,96,128]{2,1,0:T(8,128)(2,1)S(1)}, u32[]{:S(2)}, u32[]{:S(2)}) collective-permute-start(bf16[8,96,128]{2,1,0:T(8,128)(2,1)} %shard_map.86.refs_0_), channel_id=1, source_target_pairs={{0,64},{64,128},{128,192},{192,256},{256,320},{320,384},{384,448},... | collective-permute-start | bytes 589832 | tf_op jit(solution)/shard_map/ppermute | solution.py:207
  55.8 0.0 copy-done.4
  55.8 0.0 copy-start.6
  55.9 0.0 collective-permute-done.1.recv_ref
  55.9 0.0 copy-start.5
  55.9 1.0 copy-done.6
  56.9 3.8 %collective-permute-start.5 = (bf16[8,96,128]{2,1,0:T(8,128)(2,1)S(1)}, bf16[8,96,128]{2,1,0:T(8,128)(2,1)S(1)}, u32[]{:S(2)}, u32[]{:S(2)}) collective-permute-start(bf16[8,96,128]{2,1,0:T(8,128)(2,1)S(1)} %copy-done.6), channel_id=1, source_target_pairs={{0,448},{64,0},{128,64},{192,128},{256,192},{320,256},{384,320},{4... | collective-permute-start | bytes 589832 | tf_op jit(solution)/shard_map/ppermute | solution.py:207
  60.7 1.0 collective-permute-done.4.refs_1_
  61.8 1.9 %collective-permute-start.6 = (bf16[8,96,128]{2,1,0:T(8,128)(2,1)S(1)}, bf16[8,96,128]{2,1,0:T(8,128)(2,1)S(1)}, u32[]{:S(2)}, u32[]{:S(2)}) collective-permute-start(bf16[8,96,128]{2,1,0:T(8,128)(2,1)S(1)} %collective-permute-done.4.refs_1_), channel_id=1, source_target_pairs={{0,64},{64,128},{128,192},{192,256},{256,320},{320,384},{384,448},... | collective-permute-start | bytes 589832 | tf_op jit(solution)/shard_map/ppermute | solution.py:207
  63.7 0.1 pad_maximum_fusion
  63.8 0.0 copy-done.5
  63.8 0.0 copy-done.9
  63.8 3.1 %collective-permute-start.2 = (bf16[2,8,128,128]{3,2,1,0:T(8,128)(2,1)S(1)}, bf16[2,8,128,128]{3,2,1,0:T(8,128)(2,1)S(1)}, u32[]{:S(2)}, u32[]{:S(2)}) collective-permute-start(bf16[2,8,128,128]{3,2,1,0:T(8,128)(2,1)S(1)} %pad_maximum_fusion), channel_id=1, source_target_pairs={{0,32},{32,0},{1,33},{33,1},{2,34},{34,2},{3,35},{35,3},{4,36},{36... | collective-permute-start | bytes 1572872 | tf_op jit(solution)/shard_map/ppermute | solution.py:207
  66.9 0.0 collective-permute-done.5.refs_2_
  66.9 0.0 copy-start.10
  66.9 4.6 %collective-permute-start.7 = (bf16[8,96,128]{2,1,0:T(8,128)(2,1)S(1)}, bf16[8,96,128]{2,1,0:T(8,128)(2,1)S(1)}, u32[]{:S(2)}, u32[]{:S(2)}) collective-permute-start(bf16[8,96,128]{2,1,0:T(8,128)(2,1)S(1)} %collective-permute-done.5.refs_2_), channel_id=1, source_target_pairs={{0,448},{64,0},{128,64},{192,128},{256,192},{320,256},{384,320},{4... | collective-permute-start | bytes 589832 | tf_op jit(solution)/shard_map/ppermute | solution.py:207
  71.5 0.0 collective-permute-done.6.refs_3_
  71.5 0.0 copy-start.11
  71.5 1.9 %collective-permute-start.8 = (bf16[8,96,128]{2,1,0:T(8,128)(2,1)S(1)}, bf16[8,96,128]{2,1,0:T(8,128)(2,1)S(1)}, u32[]{:S(2)}, u32[]{:S(2)}) collective-permute-start(bf16[8,96,128]{2,1,0:T(8,128)(2,1)S(1)} %collective-permute-done.6.refs_3_), channel_id=1, source_target_pairs={{0,64},{64,128},{128,192},{192,256},{256,320},{320,384},{384,448},... | collective-permute-start | bytes 589832 | tf_op jit(solution)/shard_map/ppermute | solution.py:207
  73.4 0.0 copy-done.10
  73.4 0.0 copy-done.11
  73.5 6.9 %all-to-all-start.1 = ((bf16[8,4,48,128]{3,2,1,0:T(8,128)(2,1)}), bf16[8,4,48,128]{3,2,1,0:T(8,128)(2,1)S(1)}, u32[]{:S(2)}, u32[]{:S(2)}) async-start(bf16[8,4,48,128]{3,2,1,0:T(8,128)(2,1)} %get-tuple-element.11), calls=%async_computation.1 | async-start | bytes 786432 | tf_op jit(solution)/shard_map/all_to_all | solution.py:267
  80.3 0.0 collective-permute-done.7.refs_4_
  80.3 4.9 %collective-permute-start.9 = (bf16[8,96,128]{2,1,0:T(8,128)(2,1)S(1)}, bf16[8,96,128]{2,1,0:T(8,128)(2,1)S(1)}, u32[]{:S(2)}, u32[]{:S(2)}) collective-permute-start(bf16[8,96,128]{2,1,0:T(8,128)(2,1)S(1)} %collective-permute-done.7.refs_4_), channel_id=1, source_target_pairs={{0,448},{64,0},{128,64},{192,128},{256,192},{320,256},{384,320},{4... | collective-permute-start | bytes 589832 | tf_op jit(solution)/shard_map/ppermute | solution.py:207
  85.2 0.0 collective-permute-done.8.refs_5_
  85.2 0.0 copy-start.13
  85.2 1.9 %collective-permute-start.10 = (bf16[8,96,128]{2,1,0:T(8,128)(2,1)S(1)}, bf16[8,96,128]{2,1,0:T(8,128)(2,1)S(1)}, u32[]{:S(2)}, u32[]{:S(2)}) collective-permute-start(bf16[8,96,128]{2,1,0:T(8,128)(2,1)S(1)} %collective-permute-done.8.refs_5_), channel_id=1, source_target_pairs={{0,64},{64,128},{128,192},{192,256},{256,320},{320,384},{384,448},... | collective-permute-start | bytes 589832 | tf_op jit(solution)/shard_map/ppermute | solution.py:207
  87.1 0.6 add_add_fusion.1.pos_ref
  87.7 0.6 all-to-all-done.1.q_ref
  88.3 0.8 copy-done.2
  89.1 1.9 %shard_map.84.q_ref = bf16[8,48,512]{2,1,0:T(8,128)(2,1)} custom-call(s32[4]{0:T(128)} %add_add_fusion.pos_ref, bf16[8,4,48,128]{3,2,1,0:T(8,128)(2,1)} %copy-done.2), custom_call_target="tpu_custom_call" | custom-call | tf_op jit(solution)/shard_map/pallas_call | solution.py:222
  91.0 0.0 collective-permute-done.2.far_ref
  91.0 0.0 collective-permute-done.9.refs_6_
  91.0 3.5 %collective-permute-done.10.refs_7_ = bf16[8,96,128]{2,1,0:T(8,128)(2,1)S(1)} collective-permute-done((bf16[8,96,128]{2,1,0:T(8,128)(2,1)S(1)}, bf16[8,96,128]{2,1,0:T(8,128)(2,1)S(1)}, u32[]{:S(2)}, u32[]{:S(2)}) %collective-permute-start.10) | collective-permute-done | bytes 196640 | tf_op jit(solution)/shard_map/ppermute | solution.py:207
  94.5 0.0 copy-done.14
  94.5 0.0 copy-start.15
  94.6 0.7 copy-done.15
  95.2 14.1 %shard_map.87 = bf16[8,4,64,128]{3,2,1,0:T(8,128)(2,1)} custom-call(s32[4]{0:T(128)} %add_add_fusion.1.pos_ref, bf16[8,48,512]{2,1,0:T(8,128)(2,1)} %shard_map.84.q_ref, bf16[2,8,128,128]{3,2,1,0:T(8,128)(2,1)} %get-tuple-element.12.keep_ref, bf16[2,8,128,128]{3,2,1,0:T(8,128)(2,1)} %copy-done.5, bf16[2,8,128,128]{3,2,1,0:T(8,128)(2,1)} %copy-done.7, ...), custom_call_target="tpu_custom_call" | custom-call | tf_op jit(solution)/shard_map/pallas_call | solution.py:275
  109.3 15.1 %all_to_all.20.p_ref = bf16[8,4,64,128]{3,2,1,0:T(8,128)(2,1)} all-to-all(bf16[8,4,64,128]{3,2,1,0:T(8,128)(2,1)} %shard_map.87), channel_id=1, replica_groups=mesh['y'=8,'xlo'=2,'core'=2,'z'=8,'xhi'=2] {'xlo','core','xhi'}, dimensions={0} | all-to-all | bytes 1048576 | tf_op jit(solution)/shard_map/all_to_all | solution.py:286
  124.4 2.9 %shard_map.88 = bf16[8,64,768]{2,1,0:T(8,128)(2,1)} custom-call(s32[4]{0:T(128)} %add_add_fusion.pos_ref, bf16[8,4,64,128]{3,2,1,0:T(8,128)(2,1)} %all_to_all.20.p_ref, f32[2,4,48,128]{3,2,1,0:T(8,128)} %get-tuple-element.16.gate_ref, bf16[240,768]{1,0:T(8,128)(2,1)} %copy-done, bf16[240,768]{1,0:T(8,128)(2,1)} %copy-done.3), custom_call_target="tpu_custom_call" | custom-call | tf_op jit(solution)/shard_map/pallas_call | solution.py:222
  127.3 27.8 %all_to_all.21.x_ref = bf16[8,64,768]{2,1,0:T(8,128)(2,1)} all-to-all(bf16[8,64,768]{2,1,0:T(8,128)(2,1)} %shard_map.88), channel_id=1, replica_groups=mesh['y'=8,'xlo'=2,'core'=2,'z'=8,'xhi'=2] {'z'}, dimensions={0} | all-to-all | bytes 1572864 | tf_op jit(solution)/shard_map/all_to_all | solution.py:297
  155.1 1.9 %shard_map.89 = bf16[64,768]{1,0:T(8,128)(2,1)} custom-call(bf16[8,64,768]{2,1,0:T(8,128)(2,1)} %all_to_all.21.x_ref), custom_call_target="tpu_custom_call" | custom-call | tf_op jit(solution)/shard_map/pallas_call | solution.py:222
  (17 shorter events, 0.1 us)
Async XLA Ops:
  0.0 0.7 copy-start.18
  4.2 11.0 %copy-start.8 = (bf16[768,192]{0,1:T(8,128)(2,1)S(1)}, bf16[768,192]{0,1:T(8,128)(2,1)}, u32[]{:S(2)}) copy-start(bf16[768,192]{0,1:T(8,128)(2,1)} %param.13) | copy-start | bytes 884740
  4.2 11.0 %copy-start.17 = (bf16[48,768]{1,0:T(8,128)(2,1)S(1)}, bf16[48,768]{1,0:T(8,128)(2,1)}, u32[]{:S(2)}) copy-start(bf16[48,768]{1,0:T(8,128)(2,1)} %param.15) | copy-start | bytes 221188
  4.2 34.6 %all-to-all-start = ((bf16[8,64,768]{2,1,0:T(8,128)(2,1)}), bf16[8,64,768]{2,1,0:T(8,128)(2,1)S(1)}, u32[]{:S(2)}, u32[]{:S(2)}) async-start(bf16[8,64,768]{2,1,0:T(8,128)(2,1)} %shard_map.82), calls=%async_computation | async-start | bytes 1572864 | tf_op jit(solution)/shard_map/all_to_all | solution.py:243
  15.2 16.4 %copy-start = (bf16[240,768]{1,0:T(8,128)(2,1)}, bf16[240,768]{1,0:T(8,128)(2,1)S(1)}, u32[]{:S(2)}) copy-start(bf16[240,768]{1,0:T(8,128)(2,1)S(1)} %pad_maximum_fusion.1.own_ref.w_own_ref) | copy-start | bytes 1105924
  15.2 19.6 %collective-permute-start = (bf16[240,768]{1,0:T(8,128)(2,1)S(1)}, bf16[240,768]{1,0:T(8,128)(2,1)S(1)}, u32[]{:S(2)}, u32[]{:S(2)}) collective-permute-start(bf16[240,768]{1,0:T(8,128)(2,1)S(1)} %pad_maximum_fusion.1.own_ref.w_own_ref), channel_id=1, source_target_pairs={{0,1},{1,0},{2,3},{3,2},{4,5},{5,4},{6,7},{7,6},{8,9},{9,8},{10,11... | collective-permute-start | bytes 1105928 | tf_op jit(solution)/shard_map/ppermute | solution.py:207
  31.7 24.2 %collective-permute-start.1 = (bf16[2,8,128,128]{3,2,1,0:T(8,128)(2,1)}, bf16[2,8,128,128]{3,2,1,0:T(8,128)(2,1)S(1)}, u32[]{:S(2)}, u32[]{:S(2)}) collective-permute-start(bf16[2,8,128,128]{3,2,1,0:T(8,128)(2,1)} %get-tuple-element.13), channel_id=1, source_target_pairs={{0,16},{16,0},{1,17},{17,1},{2,18},{18,2},{3,19},{19,3},{4,20},{20... | collective-permute-start | bytes 1572872 | tf_op jit(solution)/shard_map/ppermute | solution.py:207
  34.8 3.9 %copy-start.3 = (bf16[240,768]{1,0:T(8,128)(2,1)}, bf16[240,768]{1,0:T(8,128)(2,1)S(1)}, u32[]{:S(2)}) copy-start(bf16[240,768]{1,0:T(8,128)(2,1)S(1)} %collective-permute-done.other_ref.w_other_ref) | copy-start | bytes 1105924
  38.7 0.9 copy-start.1
  39.6 16.2 %copy-start.4 = (bf16[2,8,128,128]{3,2,1,0:T(8,128)(2,1)S(1)}, bf16[2,8,128,128]{3,2,1,0:T(8,128)(2,1)}, u32[]{:S(2)}) copy-start(bf16[2,8,128,128]{3,2,1,0:T(8,128)(2,1)} %get-tuple-element.12.keep_ref) | copy-start | bytes 1572868
  42.8 7.5 %collective-permute-start.3 = (bf16[4,96,128]{2,1,0:T(8,128)(2,1)}, bf16[4,96,128]{2,1,0:T(8,128)(2,1)S(1)}, u32[]{:S(2)}, u32[]{:S(2)}) collective-permute-start(bf16[4,96,128]{2,1,0:T(8,128)(2,1)} %get-tuple-element.15), channel_id=1, source_target_pairs={{0,1},{1,0},{2,3},{3,2},{4,5},{5,4},{6,7},{7,6},{8,9},{9,8},{10,11... | collective-permute-start | bytes 294920 | tf_op jit(solution)/shard_map/ppermute | solution.py:207
  50.2 0.6 copy-start.16
  52.6 9.2 %collective-permute-start.4 = (bf16[8,96,128]{2,1,0:T(8,128)(2,1)}, bf16[8,96,128]{2,1,0:T(8,128)(2,1)S(1)}, u32[]{:S(2)}, u32[]{:S(2)}) collective-permute-start(bf16[8,96,128]{2,1,0:T(8,128)(2,1)} %shard_map.86.refs_0_), channel_id=1, source_target_pairs={{0,64},{64,128},{128,192},{192,256},{256,320},{320,384},{384,448},... | collective-permute-start | bytes 589832 | tf_op jit(solution)/shard_map/ppermute | solution.py:207
  55.8 1.1 copy-start.6
  55.9 7.9 %copy-start.5 = (bf16[2,8,128,128]{3,2,1,0:T(8,128)(2,1)}, bf16[2,8,128,128]{3,2,1,0:T(8,128)(2,1)S(1)}, u32[]{:S(2)}) copy-start(bf16[2,8,128,128]{3,2,1,0:T(8,128)(2,1)S(1)} %collective-permute-done.1.recv_ref) | copy-start | bytes 1572868
  56.9 10.0 %collective-permute-start.5 = (bf16[8,96,128]{2,1,0:T(8,128)(2,1)S(1)}, bf16[8,96,128]{2,1,0:T(8,128)(2,1)S(1)}, u32[]{:S(2)}, u32[]{:S(2)}) collective-permute-start(bf16[8,96,128]{2,1,0:T(8,128)(2,1)S(1)} %copy-done.6), channel_id=1, source_target_pairs={{0,448},{64,0},{128,64},{192,128},{256,192},{320,256},{384,320},{4... | collective-permute-start | bytes 589832 | tf_op jit(solution)/shard_map/ppermute | solution.py:207
  61.8 2.0 %copy-start.9 = (bf16[8,96,128]{2,1,0:T(8,128)(2,1)}, bf16[8,96,128]{2,1,0:T(8,128)(2,1)S(1)}, u32[]{:S(2)}) copy-start(bf16[8,96,128]{2,1,0:T(8,128)(2,1)S(1)} %collective-permute-done.4.refs_1_) | copy-start | bytes 589828
  61.8 9.7 %collective-permute-start.6 = (bf16[8,96,128]{2,1,0:T(8,128)(2,1)S(1)}, bf16[8,96,128]{2,1,0:T(8,128)(2,1)S(1)}, u32[]{:S(2)}, u32[]{:S(2)}) collective-permute-start(bf16[8,96,128]{2,1,0:T(8,128)(2,1)S(1)} %collective-permute-done.4.refs_1_), channel_id=1, source_target_pairs={{0,64},{64,128},{128,192},{192,256},{256,320},{320,384},{384,448},... | collective-permute-start | bytes 589832 | tf_op jit(solution)/shard_map/ppermute | solution.py:207
  63.8 27.2 %collective-permute-start.2 = (bf16[2,8,128,128]{3,2,1,0:T(8,128)(2,1)S(1)}, bf16[2,8,128,128]{3,2,1,0:T(8,128)(2,1)S(1)}, u32[]{:S(2)}, u32[]{:S(2)}) collective-permute-start(bf16[2,8,128,128]{3,2,1,0:T(8,128)(2,1)S(1)} %pad_maximum_fusion), channel_id=1, source_target_pairs={{0,32},{32,0},{1,33},{33,1},{2,34},{34,2},{3,35},{35,3},{4,36},{36... | collective-permute-start | bytes 1572872 | tf_op jit(solution)/shard_map/ppermute | solution.py:207
  66.9 6.5 %copy-start.10 = (bf16[8,96,128]{2,1,0:T(8,128)(2,1)}, bf16[8,96,128]{2,1,0:T(8,128)(2,1)S(1)}, u32[]{:S(2)}) copy-start(bf16[8,96,128]{2,1,0:T(8,128)(2,1)S(1)} %collective-permute-done.5.refs_2_) | copy-start | bytes 589828
  66.9 13.4 %collective-permute-start.7 = (bf16[8,96,128]{2,1,0:T(8,128)(2,1)S(1)}, bf16[8,96,128]{2,1,0:T(8,128)(2,1)S(1)}, u32[]{:S(2)}, u32[]{:S(2)}) collective-permute-start(bf16[8,96,128]{2,1,0:T(8,128)(2,1)S(1)} %collective-permute-done.5.refs_2_), channel_id=1, source_target_pairs={{0,448},{64,0},{128,64},{192,128},{256,192},{320,256},{384,320},{4... | collective-permute-start | bytes 589832 | tf_op jit(solution)/shard_map/ppermute | solution.py:207
  71.5 2.0 %copy-start.11 = (bf16[8,96,128]{2,1,0:T(8,128)(2,1)}, bf16[8,96,128]{2,1,0:T(8,128)(2,1)S(1)}, u32[]{:S(2)}) copy-start(bf16[8,96,128]{2,1,0:T(8,128)(2,1)S(1)} %collective-permute-done.6.refs_3_) | copy-start | bytes 589828
  71.5 13.7 %collective-permute-start.8 = (bf16[8,96,128]{2,1,0:T(8,128)(2,1)S(1)}, bf16[8,96,128]{2,1,0:T(8,128)(2,1)S(1)}, u32[]{:S(2)}, u32[]{:S(2)}) collective-permute-start(bf16[8,96,128]{2,1,0:T(8,128)(2,1)S(1)} %collective-permute-done.6.refs_3_), channel_id=1, source_target_pairs={{0,64},{64,128},{128,192},{192,256},{256,320},{320,384},{384,448},... | collective-permute-start | bytes 589832 | tf_op jit(solution)/shard_map/ppermute | solution.py:207
  73.5 14.8 %all-to-all-start.1 = ((bf16[8,4,48,128]{3,2,1,0:T(8,128)(2,1)}), bf16[8,4,48,128]{3,2,1,0:T(8,128)(2,1)S(1)}, u32[]{:S(2)}, u32[]{:S(2)}) async-start(bf16[8,4,48,128]{3,2,1,0:T(8,128)(2,1)} %get-tuple-element.11), calls=%async_computation.1 | async-start | bytes 786432 | tf_op jit(solution)/shard_map/all_to_all | solution.py:267
  80.3 14.2 %copy-start.12 = (bf16[8,96,128]{2,1,0:T(8,128)(2,1)}, bf16[8,96,128]{2,1,0:T(8,128)(2,1)S(1)}, u32[]{:S(2)}) copy-start(bf16[8,96,128]{2,1,0:T(8,128)(2,1)S(1)} %collective-permute-done.7.refs_4_) | copy-start | bytes 589828
  80.3 10.7 %collective-permute-start.9 = (bf16[8,96,128]{2,1,0:T(8,128)(2,1)S(1)}, bf16[8,96,128]{2,1,0:T(8,128)(2,1)S(1)}, u32[]{:S(2)}, u32[]{:S(2)}) collective-permute-start(bf16[8,96,128]{2,1,0:T(8,128)(2,1)S(1)} %collective-permute-done.7.refs_4_), channel_id=1, source_target_pairs={{0,448},{64,0},{128,64},{192,128},{256,192},{320,256},{384,320},{4... | collective-permute-start | bytes 589832 | tf_op jit(solution)/shard_map/ppermute | solution.py:207
  85.2 9.3 %copy-start.13 = (bf16[8,96,128]{2,1,0:T(8,128)(2,1)}, bf16[8,96,128]{2,1,0:T(8,128)(2,1)S(1)}, u32[]{:S(2)}) copy-start(bf16[8,96,128]{2,1,0:T(8,128)(2,1)S(1)} %collective-permute-done.8.refs_5_) | copy-start | bytes 589828
  85.2 9.3 %collective-permute-start.10 = (bf16[8,96,128]{2,1,0:T(8,128)(2,1)S(1)}, bf16[8,96,128]{2,1,0:T(8,128)(2,1)S(1)}, u32[]{:S(2)}, u32[]{:S(2)}) collective-permute-start(bf16[8,96,128]{2,1,0:T(8,128)(2,1)S(1)} %collective-permute-done.8.refs_5_), channel_id=1, source_target_pairs={{0,64},{64,128},{128,192},{192,256},{256,320},{320,384},{384,448},... | collective-permute-start | bytes 589832 | tf_op jit(solution)/shard_map/ppermute | solution.py:207
  88.3 0.8 copy-start.2
  91.0 3.5 %copy-start.7 = (bf16[2,8,128,128]{3,2,1,0:T(8,128)(2,1)}, bf16[2,8,128,128]{3,2,1,0:T(8,128)(2,1)S(1)}, u32[]{:S(2)}) copy-start(bf16[2,8,128,128]{3,2,1,0:T(8,128)(2,1)S(1)} %collective-permute-done.2.far_ref) | copy-start | bytes 1572868
  91.0 3.5 %copy-start.14 = (bf16[8,96,128]{2,1,0:T(8,128)(2,1)}, bf16[8,96,128]{2,1,0:T(8,128)(2,1)S(1)}, u32[]{:S(2)}) copy-start(bf16[8,96,128]{2,1,0:T(8,128)(2,1)S(1)} %collective-permute-done.9.refs_6_) | copy-start | bytes 589828
  94.5 0.7 copy-start.15

commit v3 on v2

v3 whole, which is shorter than its diff:
```python
import functools

import jax
import jax.numpy as jnp
import numpy as np
from jax import lax
from jax.experimental import pallas as pl
from jax.experimental.pallas import tpu as pltpu
from jax.sharding import Mesh
from jax.sharding import PartitionSpec as P

HD = 48
AXES = ("y", "xlo", "core", "z", "xhi")
SIZES = (8, 2, 2, 8, 2)
HEADS = ("z", "xhi")
OCT = ("xlo", "core", "xhi")
F32, BF16 = jnp.float32, jnp.bfloat16
VMEM = 56 * 1024 * 1024


def params():
    return pltpu.CompilerParams(vmem_limit_bytes=VMEM)


def dot(a, b, da, db):
    return lax.dot_general(a, b, (((da,), (db,)), ((), ())), preferred_element_type=F32)


def norm_kernel(pos_ref, chain_ref, hot_ref, tok_ref, emb_ref, hemb_ref, out_ref):
    samples, tok_dev, width = tok_ref.shape
    first = pos_ref[0]
    emb = emb_ref[...].astype(F32)
    hemb = hemb_ref[...].astype(F32)
    row_of = lax.broadcasted_iota(jnp.int32, (tok_dev, width), 0)
    cond = jnp.zeros((tok_dev, width), F32)
    for t in range(tok_dev):
        chain = chain_ref[t]
        row = jnp.zeros((1, width), F32)
        for c in range(emb_ref.shape[0]):
            row = row + jnp.where(chain == c, 1.0, 0.0) * emb[c : c + 1]
        hits = jnp.int32(0)
        for i in range(hot_ref.shape[0]):
            hits = hits + jnp.where(hot_ref[i] == first + t, 1, 0)
        row = row + jnp.where(hits > 0, 1.0, 0.0) * hemb
        cond = cond + jnp.where(row_of == t, row, 0.0)
    shifted = tok_ref[...].astype(F32) + cond[None]
    average = jnp.mean(shifted, axis=-1, keepdims=True)
    centred = shifted - average
    spread = jnp.mean(centred * centred, axis=-1, keepdims=True)
    normed = (centred * lax.rsqrt(spread + 1e-05)).reshape(samples * tok_dev, width).astype(BF16)
    for g in range(out_ref.shape[0]):
        out_ref[g] = normed


def bias_kernel(pos_ref, b_ref, keep_ref, away_ref, rows_ref):
    xlo, core, xhi = pos_ref[1], pos_ref[2], pos_ref[3]
    row = lax.broadcasted_iota(jnp.int32, (128, 128), 0)
    col = lax.broadcasted_iota(jnp.int32, (128, 128), 1)
    z, t = (row % 64) // 8, row % 8
    from_q = (z * 2 + row // 64) * 8 + t
    from_k = (z * 2 + jnp.bitwise_xor(row // 64, xhi)) * 8 + t
    pick_q = jnp.where(col == from_q, 1.0, 0.0).astype(BF16)
    pick_k = jnp.where(col == from_k, 1.0, 0.0).astype(BF16)
    for b in range(32):
        rows_ref[b] = dot(pick_q, b_ref[0, :, b * 128 : (b + 1) * 128], 1, 0).astype(BF16)
    for role in range(2):
        xl = jnp.bitwise_xor(xlo, role)
        for y in range(8):
            at = (y * 2 + xl) * 2
            keep_ref[role, y] = dot(pick_k, rows_ref[at + core], 1, 1).astype(BF16)
            away_ref[role, y] = dot(pick_k, rows_ref[at + 1 - core], 1, 1).astype(BF16)


def proj_kernel(pos_ref, x_ref, own_ref, other_ref, q_ref, kv_own_ref, kv_other_ref, gate_ref):
    peers, rows, width = x_ref.shape
    pairs = kv_own_ref.shape[0]
    tok = rows // (2 * pairs)
    xhi = pos_ref[3]
    x = x_ref[...].reshape(peers * rows, width)
    for role, w_ref in enumerate((own_ref, other_ref)):
        kv_ref = (kv_own_ref, kv_other_ref)[role]
        full = dot(x, w_ref[: 4 * HD], 1, 1).reshape(peers, 2 * pairs, tok, 4 * HD)
        for p in range(pairs):
            two = jnp.concatenate([full[:, 2 * p + i].reshape(peers * tok, 4 * HD) for i in range(2)], axis=0)
            turned = jnp.transpose(two)
            queries = (turned[:HD] * (1.0 / HD**0.5)).astype(BF16)
            for d in range(4):
                q_ref[2 * d + jnp.bitwise_xor(xhi, role), p] = queries
            kv_ref[p] = turned[HD : 3 * HD].astype(BF16)
            gate_ref[jnp.bitwise_xor(xhi, role), p] = jax.nn.sigmoid(turned[3 * HD :])


def join(a, b):
    lane = lax.broadcasted_iota(jnp.int32, a.shape, 1)
    return jnp.where(lane < 64, a, pltpu.roll(b, 64, 1)), jnp.where(lane < 64, pltpu.roll(a, 64, 1), b)


def join_kernel(own_ref, other_ref, first_ref, second_ref):
    pairs = own_ref.shape[0]
    for p in range(pairs):
        half, at = divmod(p, pairs // 2)
        out_ref = (first_ref, second_ref)[half]
        both = join(own_ref[p].astype(F32), other_ref[p].astype(F32))
        for i in range(2):
            one = both[i].astype(BF16)
            for y in range(out_ref.shape[0]):
                out_ref[y, 2 * at + i] = one


def join_q_kernel(pos_ref, q_ref, out_ref):
    me = pos_ref[1] * 2 + pos_ref[2]
    for role in range(4):
        d = 2 * jnp.bitwise_xor(me, role)
        for p in range(q_ref.shape[1]):
            even, odd = join(q_ref[d, p].astype(F32), q_ref[d + 1, p].astype(F32))
            out_ref[2 * p, :, role * 128 : (role + 1) * 128] = even.astype(BF16)
            out_ref[2 * p + 1, :, role * 128 : (role + 1) * 128] = odd.astype(BF16)


def attend_kernel(pos_ref, q_ref, keep_ref, recv_ref, far_ref, kv_ref, out_ref):
    me = pos_ref[1] * 2 + pos_ref[2]
    acc, top = [None, None], [None, None]
    for y in range(0, 8, 2):
        bias = [
            jnp.concatenate([keep_ref[0, b], recv_ref[0, b], far_ref[0, b], far_ref[1, b]], axis=1).astype(F32)
            for b in (y, y + 1)
        ]
        bias = jnp.concatenate(bias, axis=0)
        for i in range(2):
            keys = [jnp.transpose(kv_ref[b, i, :HD].astype(F32)).astype(BF16) for b in (y, y + 1)]
            keys = jnp.concatenate(keys, axis=0)
            vals = jnp.concatenate([kv_ref[y, i, HD:], kv_ref[y + 1, i, HD:]], axis=1)
            vals = jnp.concatenate([vals, jnp.ones((16, vals.shape[1]), BF16)], axis=0)
            scores = jnp.dot(keys, q_ref[i], preferred_element_type=F32) + bias
            best = jnp.max(scores, axis=0, keepdims=True)
            if top[i] is not None:
                best = jnp.maximum(best, top[i])
            probs = jnp.exp(scores - best).astype(BF16)
            part = jnp.dot(vals, probs, preferred_element_type=F32)
            if top[i] is not None:
                part = part + acc[i] * jnp.exp(top[i] - best)
            acc[i], top[i] = part, best
    row = lax.broadcasted_iota(jnp.int32, (16, 128), 0)
    for role in range(4):
        d = 2 * jnp.bitwise_xor(me, role)
        tiles = []
        for i in range(2):
            mine = acc[i][:, role * 128 : (role + 1) * 128]
            total = mine[HD : HD + 1]
            lse = top[i][:, role * 128 : (role + 1) * 128] + jnp.log(total)
            hi = lse.astype(BF16).astype(F32)
            mid = (lse - hi).astype(BF16).astype(F32)
            low = lse - hi - mid
            tail = jnp.where(row == 0, hi, jnp.where(row == 1, mid, jnp.where(row == 2, low, 0.0)))
            tiles.append(jnp.concatenate([mine[:HD] / total, tail], axis=0))
        even, odd = join(tiles[0], tiles[1])
        out_ref[d, 0] = even.astype(BF16)
        out_ref[d + 1, 0] = odd.astype(BF16)


def merge_kernel(pos_ref, first_ref, second_ref, gate_ref, out_ref):
    xhi = pos_ref[3]
    per_half = first_ref.shape[1]
    peers = out_ref.shape[0]
    tok = 64 // peers
    for p in range(2 * per_half):
        half, at = divmod(p, per_half)
        p_ref = (first_ref, second_ref)[half]
        gated = []
        for role in range(2):
            h = jnp.bitwise_xor(xhi, role)
            rows = [p_ref[2 * i + h, at].astype(F32) for i in range(4)]
            lse = [r[HD : HD + 1] + r[HD + 1 : HD + 2] + r[HD + 2 : HD + 3] for r in rows]
            top = functools.reduce(jnp.maximum, lse)
            weight = [jnp.exp(v - top) for v in lse]
            gated.append(sum(w * r[:HD] for w, r in zip(weight, rows)) / sum(weight) * gate_ref[h, p])
        turned = jnp.transpose(jnp.concatenate(gated + [jnp.zeros((128 - 2 * HD, 128), F32)], axis=0))
        split = turned.reshape(2, peers, tok, 128)
        for g in range(peers):
            both = jnp.concatenate([split[0, g], split[1, g]], axis=0)
            out_ref[g, 2 * tok * p : 2 * tok * (p + 1)] = both.astype(BF16)


def out_kernel(pos_ref, g_ref, *refs):
    w_refs, out_ref = refs[:-1], refs[-1]
    total = None
    for by, w_ref in enumerate(w_refs):
        gated = g_ref[lax.rem(pos_ref[4] + 8 - by, 8)]
        term = jnp.dot(gated[:, : 2 * HD], w_ref[...], preferred_element_type=F32)
        total = term if total is None else total + term
    out_ref[...] = total.astype(BF16)


def shift(x, axis, by):
    n = SIZES[AXES.index(axis)]
    return lax.ppermute(x, axis, [(i, (i + by) % n) for i in range(n)])


def body(tokens, chain_id, hotspots, chain_embed, hot_embed, w_proj, pair_bias, w_out):
    samples, tok_dev, width = tokens.shape
    pairs, peers = samples // 2, 8
    at = {a: lax.axis_index(a) for a in AXES}
    first = ((((at["y"] * 2 + at["xlo"]) * 2 + at["core"]) * 8 + at["z"]) * 2 + at["xhi"]) * tok_dev
    pos = jnp.stack([first, at["xlo"], at["core"], at["xhi"], at["z"]])
    vm = pl.BlockSpec(memory_space=pltpu.VMEM)
    sm = pl.BlockSpec(memory_space=pltpu.SMEM)

    def call(kernel, specs, out, *args, scratch=()):
        shapes = [jax.ShapeDtypeStruct(s, t) for s, t in out]
        return pl.pallas_call(
            kernel,
            out_shape=shapes,
            in_specs=specs,
            out_specs=[vm] * len(out),
            scratch_shapes=scratch,
            compiler_params=params(),
        )(*args)

    def exchange(x, axes):
        return lax.all_to_all(x, axes, split_axis=0, concat_axis=0, tiled=True)

    weights = jnp.concatenate([jnp.transpose(w_proj), w_out], axis=0)
    weights_other = shift(weights, "xhi", 1)
    keep, away = call(
        bias_kernel,
        [sm, vm],
        [((2, 8, 128, 128), BF16)] * 2,
        pos,
        pair_bias,
        scratch=[pltpu.VMEM((32, 128, 128), BF16)],
    )
    recv = shift(away, "core", 1)
    far_out = jnp.stack([keep[1], recv[1]])

    (copies,) = call(
        norm_kernel,
        [sm, sm, sm, vm, vm, vm],
        [((peers, samples * tok_dev, width), BF16)],
        pos,
        chain_id,
        hotspots,
        tokens,
        chain_embed,
        hot_embed[None],
    )
    gathered, far_out = lax.optimization_barrier((exchange(copies, "z"), far_out))
    far = shift(far_out, "xlo", 1)
    q_out, kv_own, kv_other, gate = call(
        proj_kernel,
        [sm, vm, vm, vm],
        [
            ((8, pairs, HD, 128), BF16),
            ((pairs, 2 * HD, 128), BF16),
            ((pairs, 2 * HD, 128), BF16),
            ((2, pairs, HD, 128), F32),
        ],
        pos,
        gathered,
        weights,
        weights_other,
    )
    kv_other, q_in = lax.optimization_barrier((shift(kv_other, "xhi", 1), exchange(q_out, OCT)))
    half = samples // 2
    kv = call(join_kernel, [vm, vm], [((8, half, 2 * HD, 128), BF16)] * 2, kv_own, kv_other)
    w_rows = jnp.concatenate([weights[4 * HD :], weights_other[4 * HD :]], axis=0)
    w_rows, kv_first = lax.optimization_barrier((w_rows, kv[0]))
    w_all = [w_rows] + [shift(w_rows, "z", by) for by in range(1, peers)]
    (q_all,) = call(join_q_kernel, [sm, vm], [((samples, HD, 512), BF16)], pos, q_in)
    kv_first, kv_second, far, q_all, *w_all[1:5] = lax.optimization_barrier(
        (exchange(kv_first, "y"), kv[1], far, q_all, *w_all[1:5])
    )
    kv_second, *w_all[5:] = lax.optimization_barrier((exchange(kv_second, "y"), *w_all[5:]))
    kv_in = [kv_first, kv_second]

    whole = pl.BlockSpec((2, 8, 128, 128), lambda s, _: (0, 0, 0, 0))
    mine = []
    for part in range(2):
        steps = pairs // 2
        result = pl.pallas_call(
            attend_kernel,
            out_shape=jax.ShapeDtypeStruct((8, steps, 64, 128), BF16),
            grid_spec=pltpu.PrefetchScalarGridSpec(
                num_scalar_prefetch=1,
                grid=(steps,),
                in_specs=[
                    pl.BlockSpec((2, HD, 512), lambda s, _, base=part * steps: (base + s, 0, 0)),
                    whole,
                    whole,
                    whole,
                    pl.BlockSpec((8, 2, 2 * HD, 128), lambda s, _: (0, s, 0, 0)),
                ],
                out_specs=pl.BlockSpec((8, 1, 64, 128), lambda s, _: (0, s, 0, 0)),
            ),
            compiler_params=params(),
            cost_estimate=pl.CostEstimate(flops=4 * half * 512 * 1024 * 64, bytes_accessed=5 << 20, transcendentals=half << 19),
        )(pos, q_all, keep, recv, far, kv_in[part])
        if part == 0:
            result, kv_in[1] = lax.optimization_barrier((result, kv_in[1]))
        mine.append(exchange(result, OCT))
    (gated,) = call(
        merge_kernel,
        [sm, vm, vm, vm],
        [((peers, samples * tok_dev, 128), BF16)],
        pos,
        mine[0],
        mine[1],
        gate,
    )
    (update,) = call(
        out_kernel,
        [sm, vm] + [vm] * peers,
        [((samples * tok_dev, width), BF16)],
        pos,
        exchange(gated, "z"),
        *w_all,
    )
    return update.reshape(samples, tok_dev, width)


def solution(mesh):
    fine = Mesh(np.asarray(mesh.devices).reshape(SIZES), AXES)
    blk = ("y", "xlo", "core")
    in_specs = (
        P(None, AXES, None),
        P(AXES),
        P(),
        P(),
        P(),
        P(None, HEADS),
        P(HEADS, blk, None),
        P(HEADS, None),
    )
    return jax.shard_map(body, mesh=fine, in_specs=in_specs, out_specs=P(None, AXES, None), check_vma=False)
```

time: 158 us -> 174 us (1.10)
  starting transfers between devices: 55.6 us -> 78.2 us
  blocking collectives: 42.9 us -> 24.2 us
  waiting for transfers between devices: 11.8 us -> 28.8 us
  Pallas kernels: 39.7 us -> 34.1 us
    all_to_all x2, blocking collectives: 42.9 us -> 24.2 us  [exchange(): return lax.all_to_all(x, axes, split_axis=0, concat_axis=0, tiled=True)]
    all_to_all x2 -> x5, starting transfers between devices: 17.9 us -> 33.8 us  [exchange(): return lax.all_to_all(x, axes, split_axis=0, concat_axis=0, tiled=True)]
    ppermute x11, waiting for transfers between devices: 7.36 us -> 17.4 us  [shift(): return lax.ppermute(x, axis, [(i, (i + by) % n) for i in range(n)])]
    pallas_call x7, Pallas kernels: 25.6 us -> 17.4 us  [call(): pl.pallas_call(kernel, out_shape=shapes, in_specs=specs, out_specs=[vm] *...]
    all_to_all x2 -> x5, waiting for transfers between devices: 4.48 us -> 11.4 us  [exchange(): return lax.all_to_all(x, axes, split_axis=0, concat_axis=0, tiled=True)]
    ppermute x11, starting transfers between devices: 37.7 us -> 44.4 us  [shift(): return lax.ppermute(x, axis, [(i, (i + by) % n) for i in range(n)])]
    pallas_call x1 -> x2, Pallas kernels: 14.1 us -> 16.7 us  [body(): pl.pallas_call(attend_kernel, out_shape=jax.ShapeDtypeStruct((8, steps, 6...]
    unnamed x38 -> x46, local copies, waits for them, and re-layouts: 4.72 us -> 5.36 us
  transfers between devices with their start and end apart: 13 -> 16, of which waited for: 5 -> 5; matrix products, arithmetic and copies ran while one was open for 0% -> 0% of each run, Pallas kernels for 12% -> 13%
where the time goes in v3:
time: 174 us; the launch traced here: 172 us
  starting transfers between devices  78.2 us (45%)
  Pallas kernels  34.1 us (20%)
  waiting for transfers between devices  28.8 us (17%)
  blocking collectives  24.2 us (14%)
  local copies, waits for them, and re-layouts  6.59 us (4%)
    ppermute x11, starting transfers between devices, shift(): return lax.ppermute(x, axis, [(i, (i + by) % n) for i in range(n)])  44.4 us
    all_to_all x5, starting transfers between devices, exchange(): return lax.all_to_all(x, axes, split_axis=0, concat_axis=0, tiled=True)  33.8 us
    all_to_all x2, blocking collectives, exchange(): return lax.all_to_all(x, axes, split_axis=0, concat_axis=0, tiled=True)  24.2 us
    ppermute x11, waiting for transfers between devices, shift(): return lax.ppermute(x, axis, [(i, (i + by) % n) for i in range(n)])  17.4 us
    pallas_call x7, Pallas kernels, call(): pl.pallas_call(kernel, out_shape=shapes, in_specs=specs, out_specs=[vm] *...  17.4 us
    pallas_call x2, Pallas kernels, body(): pl.pallas_call(attend_kernel, out_shape=jax.ShapeDtypeStruct((8, steps, 6...  16.7 us
    all_to_all x5, waiting for transfers between devices, exchange(): return lax.all_to_all(x, axes, split_axis=0, concat_axis=0, tiled=True)  11.4 us
    unnamed x46, local copies, waits for them, and re-layouts  5.36 us
  transfers between devices with their start and end apart: 16, of which 5 were waited for; matrix products, arithmetic and copies ran while one was open for 0% of the time, Pallas kernels for 13%

profile of v3, /device:TPU:1, one launch (start us, length us, event | category | flops | bytes accessed | tf_op | source)
XLA Modules:
  0.0 172.2 jit_solution(11420325496080571122)
XLA Ops:
  0.0 0.7 copy-done.20
  0.7 0.6 broadcast_in_dim.3.hemb_ref
  1.3 0.6 stack.26.pos_ref
  1.9 2.2 %shard_map.82 = bf16[8,64,768]{2,1,0:T(8,128)(2,1)} custom-call(s32[5]{0:T(128)} %stack.26.pos_ref, s32[8]{0:T(128)} %chain_ref.1, s32[16]{0:T(128)} %hot_ref.1, bf16[8,8,768]{2,1,0:T(8,128)(2,1)} %tok_ref.1, bf16[4,768]{1,0:T(4,128)(2,1)} %emb_ref.1, bf16[1,768]{1,0:T(2,128)(2,1)} %broadcast_in_dim.3.hemb_ref), custom_call_target="tpu_custom_call" | custom-call | tf_op jit(solution)/shard_map/pallas_call | solution.py:210
  4.1 10.9 %all-to-all-start = ((bf16[8,64,768]{2,1,0:T(8,128)(2,1)}), bf16[8,64,768]{2,1,0:T(8,128)(2,1)S(1)}, u32[]{:S(2)}, u32[]{:S(2)}) async-start(bf16[8,64,768]{2,1,0:T(8,128)(2,1)} %shard_map.82), calls=%async_computation | async-start | bytes 1572864 | tf_op jit(solution)/shard_map/all_to_all | solution.py:220
  15.0 0.0 copy-start.9
  15.0 3.6 %shard_map.83 = (bf16[2,8,128,128]{3,2,1,0:T(8,128)(2,1)}, bf16[2,8,128,128]{3,2,1,0:T(8,128)(2,1)}) custom-call(s32[5]{0:T(128)} %stack.26.pos_ref, bf16[1,128,4096]{2,1,0:T(8,128)(2,1)} %b_ref.1), custom_call_target="tpu_custom_call" | custom-call | tf_op jit(solution)/shard_map/pallas_call | solution.py:210
  18.6 3.0 %collective-permute-start.1 = (bf16[2,8,128,128]{3,2,1,0:T(8,128)(2,1)}, bf16[2,8,128,128]{3,2,1,0:T(8,128)(2,1)S(1)}, u32[]{:S(2)}, u32[]{:S(2)}) collective-permute-start(bf16[2,8,128,128]{3,2,1,0:T(8,128)(2,1)} %get-tuple-element.34), channel_id=1, source_target_pairs={{0,16},{16,0},{1,17},{17,1},{2,18},{18,2},{3,19},{19,3},{4,20},{20... | collective-permute-start | bytes 1572872 | tf_op jit(solution)/shard_map/ppermute | solution.py:196
  21.5 0.0 copy-done.8
  21.6 0.0 copy-done.9
  21.6 0.0 copy-start.2
  21.6 4.7 %collective-permute-start = (bf16[240,768]{1,0:T(8,128)(2,1)S(1)}, bf16[240,768]{1,0:T(8,128)(2,1)S(1)}, u32[]{:S(2)}, u32[]{:S(2)}) collective-permute-start(bf16[240,768]{1,0:T(8,128)(2,1)S(1)} %pad_maximum_fusion.1.own_ref), channel_id=1, source_target_pairs={{0,1},{1,0},{2,3},{3,2},{4,5},{5,4},{6,7},{7,6},{8,9},{9,8},{10,11... | collective-permute-start | bytes 1105928 | tf_op jit(solution)/shard_map/ppermute | solution.py:196
  26.3 0.0 copy-done.17
  26.3 0.0 collective-permute-done.1.recv_ref
  26.3 0.8 copy-done.18
  27.2 0.1 pad_maximum_fusion
  27.2 11.3 %all-to-all-done.x_ref = bf16[8,64,768]{2,1,0:T(8,128)(2,1)S(1)} async-done(((bf16[8,64,768]{2,1,0:T(8,128)(2,1)}), bf16[8,64,768]{2,1,0:T(8,128)(2,1)S(1)}, u32[]{:S(2)}, u32[]{:S(2)}) %all-to-all-start) | async-done | bytes 786464 | tf_op jit(solution)/shard_map/all_to_all | solution.py:220
  38.6 0.0 collective-permute-done.other_ref
  38.6 0.9 copy-done
  39.5 0.7 copy-done.7
  40.2 3.1 %shard_map.84 = (bf16[8,4,48,128]{3,2,1,0:T(8,128)(2,1)}, bf16[4,96,128]{2,1,0:T(8,128)(2,1)}, bf16[4,96,128]{2,1,0:T(8,128)(2,1)}, f32[2,4,48,128]{3,2,1,0:T(8,128)}) custom-call(s32[5]{0:T(128)} %stack.26.pos_ref, bf16[8,64,768]{2,1,0:T(8,128)(2,1)} %copy-done, bf16[240,768]{1,0:T(8,128)(2,1)} %copy-done.2, bf16[240,768]{1,0:T(8,128)(2,1)} %copy-done.7), custom_call_target="tpu_custom_call" | custom-call | tf_op jit(solution)/shard_map/pallas_call | solution.py:210
  43.3 4.9 %all-to-all-start.1 = ((bf16[8,4,48,128]{3,2,1,0:T(8,128)(2,1)}), bf16[8,4,48,128]{3,2,1,0:T(8,128)(2,1)S(1)}, u32[]{:S(2)}, u32[]{:S(2)}) async-start(bf16[8,4,48,128]{3,2,1,0:T(8,128)(2,1)} %get-tuple-element.38), calls=%async_computation.1 | async-start | bytes 786432 | tf_op jit(solution)/shard_map/all_to_all | solution.py:220
  48.2 0.0 copy-done.22
  48.2 4.9 %collective-permute-start.2 = (bf16[4,96,128]{2,1,0:T(8,128)(2,1)S(1)}, bf16[4,96,128]{2,1,0:T(8,128)(2,1)S(1)}, u32[]{:S(2)}, u32[]{:S(2)}) collective-permute-start(bf16[4,96,128]{2,1,0:T(8,128)(2,1)S(1)} %copy-done.22), channel_id=1, source_target_pairs={{0,1},{1,0},{2,3},{3,2},{4,5},{5,4},{6,7},{7,6},{8,9},{9,8},{10,11... | collective-permute-start | bytes 294920 | tf_op jit(solution)/shard_map/ppermute | solution.py:196
  53.2 5.2 %collective-permute-done.2.other_ref = bf16[4,96,128]{2,1,0:T(8,128)(2,1)S(1)} collective-permute-done((bf16[4,96,128]{2,1,0:T(8,128)(2,1)S(1)}, bf16[4,96,128]{2,1,0:T(8,128)(2,1)S(1)}, u32[]{:S(2)}, u32[]{:S(2)}) %collective-permute-start.2) | collective-permute-done | bytes 98336 | tf_op jit(solution)/shard_map/ppermute | solution.py:196
  58.4 0.0 all-to-all-done.1.q_ref
  58.4 0.6 copy-done.19
  59.0 2.2 %shard_map.85 = (bf16[8,4,96,128]{3,2,1,0:T(8,128)(2,1)}, bf16[8,4,96,128]{3,2,1,0:T(8,128)(2,1)}) custom-call(bf16[4,96,128]{2,1,0:T(8,128)(2,1)} %get-tuple-element.36.own_ref, bf16[4,96,128]{2,1,0:T(8,128)(2,1)} %copy-done.19), custom_call_target="tpu_custom_call" | custom-call | tf_op jit(solution)/shard_map/pallas_call | solution.py:210
  61.3 0.0 copy-done.1
  61.3 6.8 %all-to-all-start.2 = ((bf16[8,4,96,128]{3,2,1,0:T(8,128)(2,1)}), bf16[8,4,96,128]{3,2,1,0:T(8,128)(2,1)S(1)}, u32[]{:S(2)}, u32[]{:S(2)}) async-start(bf16[8,4,96,128]{3,2,1,0:T(8,128)(2,1)} %get-tuple-element.41), calls=%async_computation.2 | async-start | bytes 1572864 | tf_op jit(solution)/shard_map/all_to_all | solution.py:220
  68.1 2.2 %collective-permute-start.3 = (bf16[2,8,128,128]{3,2,1,0:T(8,128)(2,1)S(1)}, bf16[2,8,128,128]{3,2,1,0:T(8,128)(2,1)S(1)}, u32[]{:S(2)}, u32[]{:S(2)}) collective-permute-start(bf16[2,8,128,128]{3,2,1,0:T(8,128)(2,1)S(1)} %pad_maximum_fusion), channel_id=1, source_target_pairs={{0,32},{32,0},{1,33},{33,1},{2,34},{34,2},{3,35},{35,3},{4,36},{36... | collective-permute-start | bytes 1572872 | tf_op jit(solution)/shard_map/ppermute | solution.py:196
  70.3 2.2 %collective-permute-start.4 = (bf16[96,768]{1,0:T(8,128)(2,1)S(1)}, bf16[96,768]{1,0:T(8,128)(2,1)S(1)}, u32[]{:S(2)}, u32[]{:S(2)}) collective-permute-start(bf16[96,768]{1,0:T(8,128)(2,1)S(1)} %pad_maximum_fusion.2.refs_0_), channel_id=1, source_target_pairs={{0,2},{2,4},{4,6},{6,8},{8,10},{10,12},{12,14},{14,0},{1,3},{3,5},... | collective-permute-start | bytes 442376 | tf_op jit(solution)/shard_map/ppermute | solution.py:196
  72.5 1.9 %collective-permute-start.5 = (bf16[96,768]{1,0:T(8,128)(2,1)S(1)}, bf16[96,768]{1,0:T(8,128)(2,1)S(1)}, u32[]{:S(2)}, u32[]{:S(2)}) collective-permute-start(bf16[96,768]{1,0:T(8,128)(2,1)S(1)} %pad_maximum_fusion.2.refs_0_), channel_id=1, source_target_pairs={{0,4},{2,6},{4,8},{6,10},{8,12},{10,14},{12,0},{14,2},{1,5},{3,7},... | collective-permute-start | bytes 442376 | tf_op jit(solution)/shard_map/ppermute | solution.py:196
  74.4 4.1 %collective-permute-start.6 = (bf16[96,768]{1,0:T(8,128)(2,1)S(1)}, bf16[96,768]{1,0:T(8,128)(2,1)S(1)}, u32[]{:S(2)}, u32[]{:S(2)}) collective-permute-start(bf16[96,768]{1,0:T(8,128)(2,1)S(1)} %pad_maximum_fusion.2.refs_0_), channel_id=1, source_target_pairs={{0,6},{2,8},{4,10},{6,12},{8,14},{10,0},{12,2},{14,4},{1,7},{3,9},... | collective-permute-start | bytes 442376 | tf_op jit(solution)/shard_map/ppermute | solution.py:196
  78.5 5.3 %collective-permute-start.7 = (bf16[96,768]{1,0:T(8,128)(2,1)S(1)}, bf16[96,768]{1,0:T(8,128)(2,1)S(1)}, u32[]{:S(2)}, u32[]{:S(2)}) collective-permute-start(bf16[96,768]{1,0:T(8,128)(2,1)S(1)} %pad_maximum_fusion.2.refs_0_), channel_id=1, source_target_pairs={{0,8},{2,10},{4,12},{6,14},{8,0},{10,2},{12,4},{14,6},{1,9},{3,11}... | collective-permute-start | bytes 442376 | tf_op jit(solution)/shard_map/ppermute | solution.py:196
  83.8 1.9 %shard_map.86.q_ref = bf16[8,48,512]{2,1,0:T(8,128)(2,1)} custom-call(s32[5]{0:T(128)} %stack.26.pos_ref, bf16[8,4,48,128]{3,2,1,0:T(8,128)(2,1)} %copy-done.1), custom_call_target="tpu_custom_call" | custom-call | tf_op jit(solution)/shard_map/pallas_call | solution.py:210
  85.7 0.0 collective-permute-done.4.refs_1_
  85.7 0.0 collective-permute-done.5.refs_2_
  85.7 8.5 %collective-permute-done.6.refs_3_ = bf16[96,768]{1,0:T(8,128)(2,1)S(1)} collective-permute-done((bf16[96,768]{1,0:T(8,128)(2,1)S(1)}, bf16[96,768]{1,0:T(8,128)(2,1)S(1)}, u32[]{:S(2)}, u32[]{:S(2)}) %collective-permute-start.6) | collective-permute-done | bytes 147488 | tf_op jit(solution)/shard_map/ppermute | solution.py:196
  94.2 1.6 collective-permute-done.7.refs_4_
  95.9 0.0 collective-permute-done.3.far_ref
  95.9 0.0 all-to-all-done.2.kv_ref
  95.9 0.6 copy-done.13
  96.5 0.3 copy-done.4
  96.8 6.8 %all-to-all-start.3 = ((bf16[8,4,96,128]{3,2,1,0:T(8,128)(2,1)}), bf16[8,4,96,128]{3,2,1,0:T(8,128)(2,1)S(1)}, u32[]{:S(2)}, u32[]{:S(2)}) async-start(bf16[8,4,96,128]{3,2,1,0:T(8,128)(2,1)} %get-tuple-element.49), calls=%async_computation.3 | async-start | bytes 1572864 | tf_op jit(solution)/shard_map/all_to_all | solution.py:220
  103.6 4.0 %collective-permute-start.8 = (bf16[96,768]{1,0:T(8,128)(2,1)S(1)}, bf16[96,768]{1,0:T(8,128)(2,1)S(1)}, u32[]{:S(2)}, u32[]{:S(2)}) collective-permute-start(bf16[96,768]{1,0:T(8,128)(2,1)S(1)} %pad_maximum_fusion.2.refs_0_), channel_id=1, source_target_pairs={{0,10},{2,12},{4,14},{6,0},{8,2},{10,4},{12,6},{14,8},{1,11},{3,13... | collective-permute-start | bytes 442376 | tf_op jit(solution)/shard_map/ppermute | solution.py:196
  107.6 6.8 %collective-permute-start.9 = (bf16[96,768]{1,0:T(8,128)(2,1)S(1)}, bf16[96,768]{1,0:T(8,128)(2,1)S(1)}, u32[]{:S(2)}, u32[]{:S(2)}) collective-permute-start(bf16[96,768]{1,0:T(8,128)(2,1)S(1)} %pad_maximum_fusion.2.refs_0_), channel_id=1, source_target_pairs={{0,12},{2,14},{4,0},{6,2},{8,4},{10,6},{12,8},{14,10},{1,13},{3,15... | collective-permute-start | bytes 442376 | tf_op jit(solution)/shard_map/ppermute | solution.py:196
  114.5 5.4 %collective-permute-start.10 = (bf16[96,768]{1,0:T(8,128)(2,1)S(1)}, bf16[96,768]{1,0:T(8,128)(2,1)S(1)}, u32[]{:S(2)}, u32[]{:S(2)}) collective-permute-start(bf16[96,768]{1,0:T(8,128)(2,1)S(1)} %pad_maximum_fusion.2.refs_0_), channel_id=1, source_target_pairs={{0,14},{2,0},{4,2},{6,4},{8,6},{10,8},{12,10},{14,12},{1,15},{3,1}... | collective-permute-start | bytes 442376 | tf_op jit(solution)/shard_map/ppermute | solution.py:196
  119.9 0.0 copy-done.21
  119.9 8.4 %shard_map.87 = bf16[8,2,64,128]{3,2,1,0:T(8,128)(2,1)} custom-call(s32[5]{0:T(128)} %stack.26.pos_ref, bf16[8,48,512]{2,1,0:T(8,128)(2,1)} %shard_map.86.q_ref, bf16[2,8,128,128]{3,2,1,0:T(8,128)(2,1)} %get-tuple-element.33.keep_ref, bf16[2,8,128,128]{3,2,1,0:T(8,128)(2,1)} %copy-done.18, bf16[2,8,128,128]{3,2,1,0:T(8,128)(2,1)} %copy-done.21, ...), custom_call_target="tpu_custom_call" | custom-call | flops 536870912 | bytes 5242880 | tf_op jit(solution)/shard_map/pallas_call | solution.py:279
  128.2 0.0 collective-permute-done.8.refs_5_
  128.2 0.0 collective-permute-done.9.refs_6_
  128.3 2.0 %collective-permute-done.10.refs_7_ = bf16[96,768]{1,0:T(8,128)(2,1)S(1)} collective-permute-done((bf16[96,768]{1,0:T(8,128)(2,1)S(1)}, bf16[96,768]{1,0:T(8,128)(2,1)S(1)}, u32[]{:S(2)}, u32[]{:S(2)}) %collective-permute-start.10) | collective-permute-done | bytes 147488 | tf_op jit(solution)/shard_map/ppermute | solution.py:196
  130.3 0.0 all-to-all-done.3.kv_ref
  130.3 0.6 copy-done.16
  131.0 4.4 %all-to-all-start.4 = ((bf16[8,2,64,128]{3,2,1,0:T(8,128)(2,1)}), bf16[8,2,64,128]{3,2,1,0:T(8,128)(2,1)S(1)}, u32[]{:S(2)}, u32[]{:S(2)}) async-start(bf16[8,2,64,128]{3,2,1,0:T(8,128)(2,1)} %shard_map.87), calls=%async_computation.4 | async-start | bytes 524288 | tf_op jit(solution)/shard_map/all_to_all | solution.py:220
  135.3 0.0 copy-done.5
  135.3 8.4 %shard_map.88 = bf16[8,2,64,128]{3,2,1,0:T(8,128)(2,1)} custom-call(s32[5]{0:T(128)} %stack.26.pos_ref, bf16[8,48,512]{2,1,0:T(8,128)(2,1)} %shard_map.86.q_ref, bf16[2,8,128,128]{3,2,1,0:T(8,128)(2,1)} %get-tuple-element.33.keep_ref, bf16[2,8,128,128]{3,2,1,0:T(8,128)(2,1)} %copy-done.18, bf16[2,8,128,128]{3,2,1,0:T(8,128)(2,1)} %copy-done.21, ...), custom_call_target="tpu_custom_call" | custom-call | flops 536870912 | bytes 5242880 | tf_op jit(solution)/shard_map/pallas_call | solution.py:279
  143.7 0.0 all-to-all-done.4.first_ref
  143.7 11.5 %all_to_all.35.second_ref = bf16[8,2,64,128]{3,2,1,0:T(8,128)(2,1)} all-to-all(bf16[8,2,64,128]{3,2,1,0:T(8,128)(2,1)} %shard_map.88), channel_id=1, replica_groups=mesh['y'=8,'xlo'=2,'core'=2,'z'=8,'xhi'=2] {'xlo','core','xhi'}, dimensions={0} | all-to-all | bytes 524288 | tf_op jit(solution)/shard_map/all_to_all | solution.py:220
  155.2 0.0 copy-done.3
  155.2 2.0 %shard_map.89 = bf16[8,64,128]{2,1,0:T(8,128)(2,1)} custom-call(s32[5]{0:T(128)} %stack.26.pos_ref, bf16[8,2,64,128]{3,2,1,0:T(8,128)(2,1)} %copy-done.3, bf16[8,2,64,128]{3,2,1,0:T(8,128)(2,1)} %all_to_all.35.second_ref, f32[2,4,48,128]{3,2,1,0:T(8,128)} %get-tuple-element.53.gate_ref), custom_call_target="tpu_custom_call" | custom-call | tf_op jit(solution)/shard_map/pallas_call | solution.py:210
  157.1 12.7 %all_to_all.36.g_ref = bf16[8,64,128]{2,1,0:T(8,128)(2,1)} all-to-all(bf16[8,64,128]{2,1,0:T(8,128)(2,1)} %shard_map.89), channel_id=1, replica_groups=mesh['y'=8,'xlo'=2,'core'=2,'z'=8,'xhi'=2] {'z'}, dimensions={0} | all-to-all | bytes 262144 | tf_op jit(solution)/shard_map/all_to_all | solution.py:220
  169.9 2.4 %shard_map.90 = bf16[64,768]{1,0:T(8,128)(2,1)} custom-call(s32[5]{0:T(128)} %stack.26.pos_ref, bf16[8,64,128]{2,1,0:T(8,128)(2,1)} %all_to_all.36.g_ref, bf16[96,768]{1,0:T(8,128)(2,1)} %copy-done.6, bf16[96,768]{1,0:T(8,128)(2,1)} %copy-done.10, bf16[96,768]{1,0:T(8,128)(2,1)} %copy-done.11, bf16[96,768]{1,0:T(8,128)(2,1)} %copy-done.12, ...), custom_call_target="tpu_custom_call" | custom-call | tf_op jit(solution)/shard_map/pallas_call | solution.py:210
  (34 shorter events, 0.1 us)
Async XLA Ops:
  0.0 0.7 copy-start.20
  4.1 34.4 %all-to-all-start = ((bf16[8,64,768]{2,1,0:T(8,128)(2,1)}), bf16[8,64,768]{2,1,0:T(8,128)(2,1)S(1)}, u32[]{:S(2)}, u32[]{:S(2)}) async-start(bf16[8,64,768]{2,1,0:T(8,128)(2,1)} %shard_map.82), calls=%async_computation | async-start | bytes 1572864 | tf_op jit(solution)/shard_map/all_to_all | solution.py:220
  15.0 6.6 %copy-start.8 = (bf16[48,768]{1,0:T(8,128)(2,1)S(1)}, bf16[48,768]{1,0:T(8,128)(2,1)}, u32[]{:S(2)}) copy-start(bf16[48,768]{1,0:T(8,128)(2,1)} %param.15) | copy-start | bytes 221188
  15.0 6.6 %copy-start.9 = (bf16[768,192]{0,1:T(8,128)(2,1)S(1)}, bf16[768,192]{0,1:T(8,128)(2,1)}, u32[]{:S(2)}) copy-start(bf16[768,192]{0,1:T(8,128)(2,1)} %param.13) | copy-start | bytes 884740
  18.6 7.7 %copy-start.17 = (bf16[2,8,128,128]{3,2,1,0:T(8,128)(2,1)S(1)}, bf16[2,8,128,128]{3,2,1,0:T(8,128)(2,1)}, u32[]{:S(2)}) copy-start(bf16[2,8,128,128]{3,2,1,0:T(8,128)(2,1)} %get-tuple-element.33.keep_ref) | copy-start | bytes 1572868
  18.6 7.8 %collective-permute-start.1 = (bf16[2,8,128,128]{3,2,1,0:T(8,128)(2,1)}, bf16[2,8,128,128]{3,2,1,0:T(8,128)(2,1)S(1)}, u32[]{:S(2)}, u32[]{:S(2)}) collective-permute-start(bf16[2,8,128,128]{3,2,1,0:T(8,128)(2,1)} %get-tuple-element.34), channel_id=1, source_target_pairs={{0,16},{16,0},{1,17},{17,1},{2,18},{18,2},{3,19},{19,3},{4,20},{20... | collective-permute-start | bytes 1572872 | tf_op jit(solution)/shard_map/ppermute | solution.py:196
  21.6 5.6 %copy-start.2 = (bf16[240,768]{1,0:T(8,128)(2,1)}, bf16[240,768]{1,0:T(8,128)(2,1)S(1)}, u32[]{:S(2)}) copy-start(bf16[240,768]{1,0:T(8,128)(2,1)S(1)} %pad_maximum_fusion.1.own_ref) | copy-start | bytes 1105924
  21.6 17.0 %collective-permute-start = (bf16[240,768]{1,0:T(8,128)(2,1)S(1)}, bf16[240,768]{1,0:T(8,128)(2,1)S(1)}, u32[]{:S(2)}, u32[]{:S(2)}) collective-permute-start(bf16[240,768]{1,0:T(8,128)(2,1)S(1)} %pad_maximum_fusion.1.own_ref), channel_id=1, source_target_pairs={{0,1},{1,0},{2,3},{3,2},{4,5},{5,4},{6,7},{7,6},{8,9},{9,8},{10,11... | collective-permute-start | bytes 1105928 | tf_op jit(solution)/shard_map/ppermute | solution.py:196
  26.3 0.8 copy-start.18
  38.6 0.9 copy-start
  39.5 0.7 copy-start.7
  43.3 4.9 %copy-start.22 = (bf16[4,96,128]{2,1,0:T(8,128)(2,1)S(1)}, bf16[4,96,128]{2,1,0:T(8,128)(2,1)}, u32[]{:S(2)}) copy-start(bf16[4,96,128]{2,1,0:T(8,128)(2,1)} %get-tuple-element.37) | copy-start | bytes 294916
  43.3 15.1 %all-to-all-start.1 = ((bf16[8,4,48,128]{3,2,1,0:T(8,128)(2,1)}), bf16[8,4,48,128]{3,2,1,0:T(8,128)(2,1)S(1)}, u32[]{:S(2)}, u32[]{:S(2)}) async-start(bf16[8,4,48,128]{3,2,1,0:T(8,128)(2,1)} %get-tuple-element.38), calls=%async_computation.1 | async-start | bytes 786432 | tf_op jit(solution)/shard_map/all_to_all | solution.py:220
  48.2 4.9 %slice-start = ((bf16[240,768]{1,0:T(8,128)(2,1)}), bf16[48,768]{1,0:T(8,128)(2,1)S(1)}, s32[]{:S(2)}) async-start(bf16[240,768]{1,0:T(8,128)(2,1)} %copy-done.7), calls=%async_computation.7 | async-start | bytes 147456 | tf_op jit(solution)/shard_map/slice | solution.py:265
  48.2 10.2 %collective-permute-start.2 = (bf16[4,96,128]{2,1,0:T(8,128)(2,1)S(1)}, bf16[4,96,128]{2,1,0:T(8,128)(2,1)S(1)}, u32[]{:S(2)}, u32[]{:S(2)}) collective-permute-start(bf16[4,96,128]{2,1,0:T(8,128)(2,1)S(1)} %copy-done.22), channel_id=1, source_target_pairs={{0,1},{1,0},{2,3},{3,2},{4,5},{5,4},{6,7},{7,6},{8,9},{9,8},{10,11... | collective-permute-start | bytes 294920 | tf_op jit(solution)/shard_map/ppermute | solution.py:196
  53.2 61.3 %copy-start.6 = (bf16[96,768]{1,0:T(8,128)(2,1)}, bf16[96,768]{1,0:T(8,128)(2,1)S(1)}, u32[]{:S(2)}) copy-start(bf16[96,768]{1,0:T(8,128)(2,1)S(1)} %pad_maximum_fusion.2.refs_0_) | copy-start | bytes 442372
  58.4 0.6 copy-start.19
  58.4 2.9 %copy-start.1 = (bf16[8,4,48,128]{3,2,1,0:T(8,128)(2,1)}, bf16[8,4,48,128]{3,2,1,0:T(8,128)(2,1)S(1)}, u32[]{:S(2)}) copy-start(bf16[8,4,48,128]{3,2,1,0:T(8,128)(2,1)S(1)} %all-to-all-done.1.q_ref) | copy-start | bytes 1179652
  61.3 34.6 %all-to-all-start.2 = ((bf16[8,4,96,128]{3,2,1,0:T(8,128)(2,1)}), bf16[8,4,96,128]{3,2,1,0:T(8,128)(2,1)S(1)}, u32[]{:S(2)}, u32[]{:S(2)}) async-start(bf16[8,4,96,128]{3,2,1,0:T(8,128)(2,1)} %get-tuple-element.41), calls=%async_computation.2 | async-start | bytes 1572864 | tf_op jit(solution)/shard_map/all_to_all | solution.py:220
  68.1 27.8 %collective-permute-start.3 = (bf16[2,8,128,128]{3,2,1,0:T(8,128)(2,1)S(1)}, bf16[2,8,128,128]{3,2,1,0:T(8,128)(2,1)S(1)}, u32[]{:S(2)}, u32[]{:S(2)}) collective-permute-start(bf16[2,8,128,128]{3,2,1,0:T(8,128)(2,1)S(1)} %pad_maximum_fusion), channel_id=1, source_target_pairs={{0,32},{32,0},{1,33},{33,1},{2,34},{34,2},{3,35},{35,3},{4,36},{36... | collective-permute-start | bytes 1572872 | tf_op jit(solution)/shard_map/ppermute | solution.py:196
  70.3 15.4 %collective-permute-start.4 = (bf16[96,768]{1,0:T(8,128)(2,1)S(1)}, bf16[96,768]{1,0:T(8,128)(2,1)S(1)}, u32[]{:S(2)}, u32[]{:S(2)}) collective-permute-start(bf16[96,768]{1,0:T(8,128)(2,1)S(1)} %pad_maximum_fusion.2.refs_0_), channel_id=1, source_target_pairs={{0,2},{2,4},{4,6},{6,8},{8,10},{10,12},{12,14},{14,0},{1,3},{3,5},... | collective-permute-start | bytes 442376 | tf_op jit(solution)/shard_map/ppermute | solution.py:196
  72.5 13.2 %collective-permute-start.5 = (bf16[96,768]{1,0:T(8,128)(2,1)S(1)}, bf16[96,768]{1,0:T(8,128)(2,1)S(1)}, u32[]{:S(2)}, u32[]{:S(2)}) collective-permute-start(bf16[96,768]{1,0:T(8,128)(2,1)S(1)} %pad_maximum_fusion.2.refs_0_), channel_id=1, source_target_pairs={{0,4},{2,6},{4,8},{6,10},{8,12},{10,14},{12,0},{14,2},{1,5},{3,7},... | collective-permute-start | bytes 442376 | tf_op jit(solution)/shard_map/ppermute | solution.py:196
  74.4 19.8 %collective-permute-start.6 = (bf16[96,768]{1,0:T(8,128)(2,1)S(1)}, bf16[96,768]{1,0:T(8,128)(2,1)S(1)}, u32[]{:S(2)}, u32[]{:S(2)}) collective-permute-start(bf16[96,768]{1,0:T(8,128)(2,1)S(1)} %pad_maximum_fusion.2.refs_0_), channel_id=1, source_target_pairs={{0,6},{2,8},{4,10},{6,12},{8,14},{10,0},{12,2},{14,4},{1,7},{3,9},... | collective-permute-start | bytes 442376 | tf_op jit(solution)/shard_map/ppermute | solution.py:196
  78.5 17.4 %collective-permute-start.7 = (bf16[96,768]{1,0:T(8,128)(2,1)S(1)}, bf16[96,768]{1,0:T(8,128)(2,1)S(1)}, u32[]{:S(2)}, u32[]{:S(2)}) collective-permute-start(bf16[96,768]{1,0:T(8,128)(2,1)S(1)} %pad_maximum_fusion.2.refs_0_), channel_id=1, source_target_pairs={{0,8},{2,10},{4,12},{6,14},{8,0},{10,2},{12,4},{14,6},{1,9},{3,11}... | collective-permute-start | bytes 442376 | tf_op jit(solution)/shard_map/ppermute | solution.py:196
  85.7 10.2 %copy-start.10 = (bf16[96,768]{1,0:T(8,128)(2,1)}, bf16[96,768]{1,0:T(8,128)(2,1)S(1)}, u32[]{:S(2)}) copy-start(bf16[96,768]{1,0:T(8,128)(2,1)S(1)} %collective-permute-done.4.refs_1_) | copy-start | bytes 442372
  85.7 10.2 %copy-start.11 = (bf16[96,768]{1,0:T(8,128)(2,1)}, bf16[96,768]{1,0:T(8,128)(2,1)S(1)}, u32[]{:S(2)}) copy-start(bf16[96,768]{1,0:T(8,128)(2,1)S(1)} %collective-permute-done.5.refs_2_) | copy-start | bytes 442372
  94.2 1.7 copy-start.12
  95.9 0.7 copy-start.13
  95.9 24.0 %copy-start.21 = (bf16[2,8,128,128]{3,2,1,0:T(8,128)(2,1)}, bf16[2,8,128,128]{3,2,1,0:T(8,128)(2,1)S(1)}, u32[]{:S(2)}) copy-start(bf16[2,8,128,128]{3,2,1,0:T(8,128)(2,1)S(1)} %collective-permute-done.3.far_ref) | copy-start | bytes 1572868
  95.9 0.9 copy-start.4
  96.8 33.5 %all-to-all-start.3 = ((bf16[8,4,96,128]{3,2,1,0:T(8,128)(2,1)}), bf16[8,4,96,128]{3,2,1,0:T(8,128)(2,1)S(1)}, u32[]{:S(2)}, u32[]{:S(2)}) async-start(bf16[8,4,96,128]{3,2,1,0:T(8,128)(2,1)} %get-tuple-element.49), calls=%async_computation.3 | async-start | bytes 1572864 | tf_op jit(solution)/shard_map/all_to_all | solution.py:220
  103.6 24.6 %collective-permute-start.8 = (bf16[96,768]{1,0:T(8,128)(2,1)S(1)}, bf16[96,768]{1,0:T(8,128)(2,1)S(1)}, u32[]{:S(2)}, u32[]{:S(2)}) collective-permute-start(bf16[96,768]{1,0:T(8,128)(2,1)S(1)} %pad_maximum_fusion.2.refs_0_), channel_id=1, source_target_pairs={{0,10},{2,12},{4,14},{6,0},{8,2},{10,4},{12,6},{14,8},{1,11},{3,13... | collective-permute-start | bytes 442376 | tf_op jit(solution)/shard_map/ppermute | solution.py:196
  107.6 20.6 %collective-permute-start.9 = (bf16[96,768]{1,0:T(8,128)(2,1)S(1)}, bf16[96,768]{1,0:T(8,128)(2,1)S(1)}, u32[]{:S(2)}, u32[]{:S(2)}) collective-permute-start(bf16[96,768]{1,0:T(8,128)(2,1)S(1)} %pad_maximum_fusion.2.refs_0_), channel_id=1, source_target_pairs={{0,12},{2,14},{4,0},{6,2},{8,4},{10,6},{12,8},{14,10},{1,13},{3,15... | collective-permute-start | bytes 442376 | tf_op jit(solution)/shard_map/ppermute | solution.py:196
  114.5 15.8 %collective-permute-start.10 = (bf16[96,768]{1,0:T(8,128)(2,1)S(1)}, bf16[96,768]{1,0:T(8,128)(2,1)S(1)}, u32[]{:S(2)}, u32[]{:S(2)}) collective-permute-start(bf16[96,768]{1,0:T(8,128)(2,1)S(1)} %pad_maximum_fusion.2.refs_0_), channel_id=1, source_target_pairs={{0,14},{2,0},{4,2},{6,4},{8,6},{10,8},{12,10},{14,12},{1,15},{3,1}... | collective-permute-start | bytes 442376 | tf_op jit(solution)/shard_map/ppermute | solution.py:196
  128.2 2.1 %copy-start.14 = (bf16[96,768]{1,0:T(8,128)(2,1)}, bf16[96,768]{1,0:T(8,128)(2,1)S(1)}, u32[]{:S(2)}) copy-start(bf16[96,768]{1,0:T(8,128)(2,1)S(1)} %collective-permute-done.8.refs_5_) | copy-start | bytes 442372
  128.3 2.1 %copy-start.15 = (bf16[96,768]{1,0:T(8,128)(2,1)}, bf16[96,768]{1,0:T(8,128)(2,1)S(1)}, u32[]{:S(2)}) copy-start(bf16[96,768]{1,0:T(8,128)(2,1)S(1)} %collective-permute-done.9.refs_6_) | copy-start | bytes 442372
  130.3 0.7 copy-start.16
  130.3 5.0 %copy-start.5 = (bf16[8,4,96,128]{3,2,1,0:T(8,128)(2,1)}, bf16[8,4,96,128]{3,2,1,0:T(8,128)(2,1)S(1)}, u32[]{:S(2)}) copy-start(bf16[8,4,96,128]{3,2,1,0:T(8,128)(2,1)S(1)} %all-to-all-done.3.kv_ref) | copy-start | bytes 2359300
  131.0 12.7 %all-to-all-start.4 = ((bf16[8,2,64,128]{3,2,1,0:T(8,128)(2,1)}), bf16[8,2,64,128]{3,2,1,0:T(8,128)(2,1)S(1)}, u32[]{:S(2)}, u32[]{:S(2)}) async-start(bf16[8,2,64,128]{3,2,1,0:T(8,128)(2,1)} %shard_map.87), calls=%async_computation.4 | async-start | bytes 524288 | tf_op jit(solution)/shard_map/all_to_all | solution.py:220
  143.7 11.5 %copy-start.3 = (bf16[8,2,64,128]{3,2,1,0:T(8,128)(2,1)}, bf16[8,2,64,128]{3,2,1,0:T(8,128)(2,1)S(1)}, u32[]{:S(2)}) copy-start(bf16[8,2,64,128]{3,2,1,0:T(8,128)(2,1)S(1)} %all-to-all-done.4.first_ref) | copy-start | bytes 786436

commit v4 on v2

--- a/solution.py
+++ b/solution.py
@@ -16,7 +16,6 @@
 OCT = ("xlo", "core", "xhi")
 F32, BF16 = jnp.float32, jnp.bfloat16
 VMEM = 56 * 1024 * 1024
-SHIFTS = (0, -1, 1, -2, 2, -3, 3, -4)
 
 
 def params():
@@ -31,7 +30,7 @@
     samples, tok_dev, width = tok_ref.shape
     first = pos_ref[0]
     emb = emb_ref[...].astype(F32)
-    hemb = hemb_ref[...].astype(F32)
+    hemb = hemb_ref[...].astype(F32).reshape(1, width)
     row_of = lax.broadcasted_iota(jnp.int32, (tok_dev, width), 0)
     cond = jnp.zeros((tok_dev, width), F32)
     for t in range(tok_dev):
@@ -53,7 +52,7 @@
         out_ref[g] = normed
 
 
-def bias_kernel(pos_ref, b_ref, keep_ref, away_ref):
+def bias_kernel(pos_ref, b_ref, keep_ref, away_ref, rows_ref):
     xlo, core, xhi = pos_ref[1], pos_ref[2], pos_ref[3]
     row = lax.broadcasted_iota(jnp.int32, (128, 128), 0)
     col = lax.broadcasted_iota(jnp.int32, (128, 128), 1)
@@ -63,18 +62,13 @@
     pick_q = jnp.where(col == from_q, 1.0, 0.0).astype(BF16)
     pick_k = jnp.where(col == from_k, 1.0, 0.0).astype(BF16)
     for b in range(32):
-        y, xl, c = b // 4, (b // 2) % 2, b % 2
-        tile = dot(pick_q, b_ref[0, :, b * 128 : (b + 1) * 128], 1, 0).astype(BF16)
-        turned = dot(pick_k, tile, 1, 1).astype(BF16)
-        role = jnp.bitwise_xor(xlo, xl)
-
-        @pl.when(core == c)
-        def _():
-            keep_ref[role, y] = turned
-
-        @pl.when(core != c)
-        def _():
-            away_ref[role, y] = turned
+        rows_ref[b] = dot(pick_q, b_ref[0, :, b * 128 : (b + 1) * 128], 1, 0).astype(BF16)
+    for role in range(2):
+        xl = jnp.bitwise_xor(xlo, role)
+        for y in range(8):
+            at = (y * 2 + xl) * 2
+            keep_ref[role, y] = dot(pick_k, rows_ref[at + core], 1, 1).astype(BF16)
+            away_ref[role, y] = dot(pick_k, rows_ref[at + 1 - core], 1, 1).astype(BF16)
 
 
 def proj_kernel(pos_ref, x_ref, own_ref, other_ref, q_ref, kv_own_ref, kv_other_ref, gate_ref):
@@ -121,7 +115,7 @@
 def attend_kernel(steps, first, last, pos_ref, q_ref, keep_ref, recv_ref, far_ref, *refs):
     count = sum(len(s) for s in steps)
     kv_refs, rest = refs[:count], refs[count:]
-    me, yy = pos_ref[1] * 2 + pos_ref[2], pos_ref[0]
+    me, yy = pos_ref[1] * 2 + pos_ref[2], pos_ref[4]
     acc = [None, None] if first else [rest[0][i] for i in range(2)]
     top = [None, None] if first else [rest[1][i, :1] for i in range(2)]
     at = 0
@@ -212,22 +206,36 @@
     pairs, peers = samples // 2, 8
     at = {a: lax.axis_index(a) for a in AXES}
     first = ((((at["y"] * 2 + at["xlo"]) * 2 + at["core"]) * 8 + at["z"]) * 2 + at["xhi"]) * tok_dev
-    pos = jnp.stack([first, at["xlo"], at["core"], at["xhi"]])
-    where = jnp.stack([at["y"], at["xlo"], at["core"], at["xhi"]])
+    pos = jnp.stack([first, at["xlo"], at["core"], at["xhi"], at["y"]])
     vm = pl.BlockSpec(memory_space=pltpu.VMEM)
     sm = pl.BlockSpec(memory_space=pltpu.SMEM)
 
-    def call(kernel, specs, out, *args):
+    def call(kernel, specs, out, *args, scratch=()):
         shapes = [jax.ShapeDtypeStruct(s, t) for s, t in out]
         return pl.pallas_call(
-            kernel, out_shape=shapes, in_specs=specs, out_specs=[vm] * len(out), compiler_params=params()
+            kernel,
+            out_shape=shapes,
+            in_specs=specs,
+            out_specs=[vm] * len(out),
+            scratch_shapes=scratch,
+            compiler_params=params(),
         )(*args)
+
+    def exchange(x, axes):
+        return lax.all_to_all(x, axes, split_axis=0, concat_axis=0, tiled=True)
 
     weights = jnp.concatenate([jnp.transpose(w_proj), w_out], axis=0)
     weights_other = shift(weights, "xhi", 1)
-    keep, away = call(bias_kernel, [sm, vm], [((2, 8, 128, 128), BF16)] * 2, pos, pair_bias)
+    keep, away = call(
+        bias_kernel,
+        [sm, vm],
+        [((2, 8, 128, 128), BF16)] * 2,
+        pos,
+        pair_bias,
+        scratch=[pltpu.VMEM((32, 128, 128), BF16)],
+    )
     recv = shift(away, "core", 1)
-    far = shift(jnp.stack([keep[1], recv[1]]), "xlo", 1)
+    far_out = jnp.stack([keep[1], recv[1]])
 
     (copies,) = call(
         norm_kernel,
@@ -238,9 +246,12 @@
         hotspots,
         tokens,
         chain_embed,
-        hot_embed[None],
-    )
-    gathered = lax.all_to_all(copies, "z", split_axis=0, concat_axis=0, tiled=True)
+        hot_embed,
+    )
+    gathered = exchange(copies, "z")
+    weights_other, far_out = lax.optimization_barrier((weights_other, far_out))
+    far = shift(far_out, "xlo", 1)
+    gathered, far_out = lax.optimization_barrier((gathered, far_out))
     q_out, kv_own, kv_other, gate = call(
         proj_kernel,
         [sm, vm, vm, vm],
@@ -257,33 +268,59 @@
     )
     kv_other = shift(kv_other, "xhi", 1)
     (kv,) = call(join_kernel, [vm, vm], [((samples, 2 * HD, 128), BF16)], kv_own, kv_other)
-    right, left, ring = kv, kv, [kv]
-    for step in range(4):
-        right = shift(right, "y", 1)
-        ring.append(right)
-        if step < 3:
-            left = shift(left, "y", -1)
-            ring.append(left)
-    q_in = lax.all_to_all(q_out, OCT, split_axis=0, concat_axis=0, tiled=True)
-    (q_all,) = call(join_q_kernel, [sm, vm], [((samples, HD, 512), BF16)], pos, q_in)
 
     def two(*dims):
         return pl.BlockSpec((2,) + dims, lambda s, _: (s,) + (0,) * len(dims))
 
     whole = pl.BlockSpec((2, 8, 128, 128), lambda s, _: (0, 0, 0, 0))
-    steps = (SHIFTS[0:2], SHIFTS[2:4], SHIFTS[4:6], SHIFTS[6:8])
-    parts = pl.pallas_call(
-        functools.partial(attend_kernel, steps, True, True),
-        out_shape=jax.ShapeDtypeStruct((8, pairs, 64, 128), BF16),
-        grid_spec=pltpu.PrefetchScalarGridSpec(
-            num_scalar_prefetch=1,
-            grid=(pairs,),
-            in_specs=[two(HD, 512), whole, whole, whole] + [two(2 * HD, 128)] * 8,
-            out_specs=pl.BlockSpec((8, 1, 64, 128), lambda s, _: (0, s, 0, 0)),
-        ),
-        compiler_params=params(),
-    )(where, q_all, keep, recv, far, *ring)
-    mine = lax.all_to_all(parts, OCT, split_axis=0, concat_axis=0, tiled=True)
+    state_shape = (jax.ShapeDtypeStruct((samples, 64, 512), F32), jax.ShapeDtypeStruct((samples, 8, 512), F32))
+
+    def attend(state, steps, blocks, last=False):
+        carried = [] if state is None else list(state)
+        out = jax.ShapeDtypeStruct((8, pairs, 64, 128), BF16) if last else state_shape
+        out_specs = pl.BlockSpec((8, 1, 64, 128), lambda s, _: (0, s, 0, 0)) if last else (two(64, 512), two(8, 512))
+        count = len(blocks)
+        return pl.pallas_call(
+            functools.partial(attend_kernel, steps, state is None, last),
+            out_shape=out,
+            grid_spec=pltpu.PrefetchScalarGridSpec(
+                num_scalar_prefetch=1,
+                grid=(pairs,),
+                in_specs=[two(HD, 512), whole, whole, whole]
+                + [two(2 * HD, 128)] * count
+                + [two(64, 512), two(8, 512)][: len(carried)],
+                out_specs=out_specs,
+            ),
+            compiler_params=params(),
+            cost_estimate=pl.CostEstimate(
+                flops=count * (1 << 30), bytes_accessed=3 << 20, transcendentals=count << 19
+            ),
+        )(pos, q_all, keep, recv, far, *blocks, *carried)
+
+    def tie(x, dep):
+        return lax.optimization_barrier((x, dep))
+
+    kv, q_out, far = lax.optimization_barrier((kv, q_out, far))
+    r1, l1 = shift(kv, "y", 1), shift(kv, "y", -1)
+    q_in = exchange(q_out, OCT)
+    (q_all,) = call(join_q_kernel, [sm, vm], [((samples, HD, 512), BF16)], pos, q_in)
+    r2 = shift(r1, "y", 1)
+    state = attend(None, ((0,),), [kv])
+    l1, state = tie(l1, state)
+    l2 = shift(l1, "y", -1)
+    state = attend(state, ((-1,),), [r1])
+    r2, state = tie(r2, state)
+    r3 = shift(r2, "y", 1)
+    state = attend(state, ((1,),), [l1])
+    l2, state = tie(l2, state)
+    l3 = shift(l2, "y", -1)
+    state = attend(state, ((-2,),), [r2])
+    r3, state = tie(r3, state)
+    r4 = shift(r3, "y", 1)
+    state = attend(state, ((2, -3),), [l2, r3])
+    state = attend(state, ((3,),), [l3])
+    parts = attend(state, ((-4,),), [r4], last=True)
+    mine = exchange(parts, OCT)
     (shares,) = call(
         merge_kernel,
         [sm, vm, vm, vm, vm],
@@ -294,7 +331,7 @@
         weights,
         weights_other,
     )
-    summands = lax.all_to_all(shares, "z", split_axis=0, concat_axis=0, tiled=True)
+    summands = exchange(shares, "z")
     (update,) = call(sum_kernel, [vm], [((samples * tok_dev, width), BF16)], summands)
     return update.reshape(samples, tok_dev, width)
 

time: 158 us -> 187 us (1.18)
  Pallas kernels: 39.7 us -> 60.7 us
  waiting for transfers between devices: 11.8 us -> 18.2 us
  blocking collectives: 42.9 us -> 46.3 us
  starting transfers between devices: 55.6 us -> 53.6 us
    pallas_call x1 -> x7, Pallas kernels: 14.1 us -> 43.4 us  [attend(): pl.pallas_call(functools.partial(attend_kernel, steps, state is None, las...]
    ppermute x11, waiting for transfers between devices: 7.36 us -> 17.9 us  [shift(): return lax.ppermute(x, axis, [(i, (i + by) % n) for i in range(n)])]
    pallas_call x7, Pallas kernels: 25.6 us -> 17.3 us  [call(): pl.pallas_call(kernel, out_shape=shapes, in_specs=specs, out_specs=[vm] *...]
    all_to_all x2, waiting for transfers between devices: 4.48 us -> 0.25 us  [exchange(): return lax.all_to_all(x, axes, split_axis=0, concat_axis=0, tiled=True)]
    all_to_all x2, blocking collectives: 42.9 us -> 46.3 us  [exchange(): return lax.all_to_all(x, axes, split_axis=0, concat_axis=0, tiled=True)]
    unnamed x38 -> x36, local copies, waits for them, and re-layouts: 4.72 us -> 4.35 us
  transfers between devices with their start and end apart: 13 -> 13, of which waited for: 5 -> 4; matrix products, arithmetic and copies ran while one was open for 0% -> 0% of each run, Pallas kernels for 12% -> 26%
where the time goes in v4:
time: 187 us; the launch traced here: 184 us
  Pallas kernels  60.7 us (32%)
  starting transfers between devices  53.6 us (29%)
  blocking collectives  46.3 us (25%)
  waiting for transfers between devices  18.2 us (10%)
  local copies, waits for them, and re-layouts  4.98 us (3%)
    all_to_all x2, blocking collectives, exchange(): return lax.all_to_all(x, axes, split_axis=0, concat_axis=0, tiled=True)  46.3 us
    pallas_call x7, Pallas kernels, attend(): pl.pallas_call(functools.partial(attend_kernel, steps, state is None, las...  43.4 us
    ppermute x11, starting transfers between devices, shift(): return lax.ppermute(x, axis, [(i, (i + by) % n) for i in range(n)])  37.3 us
    ppermute x11, waiting for transfers between devices, shift(): return lax.ppermute(x, axis, [(i, (i + by) % n) for i in range(n)])  17.9 us
    pallas_call x7, Pallas kernels, call(): pl.pallas_call(kernel, out_shape=shapes, in_specs=specs, out_specs=[vm] *...  17.3 us
    all_to_all x2, starting transfers between devices, exchange(): return lax.all_to_all(x, axes, split_axis=0, concat_axis=0, tiled=True)  16.3 us
    unnamed x36, local copies, waits for them, and re-layouts  4.35 us
  transfers between devices with their start and end apart: 13, of which 4 were waited for; matrix products, arithmetic and copies ran while one was open for 0% of the time, Pallas kernels for 26%

profile of v4, /device:TPU:1, one launch (start us, length us, event | category | flops | bytes accessed | tf_op | source)
XLA Modules:
  0.0 184.2 jit_solution(5204295228209812996)
XLA Ops:
  0.0 0.6 stack.26.pos_ref
  0.6 2.2 %shard_map.82 = bf16[8,64,768]{2,1,0:T(8,128)(2,1)} custom-call(s32[5]{0:T(128)} %stack.26.pos_ref, s32[8]{0:T(128)} %chain_ref.1, s32[16]{0:T(128)} %hot_ref.1, bf16[8,8,768]{2,1,0:T(8,128)(2,1)} %tok_ref.1, bf16[4,768]{1,0:T(4,128)(2,1)} %emb_ref.1, bf16[768]{0:T(1024)(128)(2,1)} %hemb_ref.1), custom_call_target="tpu_custom_call" | custom-call | tf_op jit(solution)/shard_map/pallas_call | solution.py:215
  2.8 10.9 %all-to-all-start = ((bf16[8,64,768]{2,1,0:T(8,128)(2,1)}), bf16[8,64,768]{2,1,0:T(8,128)(2,1)S(1)}, u32[]{:S(2)}, u32[]{:S(2)}) async-start(bf16[8,64,768]{2,1,0:T(8,128)(2,1)} %shard_map.82), calls=%async_computation | async-start | bytes 1572864 | tf_op jit(solution)/shard_map/all_to_all | solution.py:225
  13.7 0.0 copy-start.9
  13.7 3.6 %shard_map.83 = (bf16[2,8,128,128]{3,2,1,0:T(8,128)(2,1)}, bf16[2,8,128,128]{3,2,1,0:T(8,128)(2,1)}) custom-call(s32[5]{0:T(128)} %stack.26.pos_ref, bf16[1,128,4096]{2,1,0:T(8,128)(2,1)} %b_ref.1), custom_call_target="tpu_custom_call" | custom-call | tf_op jit(solution)/shard_map/pallas_call | solution.py:215
  17.3 3.0 %collective-permute-start.1 = (bf16[2,8,128,128]{3,2,1,0:T(8,128)(2,1)}, bf16[2,8,128,128]{3,2,1,0:T(8,128)(2,1)S(1)}, u32[]{:S(2)}, u32[]{:S(2)}) collective-permute-start(bf16[2,8,128,128]{3,2,1,0:T(8,128)(2,1)} %get-tuple-element.42), channel_id=1, source_target_pairs={{0,16},{16,0},{1,17},{17,1},{2,18},{18,2},{3,19},{19,3},{4,20},{20... | collective-permute-start | bytes 1572872 | tf_op jit(solution)/shard_map/ppermute | solution.py:201
  20.2 0.0 copy-done.4
  20.2 0.0 copy-done.9
  20.3 0.0 copy-start
  20.3 4.7 %collective-permute-start = (bf16[240,768]{1,0:T(8,128)(2,1)S(1)}, bf16[240,768]{1,0:T(8,128)(2,1)S(1)}, u32[]{:S(2)}, u32[]{:S(2)}) collective-permute-start(bf16[240,768]{1,0:T(8,128)(2,1)S(1)} %pad_maximum_fusion.1.own_ref.w_own_ref), channel_id=1, source_target_pairs={{0,1},{1,0},{2,3},{3,2},{4,5},{5,4},{6,7},{7,6},{8,9},{9,8},{10,11... | collective-permute-start | bytes 1105928 | tf_op jit(solution)/shard_map/ppermute | solution.py:201
  25.0 0.0 copy-done.6
  25.0 0.0 collective-permute-done.1.recv_ref
  25.0 0.0 copy-start.7
  25.0 0.0 copy-done
  25.1 0.1 pad_maximum_fusion
  25.1 0.7 copy-done.7
  25.8 8.1 %collective-permute-done.other_ref.w_other_ref = bf16[240,768]{1,0:T(8,128)(2,1)S(1)} collective-permute-done((bf16[240,768]{1,0:T(8,128)(2,1)S(1)}, bf16[240,768]{1,0:T(8,128)(2,1)S(1)}, u32[]{:S(2)}, u32[]{:S(2)}) %collective-permute-start) | collective-permute-done | bytes 368672 | tf_op jit(solution)/shard_map/ppermute | solution.py:201
  33.9 3.1 %collective-permute-start.3 = (bf16[2,8,128,128]{3,2,1,0:T(8,128)(2,1)S(1)}, bf16[2,8,128,128]{3,2,1,0:T(8,128)(2,1)S(1)}, u32[]{:S(2)}, u32[]{:S(2)}) collective-permute-start(bf16[2,8,128,128]{3,2,1,0:T(8,128)(2,1)S(1)} %pad_maximum_fusion), channel_id=1, source_target_pairs={{0,32},{32,0},{1,33},{33,1},{2,34},{34,2},{3,35},{35,3},{4,36},{36... | collective-permute-start | bytes 1572872 | tf_op jit(solution)/shard_map/ppermute | solution.py:201
  37.0 0.2 all-to-all-done.x_ref
  37.3 0.0 copy-done.3
  37.3 0.9 copy-done.1
  38.2 3.1 %shard_map.84 = (bf16[8,4,48,128]{3,2,1,0:T(8,128)(2,1)}, bf16[4,96,128]{2,1,0:T(8,128)(2,1)}, bf16[4,96,128]{2,1,0:T(8,128)(2,1)}, f32[2,4,48,128]{3,2,1,0:T(8,128)}) custom-call(s32[5]{0:T(128)} %stack.26.pos_ref, bf16[8,64,768]{2,1,0:T(8,128)(2,1)} %copy-done.1, bf16[240,768]{1,0:T(8,128)(2,1)} %copy-done, bf16[240,768]{1,0:T(8,128)(2,1)} %copy-done.3), custom_call_target="tpu_custom_call" | custom-call | tf_op jit(solution)/shard_map/pallas_call | solution.py:215
  41.2 4.6 %collective-permute-start.2 = (bf16[4,96,128]{2,1,0:T(8,128)(2,1)}, bf16[4,96,128]{2,1,0:T(8,128)(2,1)S(1)}, u32[]{:S(2)}, u32[]{:S(2)}) collective-permute-start(bf16[4,96,128]{2,1,0:T(8,128)(2,1)} %get-tuple-element.47), channel_id=1, source_target_pairs={{0,1},{1,0},{2,3},{3,2},{4,5},{5,4},{6,7},{7,6},{8,9},{9,8},{10,11... | collective-permute-start | bytes 294920 | tf_op jit(solution)/shard_map/ppermute | solution.py:201
  45.9 6.6 %collective-permute-done.2.other_ref = bf16[4,96,128]{2,1,0:T(8,128)(2,1)S(1)} collective-permute-done((bf16[4,96,128]{2,1,0:T(8,128)(2,1)}, bf16[4,96,128]{2,1,0:T(8,128)(2,1)S(1)}, u32[]{:S(2)}, u32[]{:S(2)}) %collective-permute-start.2) | collective-permute-done | bytes 98336 | tf_op jit(solution)/shard_map/ppermute | solution.py:201
  52.5 0.6 copy-done.8
  53.1 1.7 shard_map.85.refs_0_
  54.8 0.0 collective-permute-done.3.far_ref
  54.9 5.5 %all-to-all-start.1 = ((bf16[8,4,48,128]{3,2,1,0:T(8,128)(2,1)}), bf16[8,4,48,128]{3,2,1,0:T(8,128)(2,1)S(1)}, u32[]{:S(2)}, u32[]{:S(2)}) async-start(bf16[8,4,48,128]{3,2,1,0:T(8,128)(2,1)} %get-tuple-element.49), calls=%async_computation.1 | async-start | bytes 786432 | tf_op jit(solution)/shard_map/all_to_all | solution.py:225
  60.3 0.0 copy-done.5
  60.3 3.2 %collective-permute-start.4 = (bf16[8,96,128]{2,1,0:T(8,128)(2,1)S(1)}, bf16[8,96,128]{2,1,0:T(8,128)(2,1)S(1)}, u32[]{:S(2)}, u32[]{:S(2)}) collective-permute-start(bf16[8,96,128]{2,1,0:T(8,128)(2,1)S(1)} %copy-done.5), channel_id=1, source_target_pairs={{0,64},{64,128},{128,192},{192,256},{256,320},{320,384},{384,448},... | collective-permute-start | bytes 589832 | tf_op jit(solution)/shard_map/ppermute | solution.py:201
  63.5 3.8 %collective-permute-start.6 = (bf16[8,96,128]{2,1,0:T(8,128)(2,1)S(1)}, bf16[8,96,128]{2,1,0:T(8,128)(2,1)S(1)}, u32[]{:S(2)}, u32[]{:S(2)}) collective-permute-start(bf16[8,96,128]{2,1,0:T(8,128)(2,1)S(1)} %copy-done.5), channel_id=1, source_target_pairs={{0,448},{64,0},{128,64},{192,128},{256,192},{320,256},{384,320},{4... | collective-permute-start | bytes 589832 | tf_op jit(solution)/shard_map/ppermute | solution.py:201
  67.4 3.2 %collective-permute-done.4.refs_0_ = bf16[8,96,128]{2,1,0:T(8,128)(2,1)S(1)} collective-permute-done((bf16[8,96,128]{2,1,0:T(8,128)(2,1)S(1)}, bf16[8,96,128]{2,1,0:T(8,128)(2,1)S(1)}, u32[]{:S(2)}, u32[]{:S(2)}) %collective-permute-start.4) | collective-permute-done | bytes 196640 | tf_op jit(solution)/shard_map/ppermute | solution.py:201
  70.6 1.9 %collective-permute-start.5 = (bf16[8,96,128]{2,1,0:T(8,128)(2,1)S(1)}, bf16[8,96,128]{2,1,0:T(8,128)(2,1)S(1)}, u32[]{:S(2)}, u32[]{:S(2)}) collective-permute-start(bf16[8,96,128]{2,1,0:T(8,128)(2,1)S(1)} %collective-permute-done.4.refs_0_), channel_id=1, source_target_pairs={{0,64},{64,128},{128,192},{192,256},{256,320},{320,384},{384,448},... | collective-permute-start | bytes 589832 | tf_op jit(solution)/shard_map/ppermute | solution.py:201
  72.5 0.0 all-to-all-done.1.q_ref
  72.5 0.0 copy-start.2
  72.5 0.7 copy-done.2
  73.3 1.9 %shard_map.86.q_ref = bf16[8,48,512]{2,1,0:T(8,128)(2,1)} custom-call(s32[5]{0:T(128)} %stack.26.pos_ref, bf16[8,4,48,128]{3,2,1,0:T(8,128)(2,1)} %copy-done.2), custom_call_target="tpu_custom_call" | custom-call | tf_op jit(solution)/shard_map/pallas_call | solution.py:215
  75.2 0.0 copy-done.10
  75.2 5.8 %shard_map.87 = (f32[8,64,512]{2,1,0:T(8,128)}, f32[8,8,512]{2,1,0:T(8,128)}) custom-call(s32[5]{0:T(128)} %stack.26.pos_ref, bf16[8,48,512]{2,1,0:T(8,128)(2,1)} %shard_map.86.q_ref, bf16[2,8,128,128]{3,2,1,0:T(8,128)(2,1)} %get-tuple-element.41.keep_ref, bf16[2,8,128,128]{3,2,1,0:T(8,128)(2,1)} %copy-done.7, bf16[2,8,128,128]{3,2,1,0:T(8,128)(2,1)} %copy-done.10, ...), custom_call_target="tpu_custom_call" | custom-call | flops 1073741824 | bytes 3145728 | tf_op jit(solution)/shard_map/pallas_call | solution.py:283
  81.0 0.0 copy-done.15
  81.0 0.0 collective-permute-done.6.refs_0_
  81.0 0.0 copy-start.13
  81.1 4.6 %collective-permute-start.8 = (bf16[8,96,128]{2,1,0:T(8,128)(2,1)S(1)}, bf16[8,96,128]{2,1,0:T(8,128)(2,1)S(1)}, u32[]{:S(2)}, u32[]{:S(2)}) collective-permute-start(bf16[8,96,128]{2,1,0:T(8,128)(2,1)S(1)} %collective-permute-done.6.refs_0_), channel_id=1, source_target_pairs={{0,448},{64,0},{128,64},{192,128},{256,192},{320,256},{384,320},{4... | collective-permute-start | bytes 589832 | tf_op jit(solution)/shard_map/ppermute | solution.py:201
  85.6 6.1 %shard_map.88 = (f32[8,64,512]{2,1,0:T(8,128)}, f32[8,8,512]{2,1,0:T(8,128)}) custom-call(s32[5]{0:T(128)} %stack.26.pos_ref, bf16[8,48,512]{2,1,0:T(8,128)(2,1)} %shard_map.86.q_ref, bf16[2,8,128,128]{3,2,1,0:T(8,128)(2,1)} %get-tuple-element.41.keep_ref, bf16[2,8,128,128]{3,2,1,0:T(8,128)(2,1)} %copy-done.7, bf16[2,8,128,128]{3,2,1,0:T(8,128)(2,1)} %copy-done.10, ...), custom_call_target="tpu_custom_call" | custom-call | flops 1073741824 | bytes 3145728 | tf_op jit(solution)/shard_map/pallas_call | solution.py:283
  91.8 0.0 collective-permute-done.5.refs_0_
  91.8 0.0 copy-start.11
  91.8 1.9 %collective-permute-start.7 = (bf16[8,96,128]{2,1,0:T(8,128)(2,1)S(1)}, bf16[8,96,128]{2,1,0:T(8,128)(2,1)S(1)}, u32[]{:S(2)}, u32[]{:S(2)}) collective-permute-start(bf16[8,96,128]{2,1,0:T(8,128)(2,1)S(1)} %collective-permute-done.5.refs_0_), channel_id=1, source_target_pairs={{0,64},{64,128},{128,192},{192,256},{256,320},{320,384},{384,448},... | collective-permute-start | bytes 589832 | tf_op jit(solution)/shard_map/ppermute | solution.py:201
  93.7 6.1 %shard_map.89 = (f32[8,64,512]{2,1,0:T(8,128)}, f32[8,8,512]{2,1,0:T(8,128)}) custom-call(s32[5]{0:T(128)} %stack.26.pos_ref, bf16[8,48,512]{2,1,0:T(8,128)(2,1)} %shard_map.86.q_ref, bf16[2,8,128,128]{3,2,1,0:T(8,128)(2,1)} %get-tuple-element.41.keep_ref, bf16[2,8,128,128]{3,2,1,0:T(8,128)(2,1)} %copy-done.7, bf16[2,8,128,128]{3,2,1,0:T(8,128)(2,1)} %copy-done.10, ...), custom_call_target="tpu_custom_call" | custom-call | flops 1073741824 | bytes 3145728 | tf_op jit(solution)/shard_map/pallas_call | solution.py:283
  99.9 0.0 collective-permute-done.8.refs_0_
  99.9 4.6 %collective-permute-start.10 = (bf16[8,96,128]{2,1,0:T(8,128)(2,1)S(1)}, bf16[8,96,128]{2,1,0:T(8,128)(2,1)S(1)}, u32[]{:S(2)}, u32[]{:S(2)}) collective-permute-start(bf16[8,96,128]{2,1,0:T(8,128)(2,1)S(1)} %collective-permute-done.8.refs_0_), channel_id=1, source_target_pairs={{0,448},{64,0},{128,64},{192,128},{256,192},{320,256},{384,320},{4... | collective-permute-start | bytes 589832 | tf_op jit(solution)/shard_map/ppermute | solution.py:201
  104.5 6.1 %shard_map.90 = (f32[8,64,512]{2,1,0:T(8,128)}, f32[8,8,512]{2,1,0:T(8,128)}) custom-call(s32[5]{0:T(128)} %stack.26.pos_ref, bf16[8,48,512]{2,1,0:T(8,128)(2,1)} %shard_map.86.q_ref, bf16[2,8,128,128]{3,2,1,0:T(8,128)(2,1)} %get-tuple-element.41.keep_ref, bf16[2,8,128,128]{3,2,1,0:T(8,128)(2,1)} %copy-done.7, bf16[2,8,128,128]{3,2,1,0:T(8,128)(2,1)} %copy-done.10, ...), custom_call_target="tpu_custom_call" | custom-call | flops 1073741824 | bytes 3145728 | tf_op jit(solution)/shard_map/pallas_call | solution.py:283
  110.6 0.0 collective-permute-done.7.refs_1_
  110.6 1.9 %collective-permute-start.9 = (bf16[8,96,128]{2,1,0:T(8,128)(2,1)S(1)}, bf16[8,96,128]{2,1,0:T(8,128)(2,1)S(1)}, u32[]{:S(2)}, u32[]{:S(2)}) collective-permute-start(bf16[8,96,128]{2,1,0:T(8,128)(2,1)S(1)} %collective-permute-done.7.refs_1_), channel_id=1, source_target_pairs={{0,64},{64,128},{128,192},{192,256},{256,320},{320,384},{384,448},... | collective-permute-start | bytes 589832 | tf_op jit(solution)/shard_map/ppermute | solution.py:201
  112.6 6.7 %shard_map.91 = (f32[8,64,512]{2,1,0:T(8,128)}, f32[8,8,512]{2,1,0:T(8,128)}) custom-call(s32[5]{0:T(128)} %stack.26.pos_ref, bf16[8,48,512]{2,1,0:T(8,128)(2,1)} %shard_map.86.q_ref, bf16[2,8,128,128]{3,2,1,0:T(8,128)(2,1)} %get-tuple-element.41.keep_ref, bf16[2,8,128,128]{3,2,1,0:T(8,128)(2,1)} %copy-done.7, bf16[2,8,128,128]{3,2,1,0:T(8,128)(2,1)} %copy-done.10, ...), custom_call_target="tpu_custom_call" | custom-call | flops 2147483648 | bytes 3145728 | tf_op jit(solution)/shard_map/pallas_call | solution.py:283
  119.2 0.0 collective-permute-done.10.refs_0_
  119.2 0.7 copy-done.16
  119.9 6.1 %shard_map.92 = (f32[8,64,512]{2,1,0:T(8,128)}, f32[8,8,512]{2,1,0:T(8,128)}) custom-call(s32[5]{0:T(128)} %stack.26.pos_ref, bf16[8,48,512]{2,1,0:T(8,128)(2,1)} %shard_map.86.q_ref, bf16[2,8,128,128]{3,2,1,0:T(8,128)(2,1)} %get-tuple-element.41.keep_ref, bf16[2,8,128,128]{3,2,1,0:T(8,128)(2,1)} %copy-done.7, bf16[2,8,128,128]{3,2,1,0:T(8,128)(2,1)} %copy-done.10, ...), custom_call_target="tpu_custom_call" | custom-call | flops 1073741824 | bytes 3145728 | tf_op jit(solution)/shard_map/pallas_call | solution.py:283
  126.1 0.0 collective-permute-done.9.refs_0_
  126.1 0.7 copy-done.17
  126.7 6.4 %shard_map.93 = bf16[8,4,64,128]{3,2,1,0:T(8,128)(2,1)} custom-call(s32[5]{0:T(128)} %stack.26.pos_ref, bf16[8,48,512]{2,1,0:T(8,128)(2,1)} %shard_map.86.q_ref, bf16[2,8,128,128]{3,2,1,0:T(8,128)(2,1)} %get-tuple-element.41.keep_ref, bf16[2,8,128,128]{3,2,1,0:T(8,128)(2,1)} %copy-done.7, bf16[2,8,128,128]{3,2,1,0:T(8,128)(2,1)} %copy-done.10, ...), custom_call_target="tpu_custom_call" | custom-call | flops 1073741824 | bytes 3145728 | tf_op jit(solution)/shard_map/pallas_call | solution.py:283
  133.1 15.7 %all_to_all.20.p_ref = bf16[8,4,64,128]{3,2,1,0:T(8,128)(2,1)} all-to-all(bf16[8,4,64,128]{3,2,1,0:T(8,128)(2,1)} %shard_map.93), channel_id=1, replica_groups=mesh['y'=8,'xlo'=2,'core'=2,'z'=8,'xhi'=2] {'xlo','core','xhi'}, dimensions={0} | all-to-all | bytes 1048576 | tf_op jit(solution)/shard_map/all_to_all | solution.py:225
  148.8 2.9 %shard_map.94 = bf16[8,64,768]{2,1,0:T(8,128)(2,1)} custom-call(s32[5]{0:T(128)} %stack.26.pos_ref, bf16[8,4,64,128]{3,2,1,0:T(8,128)(2,1)} %all_to_all.20.p_ref, f32[2,4,48,128]{3,2,1,0:T(8,128)} %get-tuple-element.76.gate_ref, bf16[240,768]{1,0:T(8,128)(2,1)} %copy-done, bf16[240,768]{1,0:T(8,128)(2,1)} %copy-done.3), custom_call_target="tpu_custom_call" | custom-call | tf_op jit(solution)/shard_map/pallas_call | solution.py:215
  151.7 30.6 %all_to_all.21.x_ref = bf16[8,64,768]{2,1,0:T(8,128)(2,1)} all-to-all(bf16[8,64,768]{2,1,0:T(8,128)(2,1)} %shard_map.94), channel_id=1, replica_groups=mesh['y'=8,'xlo'=2,'core'=2,'z'=8,'xhi'=2] {'z'}, dimensions={0} | all-to-all | bytes 1572864 | tf_op jit(solution)/shard_map/all_to_all | solution.py:225
  182.3 1.9 %shard_map.95 = bf16[64,768]{1,0:T(8,128)(2,1)} custom-call(bf16[8,64,768]{2,1,0:T(8,128)(2,1)} %all_to_all.21.x_ref), custom_call_target="tpu_custom_call" | custom-call | tf_op jit(solution)/shard_map/pallas_call | solution.py:215
  (19 shorter events, 0.1 us)
Async XLA Ops:
  2.8 34.4 %all-to-all-start = ((bf16[8,64,768]{2,1,0:T(8,128)(2,1)}), bf16[8,64,768]{2,1,0:T(8,128)(2,1)S(1)}, u32[]{:S(2)}, u32[]{:S(2)}) async-start(bf16[8,64,768]{2,1,0:T(8,128)(2,1)} %shard_map.82), calls=%async_computation | async-start | bytes 1572864 | tf_op jit(solution)/shard_map/all_to_all | solution.py:225
  13.7 6.5 %copy-start.4 = (bf16[768,192]{0,1:T(8,128)(2,1)S(1)}, bf16[768,192]{0,1:T(8,128)(2,1)}, u32[]{:S(2)}) copy-start(bf16[768,192]{0,1:T(8,128)(2,1)} %param.13) | copy-start | bytes 884740
  13.7 6.5 %copy-start.9 = (bf16[48,768]{1,0:T(8,128)(2,1)S(1)}, bf16[48,768]{1,0:T(8,128)(2,1)}, u32[]{:S(2)}) copy-start(bf16[48,768]{1,0:T(8,128)(2,1)} %param.15) | copy-start | bytes 221188
  17.3 7.7 %copy-start.6 = (bf16[2,8,128,128]{3,2,1,0:T(8,128)(2,1)S(1)}, bf16[2,8,128,128]{3,2,1,0:T(8,128)(2,1)}, u32[]{:S(2)}) copy-start(bf16[2,8,128,128]{3,2,1,0:T(8,128)(2,1)} %get-tuple-element.41.keep_ref) | copy-start | bytes 1572868
  17.3 7.7 %collective-permute-start.1 = (bf16[2,8,128,128]{3,2,1,0:T(8,128)(2,1)}, bf16[2,8,128,128]{3,2,1,0:T(8,128)(2,1)S(1)}, u32[]{:S(2)}, u32[]{:S(2)}) collective-permute-start(bf16[2,8,128,128]{3,2,1,0:T(8,128)(2,1)} %get-tuple-element.42), channel_id=1, source_target_pairs={{0,16},{16,0},{1,17},{17,1},{2,18},{18,2},{3,19},{19,3},{4,20},{20... | collective-permute-start | bytes 1572872 | tf_op jit(solution)/shard_map/ppermute | solution.py:201
  20.3 4.8 %copy-start = (bf16[240,768]{1,0:T(8,128)(2,1)}, bf16[240,768]{1,0:T(8,128)(2,1)S(1)}, u32[]{:S(2)}) copy-start(bf16[240,768]{1,0:T(8,128)(2,1)S(1)} %pad_maximum_fusion.1.own_ref.w_own_ref) | copy-start | bytes 1105924
  20.3 13.6 %collective-permute-start = (bf16[240,768]{1,0:T(8,128)(2,1)S(1)}, bf16[240,768]{1,0:T(8,128)(2,1)S(1)}, u32[]{:S(2)}, u32[]{:S(2)}) collective-permute-start(bf16[240,768]{1,0:T(8,128)(2,1)S(1)} %pad_maximum_fusion.1.own_ref.w_own_ref), channel_id=1, source_target_pairs={{0,1},{1,0},{2,3},{3,2},{4,5},{5,4},{6,7},{7,6},{8,9},{9,8},{10,11... | collective-permute-start | bytes 1105928 | tf_op jit(solution)/shard_map/ppermute | solution.py:201
  25.0 0.8 copy-start.7
  33.9 3.4 %copy-start.3 = (bf16[240,768]{1,0:T(8,128)(2,1)}, bf16[240,768]{1,0:T(8,128)(2,1)S(1)}, u32[]{:S(2)}) copy-start(bf16[240,768]{1,0:T(8,128)(2,1)S(1)} %collective-permute-done.other_ref.w_other_ref) | copy-start | bytes 1105924
  33.9 20.9 %collective-permute-start.3 = (bf16[2,8,128,128]{3,2,1,0:T(8,128)(2,1)S(1)}, bf16[2,8,128,128]{3,2,1,0:T(8,128)(2,1)S(1)}, u32[]{:S(2)}, u32[]{:S(2)}) collective-permute-start(bf16[2,8,128,128]{3,2,1,0:T(8,128)(2,1)S(1)} %pad_maximum_fusion), channel_id=1, source_target_pairs={{0,32},{32,0},{1,33},{33,1},{2,34},{34,2},{3,35},{35,3},{4,36},{36... | collective-permute-start | bytes 1572872 | tf_op jit(solution)/shard_map/ppermute | solution.py:201
  37.3 0.9 copy-start.1
  41.2 11.2 %collective-permute-start.2 = (bf16[4,96,128]{2,1,0:T(8,128)(2,1)}, bf16[4,96,128]{2,1,0:T(8,128)(2,1)S(1)}, u32[]{:S(2)}, u32[]{:S(2)}) collective-permute-start(bf16[4,96,128]{2,1,0:T(8,128)(2,1)} %get-tuple-element.47), channel_id=1, source_target_pairs={{0,1},{1,0},{2,3},{3,2},{4,5},{5,4},{6,7},{7,6},{8,9},{9,8},{10,11... | collective-permute-start | bytes 294920 | tf_op jit(solution)/shard_map/ppermute | solution.py:201
  52.5 0.6 copy-start.8
  54.8 20.3 %copy-start.10 = (bf16[2,8,128,128]{3,2,1,0:T(8,128)(2,1)}, bf16[2,8,128,128]{3,2,1,0:T(8,128)(2,1)S(1)}, u32[]{:S(2)}) copy-start(bf16[2,8,128,128]{3,2,1,0:T(8,128)(2,1)S(1)} %collective-permute-done.3.far_ref) | copy-start | bytes 1572868
  54.8 5.5 %copy-start.5 = (bf16[8,96,128]{2,1,0:T(8,128)(2,1)S(1)}, bf16[8,96,128]{2,1,0:T(8,128)(2,1)}, u32[]{:S(2)}) copy-start(bf16[8,96,128]{2,1,0:T(8,128)(2,1)} %shard_map.85.refs_0_) | copy-start | bytes 589828
  54.9 17.6 %all-to-all-start.1 = ((bf16[8,4,48,128]{3,2,1,0:T(8,128)(2,1)}), bf16[8,4,48,128]{3,2,1,0:T(8,128)(2,1)S(1)}, u32[]{:S(2)}, u32[]{:S(2)}) async-start(bf16[8,4,48,128]{3,2,1,0:T(8,128)(2,1)} %get-tuple-element.49), calls=%async_computation.1 | async-start | bytes 786432 | tf_op jit(solution)/shard_map/all_to_all | solution.py:225
  60.3 10.2 %collective-permute-start.4 = (bf16[8,96,128]{2,1,0:T(8,128)(2,1)S(1)}, bf16[8,96,128]{2,1,0:T(8,128)(2,1)S(1)}, u32[]{:S(2)}, u32[]{:S(2)}) collective-permute-start(bf16[8,96,128]{2,1,0:T(8,128)(2,1)S(1)} %copy-done.5), channel_id=1, source_target_pairs={{0,64},{64,128},{128,192},{192,256},{256,320},{320,384},{384,448},... | collective-permute-start | bytes 589832 | tf_op jit(solution)/shard_map/ppermute | solution.py:201
  63.5 17.5 %collective-permute-start.6 = (bf16[8,96,128]{2,1,0:T(8,128)(2,1)S(1)}, bf16[8,96,128]{2,1,0:T(8,128)(2,1)S(1)}, u32[]{:S(2)}, u32[]{:S(2)}) collective-permute-start(bf16[8,96,128]{2,1,0:T(8,128)(2,1)S(1)} %copy-done.5), channel_id=1, source_target_pairs={{0,448},{64,0},{128,64},{192,128},{256,192},{320,256},{384,320},{4... | collective-permute-start | bytes 589832 | tf_op jit(solution)/shard_map/ppermute | solution.py:201
  70.6 10.5 %copy-start.15 = (bf16[8,96,128]{2,1,0:T(8,128)(2,1)}, bf16[8,96,128]{2,1,0:T(8,128)(2,1)S(1)}, u32[]{:S(2)}) copy-start(bf16[8,96,128]{2,1,0:T(8,128)(2,1)S(1)} %collective-permute-done.4.refs_0_) | copy-start | bytes 589828
  70.6 21.2 %collective-permute-start.5 = (bf16[8,96,128]{2,1,0:T(8,128)(2,1)S(1)}, bf16[8,96,128]{2,1,0:T(8,128)(2,1)S(1)}, u32[]{:S(2)}, u32[]{:S(2)}) collective-permute-start(bf16[8,96,128]{2,1,0:T(8,128)(2,1)S(1)} %collective-permute-done.4.refs_0_), channel_id=1, source_target_pairs={{0,64},{64,128},{128,192},{192,256},{256,320},{320,384},{384,448},... | collective-permute-start | bytes 589832 | tf_op jit(solution)/shard_map/ppermute | solution.py:201
  72.5 0.8 copy-start.2
  81.0 10.7 %copy-start.13 = (bf16[8,96,128]{2,1,0:T(8,128)(2,1)}, bf16[8,96,128]{2,1,0:T(8,128)(2,1)S(1)}, u32[]{:S(2)}) copy-start(bf16[8,96,128]{2,1,0:T(8,128)(2,1)S(1)} %collective-permute-done.6.refs_0_) | copy-start | bytes 589828
  81.1 18.8 %collective-permute-start.8 = (bf16[8,96,128]{2,1,0:T(8,128)(2,1)S(1)}, bf16[8,96,128]{2,1,0:T(8,128)(2,1)S(1)}, u32[]{:S(2)}, u32[]{:S(2)}) collective-permute-start(bf16[8,96,128]{2,1,0:T(8,128)(2,1)S(1)} %collective-permute-done.6.refs_0_), channel_id=1, source_target_pairs={{0,448},{64,0},{128,64},{192,128},{256,192},{320,256},{384,320},{4... | collective-permute-start | bytes 589832 | tf_op jit(solution)/shard_map/ppermute | solution.py:201
  91.8 8.1 %copy-start.11 = (bf16[8,96,128]{2,1,0:T(8,128)(2,1)}, bf16[8,96,128]{2,1,0:T(8,128)(2,1)S(1)}, u32[]{:S(2)}) copy-start(bf16[8,96,128]{2,1,0:T(8,128)(2,1)S(1)} %collective-permute-done.5.refs_0_) | copy-start | bytes 589828
  91.8 18.8 %collective-permute-start.7 = (bf16[8,96,128]{2,1,0:T(8,128)(2,1)S(1)}, bf16[8,96,128]{2,1,0:T(8,128)(2,1)S(1)}, u32[]{:S(2)}, u32[]{:S(2)}) collective-permute-start(bf16[8,96,128]{2,1,0:T(8,128)(2,1)S(1)} %collective-permute-done.5.refs_0_), channel_id=1, source_target_pairs={{0,64},{64,128},{128,192},{192,256},{256,320},{320,384},{384,448},... | collective-permute-start | bytes 589832 | tf_op jit(solution)/shard_map/ppermute | solution.py:201
  99.9 10.7 %copy-start.12 = (bf16[8,96,128]{2,1,0:T(8,128)(2,1)}, bf16[8,96,128]{2,1,0:T(8,128)(2,1)S(1)}, u32[]{:S(2)}) copy-start(bf16[8,96,128]{2,1,0:T(8,128)(2,1)S(1)} %collective-permute-done.8.refs_0_) | copy-start | bytes 589828
  99.9 19.4 %collective-permute-start.10 = (bf16[8,96,128]{2,1,0:T(8,128)(2,1)S(1)}, bf16[8,96,128]{2,1,0:T(8,128)(2,1)S(1)}, u32[]{:S(2)}, u32[]{:S(2)}) collective-permute-start(bf16[8,96,128]{2,1,0:T(8,128)(2,1)S(1)} %collective-permute-done.8.refs_0_), channel_id=1, source_target_pairs={{0,448},{64,0},{128,64},{192,128},{256,192},{320,256},{384,320},{4... | collective-permute-start | bytes 589832 | tf_op jit(solution)/shard_map/ppermute | solution.py:201
  110.6 1.9 %copy-start.14 = (bf16[8,96,128]{2,1,0:T(8,128)(2,1)}, bf16[8,96,128]{2,1,0:T(8,128)(2,1)S(1)}, u32[]{:S(2)}) copy-start(bf16[8,96,128]{2,1,0:T(8,128)(2,1)S(1)} %collective-permute-done.7.refs_1_) | copy-start | bytes 589828
  110.6 15.4 %collective-permute-start.9 = (bf16[8,96,128]{2,1,0:T(8,128)(2,1)S(1)}, bf16[8,96,128]{2,1,0:T(8,128)(2,1)S(1)}, u32[]{:S(2)}, u32[]{:S(2)}) collective-permute-start(bf16[8,96,128]{2,1,0:T(8,128)(2,1)S(1)} %collective-permute-done.7.refs_1_), channel_id=1, source_target_pairs={{0,64},{64,128},{128,192},{192,256},{256,320},{320,384},{384,448},... | collective-permute-start | bytes 589832 | tf_op jit(solution)/shard_map/ppermute | solution.py:201
  119.2 0.7 copy-start.16
  126.1 0.7 copy-start.17

commit v5 on v3

--- a/solution.py
+++ b/solution.py
@@ -15,11 +15,11 @@
 HEADS = ("z", "xhi")
 OCT = ("xlo", "core", "xhi")
 F32, BF16 = jnp.float32, jnp.bfloat16
-VMEM = 56 * 1024 * 1024
-
-
-def params():
-    return pltpu.CompilerParams(vmem_limit_bytes=VMEM)
+MIB = 1024 * 1024
+
+
+def params(mib=16):
+    return pltpu.CompilerParams(vmem_limit_bytes=mib * MIB)
 
 
 def dot(a, b, da, db):
@@ -30,7 +30,7 @@
     samples, tok_dev, width = tok_ref.shape
     first = pos_ref[0]
     emb = emb_ref[...].astype(F32)
-    hemb = hemb_ref[...].astype(F32)
+    hemb = hemb_ref[...].astype(F32).reshape(1, width)
     row_of = lax.broadcasted_iota(jnp.int32, (tok_dev, width), 0)
     cond = jnp.zeros((tok_dev, width), F32)
     for t in range(tok_dev):
@@ -95,16 +95,11 @@
     return jnp.where(lane < 64, a, pltpu.roll(b, 64, 1)), jnp.where(lane < 64, pltpu.roll(a, 64, 1), b)
 
 
-def join_kernel(own_ref, other_ref, first_ref, second_ref):
-    pairs = own_ref.shape[0]
-    for p in range(pairs):
-        half, at = divmod(p, pairs // 2)
-        out_ref = (first_ref, second_ref)[half]
-        both = join(own_ref[p].astype(F32), other_ref[p].astype(F32))
-        for i in range(2):
-            one = both[i].astype(BF16)
-            for y in range(out_ref.shape[0]):
-                out_ref[y, 2 * at + i] = one
+def join_kernel(own_ref, other_ref, kv_ref):
+    for p in range(own_ref.shape[0]):
+        even, odd = join(own_ref[p].astype(F32), other_ref[p].astype(F32))
+        kv_ref[2 * p] = even.astype(BF16)
+        kv_ref[2 * p + 1] = odd.astype(BF16)
 
 
 def join_q_kernel(pos_ref, q_ref, out_ref):
@@ -117,30 +112,25 @@
             out_ref[2 * p + 1, :, role * 128 : (role + 1) * 128] = odd.astype(BF16)
 
 
-def attend_kernel(pos_ref, q_ref, keep_ref, recv_ref, far_ref, kv_ref, out_ref):
-    me = pos_ref[1] * 2 + pos_ref[2]
-    acc, top = [None, None], [None, None]
-    for y in range(0, 8, 2):
-        bias = [
-            jnp.concatenate([keep_ref[0, b], recv_ref[0, b], far_ref[0, b], far_ref[1, b]], axis=1).astype(F32)
-            for b in (y, y + 1)
-        ]
-        bias = jnp.concatenate(bias, axis=0)
-        for i in range(2):
-            keys = [jnp.transpose(kv_ref[b, i, :HD].astype(F32)).astype(BF16) for b in (y, y + 1)]
-            keys = jnp.concatenate(keys, axis=0)
-            vals = jnp.concatenate([kv_ref[y, i, HD:], kv_ref[y + 1, i, HD:]], axis=1)
-            vals = jnp.concatenate([vals, jnp.ones((16, vals.shape[1]), BF16)], axis=0)
-            scores = jnp.dot(keys, q_ref[i], preferred_element_type=F32) + bias
-            best = jnp.max(scores, axis=0, keepdims=True)
-            if top[i] is not None:
-                best = jnp.maximum(best, top[i])
-            probs = jnp.exp(scores - best).astype(BF16)
-            part = jnp.dot(vals, probs, preferred_element_type=F32)
-            if top[i] is not None:
-                part = part + acc[i] * jnp.exp(top[i] - best)
-            acc[i], top[i] = part, best
+def attend_kernel(shifts, pos_ref, q_ref, keep_ref, recv_ref, far_ref, *refs):
+    kv_refs, out_ref = refs[:-1], refs[-1]
+    me, yy = pos_ref[1] * 2 + pos_ref[2], pos_ref[4]
     row = lax.broadcasted_iota(jnp.int32, (16, 128), 0)
+    bias = []
+    for by in shifts:
+        y = lax.rem(yy + 8 + by, 8)
+        bias.append(jnp.concatenate([keep_ref[0, y], recv_ref[0, y], far_ref[0, y], far_ref[1, y]], axis=1).astype(F32))
+    bias = jnp.concatenate(bias, axis=0)
+    acc, top = [], []
+    for i in range(2):
+        keys = jnp.concatenate([jnp.transpose(r[i, :HD].astype(F32)).astype(BF16) for r in kv_refs], axis=0)
+        vals = jnp.concatenate([r[i, HD:] for r in kv_refs], axis=1)
+        vals = jnp.concatenate([vals, jnp.ones((16, vals.shape[1]), BF16)], axis=0)
+        scores = jnp.dot(keys, q_ref[i], preferred_element_type=F32) + bias
+        best = jnp.max(scores, axis=0, keepdims=True)
+        probs = jnp.exp(scores - best).astype(BF16)
+        acc.append(jnp.dot(vals, probs, preferred_element_type=F32))
+        top.append(best)
     for role in range(4):
         d = 2 * jnp.bitwise_xor(me, role)
         tiles = []
@@ -158,18 +148,15 @@
         out_ref[d + 1, 0] = odd.astype(BF16)
 
 
-def merge_kernel(pos_ref, first_ref, second_ref, gate_ref, out_ref):
-    xhi = pos_ref[3]
-    per_half = first_ref.shape[1]
+def merge_kernel(pos_ref, p_ref, gate_ref, out_ref):
+    core = pos_ref[2]
     peers = out_ref.shape[0]
     tok = 64 // peers
-    for p in range(2 * per_half):
-        half, at = divmod(p, per_half)
-        p_ref = (first_ref, second_ref)[half]
+    for p in range(p_ref.shape[1]):
         gated = []
-        for role in range(2):
-            h = jnp.bitwise_xor(xhi, role)
-            rows = [p_ref[2 * i + h, at].astype(F32) for i in range(4)]
+        for other in range(2):
+            h = jnp.bitwise_xor(core, other)
+            rows = [p_ref[2 * i + h, p].astype(F32) for i in range(4)]
             lse = [r[HD : HD + 1] + r[HD + 1 : HD + 2] + r[HD + 2 : HD + 3] for r in rows]
             top = functools.reduce(jnp.maximum, lse)
             weight = [jnp.exp(v - top) for v in lse]
@@ -181,12 +168,12 @@
             out_ref[g, 2 * tok * p : 2 * tok * (p + 1)] = both.astype(BF16)
 
 
-def out_kernel(pos_ref, g_ref, *refs):
-    w_refs, out_ref = refs[:-1], refs[-1]
+def out_kernel(g_ref, w_near_ref, w_far_ref, out_ref):
     total = None
-    for by, w_ref in enumerate(w_refs):
-        gated = g_ref[lax.rem(pos_ref[4] + 8 - by, 8)]
-        term = jnp.dot(gated[:, : 2 * HD], w_ref[...], preferred_element_type=F32)
+    for g in range(g_ref.shape[0]):
+        gated = g_ref[g]
+        term = jnp.dot(gated[:, :HD], w_near_ref[g], preferred_element_type=F32)
+        term = term + jnp.dot(gated[:, HD : 2 * HD], w_far_ref[g], preferred_element_type=F32)
         total = term if total is None else total + term
     out_ref[...] = total.astype(BF16)
 
@@ -201,7 +188,7 @@
     pairs, peers = samples // 2, 8
     at = {a: lax.axis_index(a) for a in AXES}
     first = ((((at["y"] * 2 + at["xlo"]) * 2 + at["core"]) * 8 + at["z"]) * 2 + at["xhi"]) * tok_dev
-    pos = jnp.stack([first, at["xlo"], at["core"], at["xhi"], at["z"]])
+    pos = jnp.stack([first, at["xlo"], at["core"], at["xhi"], at["y"]])
     vm = pl.BlockSpec(memory_space=pltpu.VMEM)
     sm = pl.BlockSpec(memory_space=pltpu.SMEM)
 
@@ -241,10 +228,12 @@
         hotspots,
         tokens,
         chain_embed,
-        hot_embed[None],
-    )
-    gathered, far_out = lax.optimization_barrier((exchange(copies, "z"), far_out))
+        hot_embed,
+    )
+    gathered = exchange(copies, "z")
+    weights_other, far_out = lax.optimization_barrier((weights_other, far_out))
     far = shift(far_out, "xlo", 1)
+    gathered, far_out = lax.optimization_barrier((gathered, far_out))
     q_out, kv_own, kv_other, gate = call(
         proj_kernel,
         [sm, vm, vm, vm],
@@ -259,60 +248,52 @@
         weights,
         weights_other,
     )
-    kv_other, q_in = lax.optimization_barrier((shift(kv_other, "xhi", 1), exchange(q_out, OCT)))
-    half = samples // 2
-    kv = call(join_kernel, [vm, vm], [((8, half, 2 * HD, 128), BF16)] * 2, kv_own, kv_other)
-    w_rows = jnp.concatenate([weights[4 * HD :], weights_other[4 * HD :]], axis=0)
-    w_rows, kv_first = lax.optimization_barrier((w_rows, kv[0]))
-    w_all = [w_rows] + [shift(w_rows, "z", by) for by in range(1, peers)]
+    kv_other = shift(kv_other, "xhi", 1)
+    (kv,) = call(join_kernel, [vm, vm], [((samples, 2 * HD, 128), BF16)], kv_own, kv_other)
+
+    kv, far = lax.optimization_barrier((kv, far))
+    right, left, ring, shifts = kv, kv, [kv], [0]
+    for step in range(1, 5):
+        right = shift(right, "y", 1)
+        if step == 1:
+            right, q_out = lax.optimization_barrier((right, q_out))
+        ring.append(right)
+        shifts.append(-step)
+        if step < 4:
+            left = shift(left, "y", -1)
+            ring.append(left)
+            shifts.append(step)
+    q_in = exchange(q_out, OCT)
     (q_all,) = call(join_q_kernel, [sm, vm], [((samples, HD, 512), BF16)], pos, q_in)
-    kv_first, kv_second, far, q_all, *w_all[1:5] = lax.optimization_barrier(
-        (exchange(kv_first, "y"), kv[1], far, q_all, *w_all[1:5])
-    )
-    kv_second, *w_all[5:] = lax.optimization_barrier((exchange(kv_second, "y"), *w_all[5:]))
-    kv_in = [kv_first, kv_second]
+
+    w_rows = jnp.where(at["core"] == at["xhi"], w_out, weights_other[4 * HD :])
+    w_rows, q_in = lax.optimization_barrier((w_rows, q_in))
+    w_near = exchange(jnp.broadcast_to(w_rows[None], (peers, HD, width)), "z")
+
+    def two(*dims):
+        return pl.BlockSpec((2,) + dims, lambda s, _: (s,) + (0,) * len(dims))
 
     whole = pl.BlockSpec((2, 8, 128, 128), lambda s, _: (0, 0, 0, 0))
-    mine = []
-    for part in range(2):
-        steps = pairs // 2
-        result = pl.pallas_call(
-            attend_kernel,
-            out_shape=jax.ShapeDtypeStruct((8, steps, 64, 128), BF16),
-            grid_spec=pltpu.PrefetchScalarGridSpec(
-                num_scalar_prefetch=1,
-                grid=(steps,),
-                in_specs=[
-                    pl.BlockSpec((2, HD, 512), lambda s, _, base=part * steps: (base + s, 0, 0)),
-                    whole,
-                    whole,
-                    whole,
-                    pl.BlockSpec((8, 2, 2 * HD, 128), lambda s, _: (0, s, 0, 0)),
-                ],
-                out_specs=pl.BlockSpec((8, 1, 64, 128), lambda s, _: (0, s, 0, 0)),
-            ),
-            compiler_params=params(),
-            cost_estimate=pl.CostEstimate(flops=4 * half * 512 * 1024 * 64, bytes_accessed=5 << 20, transcendentals=half << 19),
-        )(pos, q_all, keep, recv, far, kv_in[part])
-        if part == 0:
-            result, kv_in[1] = lax.optimization_barrier((result, kv_in[1]))
-        mine.append(exchange(result, OCT))
+    parts = pl.pallas_call(
+        functools.partial(attend_kernel, tuple(shifts)),
+        out_shape=jax.ShapeDtypeStruct((8, pairs, 64, 128), BF16),
+        grid_spec=pltpu.PrefetchScalarGridSpec(
+            num_scalar_prefetch=1,
+            grid=(pairs,),
+            in_specs=[two(HD, 512), whole, whole, whole] + [two(2 * HD, 128)] * 8,
+            out_specs=pl.BlockSpec((8, 1, 64, 128), lambda s, _: (0, s, 0, 0)),
+        ),
+        compiler_params=params(32),
+        cost_estimate=pl.CostEstimate(flops=1 << 33, bytes_accessed=4 << 20, transcendentals=1 << 22),
+    )(pos, q_all, keep, recv, far, *ring)
+    parts, w_near = lax.optimization_barrier((parts, w_near))
+    w_far = shift(w_near, "core", 1)
+    mine = exchange(parts, OCT)
     (gated,) = call(
-        merge_kernel,
-        [sm, vm, vm, vm],
-        [((peers, samples * tok_dev, 128), BF16)],
-        pos,
-        mine[0],
-        mine[1],
-        gate,
+        merge_kernel, [sm, vm, vm], [((peers, samples * tok_dev, 128), BF16)], pos, mine, gate
     )
     (update,) = call(
-        out_kernel,
-        [sm, vm] + [vm] * peers,
-        [((samples * tok_dev, width), BF16)],
-        pos,
-        exchange(gated, "z"),
-        *w_all,
+        out_kernel, [vm, vm, vm], [((samples * tok_dev, width), BF16)], exchange(gated, "z"), w_near, w_far
     )
     return update.reshape(samples, tok_dev, width)
 

time: 174 us -> 142 us (0.82)
  blocking collectives: 24.2 us -> 0 us
  Pallas kernels: 34.1 us -> 19.7 us
  waiting for transfers between devices: 28.8 us -> 41 us
  local copies, waits for them, and re-layouts: 6.59 us -> 2.5 us
  starting transfers between devices: 78.2 us -> 75.7 us
    all_to_all x2 -> x0, blocking collectives: 24.2 us -> none  [exchange(): return lax.all_to_all(x, axes, split_axis=0, concat_axis=0, tiled=True)]
    pallas_call x7, Pallas kernels: 17.4 us -> 9.39 us  [call(): pl.pallas_call(kernel, out_shape=shapes, in_specs=specs, out_specs=[vm] *...]
    all_to_all x5, waiting for transfers between devices: 11.4 us -> 18.6 us  [exchange(): return lax.all_to_all(x, axes, split_axis=0, concat_axis=0, tiled=True)]
    pallas_call x2 -> x1, Pallas kernels: 16.7 us -> 10.3 us  [body(): pl.pallas_call(functools.partial(attend_kernel, tuple(shifts)), out_shape...]
    ppermute x11 -> x12, waiting for transfers between devices: 17.4 us -> 22.5 us  [shift(): return lax.ppermute(x, axis, [(i, (i + by) % n) for i in range(n)])]
    ppermute x11 -> x12, starting transfers between devices: 44.4 us -> 40.2 us  [shift(): return lax.ppermute(x, axis, [(i, (i + by) % n) for i in range(n)])]
    unnamed x46 -> x22, local copies, waits for them, and re-layouts: 5.36 us -> 1.52 us
    all_to_all x5, starting transfers between devices: 33.8 us -> 35.5 us  [exchange(): return lax.all_to_all(x, axes, split_axis=0, concat_axis=0, tiled=True)]
  transfers between devices with their start and end apart: 16 -> 17, of which waited for: 5 -> 9; matrix products, arithmetic and copies ran while one was open for 0% -> 1% of each run, Pallas kernels for 13% -> 12%
where the time goes in v5:
time: 142 us; the launch traced here: 140 us
  starting transfers between devices  75.7 us (53%)
  waiting for transfers between devices  41 us (29%)
  Pallas kernels  19.7 us (14%)
  local copies, waits for them, and re-layouts  2.5 us (2%)
    ppermute x12, starting transfers between devices, shift(): return lax.ppermute(x, axis, [(i, (i + by) % n) for i in range(n)])  40.2 us
    all_to_all x5, starting transfers between devices, exchange(): return lax.all_to_all(x, axes, split_axis=0, concat_axis=0, tiled=True)  35.5 us
    ppermute x12, waiting for transfers between devices, shift(): return lax.ppermute(x, axis, [(i, (i + by) % n) for i in range(n)])  22.5 us
    all_to_all x5, waiting for transfers between devices, exchange(): return lax.all_to_all(x, axes, split_axis=0, concat_axis=0, tiled=True)  18.6 us
    pallas_call x1, Pallas kernels, body(): pl.pallas_call(functools.partial(attend_kernel, tuple(shifts)), out_shape...  10.3 us
    pallas_call x7, Pallas kernels, call(): pl.pallas_call(kernel, out_shape=shapes, in_specs=specs, out_specs=[vm] *...  9.39 us
  transfers between devices with their start and end apart: 17, of which 9 were waited for; matrix products, arithmetic and copies ran while one was open for 1% of the time, Pallas kernels for 12%

profile of v5, /device:TPU:1, one launch (start us, length us, event | category | flops | bytes accessed | tf_op | source)
XLA Modules:
  0.0 140.1 jit_solution(17164878171823081885)
XLA Ops:
  0.0 0.0 copy-start.2
  0.0 0.0 copy-start.3
  0.0 0.0 copy-start.4
  0.0 0.0 copy-start.5
  0.0 0.1 stack.26.pos_ref
  0.1 0.6 copy-done.2
  0.7 0.0 copy-done.3
  0.7 0.0 copy-done.4
  0.7 0.0 copy-done.5
  0.7 0.0 copy-start.1
  0.7 0.9 copy-done.1
  1.6 0.0 copy-start
  1.6 1.9 %shard_map.82 = bf16[8,64,768]{2,1,0:T(8,128)(2,1)} custom-call(s32[5]{0:T(128)S(1)} %stack.26.pos_ref, s32[8]{0:T(128)S(1)} %copy-done.4, s32[16]{0:T(128)S(1)} %copy-done.5, bf16[8,8,768]{2,1,0:T(8,128)(2,1)S(1)} %copy-done.1, bf16[4,768]{1,0:T(4,128)(2,1)S(1)} %copy-done.2, bf16[768]{0:T(1024)(128)(2,1)S(1)} %copy-done.3), custom_call_target="tpu_custom_call" | custom-call | tf_op jit(solution)/shard_map/pallas_call | solution.py:197
  3.5 10.9 %all-to-all-start = ((bf16[8,64,768]{2,1,0:T(8,128)(2,1)}), bf16[8,64,768]{2,1,0:T(8,128)(2,1)S(1)}, u32[]{:S(2)}, u32[]{:S(2)}) async-start(bf16[8,64,768]{2,1,0:T(8,128)(2,1)} %shard_map.82), calls=%async_computation | async-start | bytes 1572864 | tf_op jit(solution)/shard_map/all_to_all | solution.py:207
  14.3 0.0 copy-done
  14.4 0.0 copy-start.8
  14.4 0.0 copy-start.10
  14.4 1.8 %shard_map.83 = (bf16[2,8,128,128]{3,2,1,0:T(8,128)(2,1)S(1)}, bf16[2,8,128,128]{3,2,1,0:T(8,128)(2,1)S(1)}) custom-call(s32[5]{0:T(128)S(1)} %stack.26.pos_ref, bf16[1,128,4096]{2,1,0:T(8,128)(2,1)S(1)} %copy-done), custom_call_target="tpu_custom_call" | custom-call | tf_op jit(solution)/shard_map/pallas_call | solution.py:197
  16.2 2.8 %collective-permute-start.1 = (bf16[2,8,128,128]{3,2,1,0:T(8,128)(2,1)S(1)}, bf16[2,8,128,128]{3,2,1,0:T(8,128)(2,1)S(1)}, u32[]{:S(2)}, u32[]{:S(2)}) collective-permute-start(bf16[2,8,128,128]{3,2,1,0:T(8,128)(2,1)S(1)} %get-tuple-element.22), channel_id=1, source_target_pairs={{0,16},{16,0},{1,17},{17,1},{2,18},{18,2},{3,19},{19,3},{4,20},{20... | collective-permute-start | bytes 1572872 | tf_op jit(solution)/shard_map/ppermute | solution.py:183
  19.1 0.0 copy-done.8
  19.1 0.0 copy-done.10
  19.1 4.7 %collective-permute-start = (bf16[240,768]{1,0:T(8,128)(2,1)S(1)}, bf16[240,768]{1,0:T(8,128)(2,1)S(1)}, u32[]{:S(2)}, u32[]{:S(2)}) collective-permute-start(bf16[240,768]{1,0:T(8,128)(2,1)S(1)} %pad_maximum_fusion.1.own_ref), channel_id=1, source_target_pairs={{0,1},{1,0},{2,3},{3,2},{4,5},{5,4},{6,7},{7,6},{8,9},{9,8},{10,11... | collective-permute-start | bytes 1105928 | tf_op jit(solution)/shard_map/ppermute | solution.py:183
  23.8 0.0 collective-permute-done.1.recv_ref
  23.9 0.9 pad_maximum_fusion
  24.7 8.0 %collective-permute-done.other_ref = bf16[240,768]{1,0:T(8,128)(2,1)S(1)} collective-permute-done((bf16[240,768]{1,0:T(8,128)(2,1)S(1)}, bf16[240,768]{1,0:T(8,128)(2,1)S(1)}, u32[]{:S(2)}, u32[]{:S(2)}) %collective-permute-start) | collective-permute-done | bytes 368672 | tf_op jit(solution)/shard_map/ppermute | solution.py:183
  32.7 3.1 %collective-permute-start.3 = (bf16[2,8,128,128]{3,2,1,0:T(8,128)(2,1)}, bf16[2,8,128,128]{3,2,1,0:T(8,128)(2,1)S(1)}, u32[]{:S(2)}, u32[]{:S(2)}) collective-permute-start(bf16[2,8,128,128]{3,2,1,0:T(8,128)(2,1)} %pad_maximum_fusion), channel_id=1, source_target_pairs={{0,32},{32,0},{1,33},{33,1},{2,34},{34,2},{3,35},{35,3},{4,36},{36... | collective-permute-start | bytes 1572872 | tf_op jit(solution)/shard_map/ppermute | solution.py:183
  35.9 2.1 %all-to-all-done.x_ref = bf16[8,64,768]{2,1,0:T(8,128)(2,1)S(1)} async-done(((bf16[8,64,768]{2,1,0:T(8,128)(2,1)}), bf16[8,64,768]{2,1,0:T(8,128)(2,1)S(1)}, u32[]{:S(2)}, u32[]{:S(2)}) %all-to-all-start) | async-done | bytes 786464 | tf_op jit(solution)/shard_map/all_to_all | solution.py:207
  37.9 2.2 %shard_map.84 = (bf16[8,4,48,128]{3,2,1,0:T(8,128)(2,1)}, bf16[4,96,128]{2,1,0:T(8,128)(2,1)S(1)}, bf16[4,96,128]{2,1,0:T(8,128)(2,1)S(1)}, f32[2,4,48,128]{3,2,1,0:T(8,128)S(1)}) custom-call(s32[5]{0:T(128)S(1)} %stack.26.pos_ref, bf16[8,64,768]{2,1,0:T(8,128)(2,1)S(1)} %all-to-all-done.x_ref, bf16[240,768]{1,0:T(8,128)(2,1)S(1)} %pad_maximum_fusion.1.own_ref, ...), custom_call_target="tpu_custom_call" | custom-call | tf_op jit(solution)/shard_map/pallas_call | solution.py:197
  40.1 4.6 %collective-permute-start.2 = (bf16[4,96,128]{2,1,0:T(8,128)(2,1)S(1)}, bf16[4,96,128]{2,1,0:T(8,128)(2,1)S(1)}, u32[]{:S(2)}, u32[]{:S(2)}) collective-permute-start(bf16[4,96,128]{2,1,0:T(8,128)(2,1)S(1)} %get-tuple-element.27), channel_id=1, source_target_pairs={{0,1},{1,0},{2,3},{3,2},{4,5},{5,4},{6,7},{7,6},{8,9},{9,8},{10,11... | collective-permute-start | bytes 294920 | tf_op jit(solution)/shard_map/ppermute | solution.py:183
  44.7 6.8 %collective-permute-done.2.other_ref = bf16[4,96,128]{2,1,0:T(8,128)(2,1)S(1)} collective-permute-done((bf16[4,96,128]{2,1,0:T(8,128)(2,1)S(1)}, bf16[4,96,128]{2,1,0:T(8,128)(2,1)S(1)}, u32[]{:S(2)}, u32[]{:S(2)}) %collective-permute-start.2) | collective-permute-done | bytes 98336 | tf_op jit(solution)/shard_map/ppermute | solution.py:183
  51.5 0.1 shard_map.85.refs_0_
  51.6 0.0 collective-permute-done.3.far_ref
  51.6 3.2 %collective-permute-start.4 = (bf16[8,96,128]{2,1,0:T(8,128)(2,1)S(1)}, bf16[8,96,128]{2,1,0:T(8,128)(2,1)S(1)}, u32[]{:S(2)}, u32[]{:S(2)}) collective-permute-start(bf16[8,96,128]{2,1,0:T(8,128)(2,1)S(1)} %shard_map.85.refs_0_), channel_id=1, source_target_pairs={{0,64},{64,128},{128,192},{192,256},{256,320},{320,384},{384,448},... | collective-permute-start | bytes 589832 | tf_op jit(solution)/shard_map/ppermute | solution.py:183
  54.9 3.8 %collective-permute-start.5 = (bf16[8,96,128]{2,1,0:T(8,128)(2,1)S(1)}, bf16[8,96,128]{2,1,0:T(8,128)(2,1)}, u32[]{:S(2)}, u32[]{:S(2)}) collective-permute-start(bf16[8,96,128]{2,1,0:T(8,128)(2,1)S(1)} %shard_map.85.refs_0_), channel_id=1, source_target_pairs={{0,448},{64,0},{128,64},{192,128},{256,192},{320,256},{384,320},{4... | collective-permute-start | bytes 589832 | tf_op jit(solution)/shard_map/ppermute | solution.py:183
  58.7 1.1 collective-permute-done.4.refs_1_
  59.8 2.0 %collective-permute-start.6 = (bf16[8,96,128]{2,1,0:T(8,128)(2,1)S(1)}, bf16[8,96,128]{2,1,0:T(8,128)(2,1)}, u32[]{:S(2)}, u32[]{:S(2)}) collective-permute-start(bf16[8,96,128]{2,1,0:T(8,128)(2,1)S(1)} %collective-permute-done.4.refs_1_), channel_id=1, source_target_pairs={{0,64},{64,128},{128,192},{192,256},{256,320},{320,384},{384,448},... | collective-permute-start | bytes 589832 | tf_op jit(solution)/shard_map/ppermute | solution.py:183
  61.8 0.0 copy-done.6
  61.9 6.3 %all-to-all-start.1 = ((bf16[8,4,48,128]{3,2,1,0:T(8,128)(2,1)}), bf16[8,4,48,128]{3,2,1,0:T(8,128)(2,1)S(1)}, u32[]{:S(2)}, u32[]{:S(2)}) async-start(bf16[8,4,48,128]{3,2,1,0:T(8,128)(2,1)} %get-tuple-element.30), calls=%async_computation.1 | async-start | bytes 786432 | tf_op jit(solution)/shard_map/all_to_all | solution.py:207
  68.2 0.0 collective-permute-done.5.refs_2_
  68.2 4.7 %collective-permute-start.7 = (bf16[8,96,128]{2,1,0:T(8,128)(2,1)}, bf16[8,96,128]{2,1,0:T(8,128)(2,1)}, u32[]{:S(2)}, u32[]{:S(2)}) collective-permute-start(bf16[8,96,128]{2,1,0:T(8,128)(2,1)} %collective-permute-done.5.refs_2_), channel_id=1, source_target_pairs={{0,448},{64,0},{128,64},{192,128},{256,192},{320,256},{384,320},{4... | collective-permute-start | bytes 589832 | tf_op jit(solution)/shard_map/ppermute | solution.py:183
  72.9 0.0 collective-permute-done.6.refs_3_
  72.9 1.9 %collective-permute-start.8 = (bf16[8,96,128]{2,1,0:T(8,128)(2,1)}, bf16[8,96,128]{2,1,0:T(8,128)(2,1)}, u32[]{:S(2)}, u32[]{:S(2)}) collective-permute-start(bf16[8,96,128]{2,1,0:T(8,128)(2,1)} %collective-permute-done.6.refs_3_), channel_id=1, source_target_pairs={{0,64},{64,128},{128,192},{192,256},{256,320},{320,384},{384,448},... | collective-permute-start | bytes 589832 | tf_op jit(solution)/shard_map/ppermute | solution.py:183
  74.9 0.0 copy-done.9
  74.9 1.3 all-to-all-done.1.q_ref
  76.2 0.9 broadcast_in_dim.2
  77.0 6.9 %all-to-all-start.2 = ((bf16[8,48,768]{2,1,0:T(8,128)(2,1)}), bf16[8,48,768]{2,1,0:T(8,128)(2,1)S(1)}, u32[]{:S(2)}, u32[]{:S(2)}) async-start(bf16[8,48,768]{2,1,0:T(8,128)(2,1)} %broadcast_in_dim.2), calls=%async_computation.2 | async-start | bytes 1179648 | tf_op jit(solution)/shard_map/all_to_all | solution.py:207
  83.9 0.0 collective-permute-done.7.refs_4_
  84.0 5.3 %collective-permute-start.9 = (bf16[8,96,128]{2,1,0:T(8,128)(2,1)}, bf16[8,96,128]{2,1,0:T(8,128)(2,1)S(1)}, u32[]{:S(2)}, u32[]{:S(2)}) collective-permute-start(bf16[8,96,128]{2,1,0:T(8,128)(2,1)} %collective-permute-done.7.refs_4_), channel_id=1, source_target_pairs={{0,448},{64,0},{128,64},{192,128},{256,192},{320,256},{384,320},{4... | collective-permute-start | bytes 589832 | tf_op jit(solution)/shard_map/ppermute | solution.py:183
  89.2 0.0 collective-permute-done.8.refs_5_
  89.2 1.9 %collective-permute-start.10 = (bf16[8,96,128]{2,1,0:T(8,128)(2,1)}, bf16[8,96,128]{2,1,0:T(8,128)(2,1)S(1)}, u32[]{:S(2)}, u32[]{:S(2)}) collective-permute-start(bf16[8,96,128]{2,1,0:T(8,128)(2,1)} %collective-permute-done.8.refs_5_), channel_id=1, source_target_pairs={{0,64},{64,128},{128,192},{192,256},{256,320},{320,384},{384,448},... | collective-permute-start | bytes 589832 | tf_op jit(solution)/shard_map/ppermute | solution.py:183
  91.2 0.7 shard_map.86.q_ref
  91.9 1.7 %collective-permute-done.9.refs_6_ = bf16[8,96,128]{2,1,0:T(8,128)(2,1)S(1)} collective-permute-done((bf16[8,96,128]{2,1,0:T(8,128)(2,1)}, bf16[8,96,128]{2,1,0:T(8,128)(2,1)S(1)}, u32[]{:S(2)}, u32[]{:S(2)}) %collective-permute-start.9) | collective-permute-done | bytes 196640 | tf_op jit(solution)/shard_map/ppermute | solution.py:183
  93.6 4.9 %collective-permute-done.10.refs_7_ = bf16[8,96,128]{2,1,0:T(8,128)(2,1)S(1)} collective-permute-done((bf16[8,96,128]{2,1,0:T(8,128)(2,1)}, bf16[8,96,128]{2,1,0:T(8,128)(2,1)S(1)}, u32[]{:S(2)}, u32[]{:S(2)}) %collective-permute-start.10) | collective-permute-done | bytes 196640 | tf_op jit(solution)/shard_map/ppermute | solution.py:183
  98.5 0.0 copy-done.7
  98.5 10.3 %shard_map.87 = bf16[8,4,64,128]{3,2,1,0:T(8,128)(2,1)} custom-call(s32[5]{0:T(128)S(1)} %stack.26.pos_ref, bf16[8,48,512]{2,1,0:T(8,128)(2,1)S(1)} %shard_map.86.q_ref, bf16[2,8,128,128]{3,2,1,0:T(8,128)(2,1)S(1)} %get-tuple-element.21.keep_ref, bf16[2,8,128,128]{3,2,1,0:T(8,128)(2,1)S(1)} %collective-permute-done.1.recv_ref, ...), custom_call_target="tpu_custom_call" | custom-call | flops 8589934592 | bytes 4194304 | tf_op jit(solution)/shard_map/pallas_call | solution.py:277
  108.7 0.0 all-to-all-done.2.w_near_ref
  108.8 4.8 %all-to-all-start.3 = ((bf16[8,4,64,128]{3,2,1,0:T(8,128)(2,1)}), bf16[8,4,64,128]{3,2,1,0:T(8,128)(2,1)S(1)}, u32[]{:S(2)}, u32[]{:S(2)}) async-start(bf16[8,4,64,128]{3,2,1,0:T(8,128)(2,1)} %shard_map.87), calls=%async_computation.3 | async-start | bytes 1048576 | tf_op jit(solution)/shard_map/all_to_all | solution.py:207
  113.6 2.0 %collective-permute-start.11 = (bf16[8,48,768]{2,1,0:T(8,128)(2,1)S(1)}, bf16[8,48,768]{2,1,0:T(8,128)(2,1)S(1)}, u32[]{:S(2)}, u32[]{:S(2)}) collective-permute-start(bf16[8,48,768]{2,1,0:T(8,128)(2,1)S(1)} %all-to-all-done.2.w_near_ref), channel_id=1, source_target_pairs={{0,16},{16,0},{1,17},{17,1},{2,18},{18,2},{3,19},{19,3},{4,20},{20... | collective-permute-start | bytes 1769480 | tf_op jit(solution)/shard_map/ppermute | solution.py:183
  115.6 7.4 %all-to-all-done.3.p_ref = bf16[8,4,64,128]{3,2,1,0:T(8,128)(2,1)S(1)} async-done(((bf16[8,4,64,128]{3,2,1,0:T(8,128)(2,1)}), bf16[8,4,64,128]{3,2,1,0:T(8,128)(2,1)S(1)}, u32[]{:S(2)}, u32[]{:S(2)}) %all-to-all-start.3) | async-done | bytes 524320 | tf_op jit(solution)/shard_map/all_to_all | solution.py:207
  122.9 1.4 %shard_map.88 = bf16[8,64,128]{2,1,0:T(8,128)(2,1)} custom-call(s32[5]{0:T(128)S(1)} %stack.26.pos_ref, bf16[8,4,64,128]{3,2,1,0:T(8,128)(2,1)S(1)} %all-to-all-done.3.p_ref, f32[2,4,48,128]{3,2,1,0:T(8,128)S(1)} %get-tuple-element.35.gate_ref), custom_call_target="tpu_custom_call" | custom-call | tf_op jit(solution)/shard_map/pallas_call | solution.py:197
  124.4 6.6 %all-to-all-start.4 = ((bf16[8,64,128]{2,1,0:T(8,128)(2,1)}), bf16[8,64,128]{2,1,0:T(8,128)(2,1)S(1)}, u32[]{:S(2)}, u32[]{:S(2)}) async-start(bf16[8,64,128]{2,1,0:T(8,128)(2,1)} %shard_map.88), calls=%async_computation.4 | async-start | bytes 262144 | tf_op jit(solution)/shard_map/all_to_all | solution.py:207
  131.0 0.0 collective-permute-done.11.w_far_ref
  131.0 7.9 %all-to-all-done.4.g_ref = bf16[8,64,128]{2,1,0:T(8,128)(2,1)S(1)} async-done(((bf16[8,64,128]{2,1,0:T(8,128)(2,1)}), bf16[8,64,128]{2,1,0:T(8,128)(2,1)S(1)}, u32[]{:S(2)}, u32[]{:S(2)}) %all-to-all-start.4) | async-done | bytes 131104 | tf_op jit(solution)/shard_map/all_to_all | solution.py:207
  138.9 1.3 shard_map.89
  (7 shorter events, 0.1 us)
Async XLA Ops:
  0.0 0.7 copy-start.2
  0.0 0.7 copy-start.3
  0.0 0.7 copy-start.4
  0.0 0.7 copy-start.5
  0.7 0.9 copy-start.1
  1.6 12.8 %copy-start = (bf16[1,128,4096]{2,1,0:T(8,128)(2,1)S(1)}, bf16[1,128,4096]{2,1,0:T(8,128)(2,1)}, u32[]{:S(2)}) copy-start(bf16[1,128,4096]{2,1,0:T(8,128)(2,1)} %b_ref.1) | copy-start | bytes 3145732
  3.5 34.4 %all-to-all-start = ((bf16[8,64,768]{2,1,0:T(8,128)(2,1)}), bf16[8,64,768]{2,1,0:T(8,128)(2,1)S(1)}, u32[]{:S(2)}, u32[]{:S(2)}) async-start(bf16[8,64,768]{2,1,0:T(8,128)(2,1)} %shard_map.82), calls=%async_computation | async-start | bytes 1572864 | tf_op jit(solution)/shard_map/all_to_all | solution.py:207
  14.4 4.7 %copy-start.8 = (bf16[48,768]{1,0:T(8,128)(2,1)S(1)}, bf16[48,768]{1,0:T(8,128)(2,1)}, u32[]{:S(2)}) copy-start(bf16[48,768]{1,0:T(8,128)(2,1)} %param.15) | copy-start | bytes 221188
  14.4 4.7 %copy-start.10 = (bf16[768,192]{0,1:T(8,128)(2,1)S(1)}, bf16[768,192]{0,1:T(8,128)(2,1)}, u32[]{:S(2)}) copy-start(bf16[768,192]{0,1:T(8,128)(2,1)} %param.13) | copy-start | bytes 884740
  16.2 7.6 %collective-permute-start.1 = (bf16[2,8,128,128]{3,2,1,0:T(8,128)(2,1)S(1)}, bf16[2,8,128,128]{3,2,1,0:T(8,128)(2,1)S(1)}, u32[]{:S(2)}, u32[]{:S(2)}) collective-permute-start(bf16[2,8,128,128]{3,2,1,0:T(8,128)(2,1)S(1)} %get-tuple-element.22), channel_id=1, source_target_pairs={{0,16},{16,0},{1,17},{17,1},{2,18},{18,2},{3,19},{19,3},{4,20},{20... | collective-permute-start | bytes 1572872 | tf_op jit(solution)/shard_map/ppermute | solution.py:183
  19.1 13.6 %collective-permute-start = (bf16[240,768]{1,0:T(8,128)(2,1)S(1)}, bf16[240,768]{1,0:T(8,128)(2,1)S(1)}, u32[]{:S(2)}, u32[]{:S(2)}) collective-permute-start(bf16[240,768]{1,0:T(8,128)(2,1)S(1)} %pad_maximum_fusion.1.own_ref), channel_id=1, source_target_pairs={{0,1},{1,0},{2,3},{3,2},{4,5},{5,4},{6,7},{7,6},{8,9},{9,8},{10,11... | collective-permute-start | bytes 1105928 | tf_op jit(solution)/shard_map/ppermute | solution.py:183
  32.7 18.9 %collective-permute-start.3 = (bf16[2,8,128,128]{3,2,1,0:T(8,128)(2,1)}, bf16[2,8,128,128]{3,2,1,0:T(8,128)(2,1)S(1)}, u32[]{:S(2)}, u32[]{:S(2)}) collective-permute-start(bf16[2,8,128,128]{3,2,1,0:T(8,128)(2,1)} %pad_maximum_fusion), channel_id=1, source_target_pairs={{0,32},{32,0},{1,33},{33,1},{2,34},{34,2},{3,35},{35,3},{4,36},{36... | collective-permute-start | bytes 1572872 | tf_op jit(solution)/shard_map/ppermute | solution.py:183
  40.1 11.4 %collective-permute-start.2 = (bf16[4,96,128]{2,1,0:T(8,128)(2,1)S(1)}, bf16[4,96,128]{2,1,0:T(8,128)(2,1)S(1)}, u32[]{:S(2)}, u32[]{:S(2)}) collective-permute-start(bf16[4,96,128]{2,1,0:T(8,128)(2,1)S(1)} %get-tuple-element.27), channel_id=1, source_target_pairs={{0,1},{1,0},{2,3},{3,2},{4,5},{5,4},{6,7},{7,6},{8,9},{9,8},{10,11... | collective-permute-start | bytes 294920 | tf_op jit(solution)/shard_map/ppermute | solution.py:183
  51.6 8.2 %collective-permute-start.4 = (bf16[8,96,128]{2,1,0:T(8,128)(2,1)S(1)}, bf16[8,96,128]{2,1,0:T(8,128)(2,1)S(1)}, u32[]{:S(2)}, u32[]{:S(2)}) collective-permute-start(bf16[8,96,128]{2,1,0:T(8,128)(2,1)S(1)} %shard_map.85.refs_0_), channel_id=1, source_target_pairs={{0,64},{64,128},{128,192},{192,256},{256,320},{320,384},{384,448},... | collective-permute-start | bytes 589832 | tf_op jit(solution)/shard_map/ppermute | solution.py:183
  54.9 13.3 %collective-permute-start.5 = (bf16[8,96,128]{2,1,0:T(8,128)(2,1)S(1)}, bf16[8,96,128]{2,1,0:T(8,128)(2,1)}, u32[]{:S(2)}, u32[]{:S(2)}) collective-permute-start(bf16[8,96,128]{2,1,0:T(8,128)(2,1)S(1)} %shard_map.85.refs_0_), channel_id=1, source_target_pairs={{0,448},{64,0},{128,64},{192,128},{256,192},{320,256},{384,320},{4... | collective-permute-start | bytes 589832 | tf_op jit(solution)/shard_map/ppermute | solution.py:183
  59.8 2.1 %copy-start.6 = (bf16[8,96,128]{2,1,0:T(8,128)(2,1)}, bf16[8,96,128]{2,1,0:T(8,128)(2,1)S(1)}, u32[]{:S(2)}) copy-start(bf16[8,96,128]{2,1,0:T(8,128)(2,1)S(1)} %collective-permute-done.4.refs_1_) | copy-start | bytes 589828
  59.8 15.1 %copy-start.9 = (bf16[48,768]{1,0:T(8,128)(2,1)S(1)}, bf16[48,768]{1,0:T(8,128)(2,1)}, u32[]{:S(2)}) copy-start(bf16[48,768]{1,0:T(8,128)(2,1)} %param.15) | copy-start | bytes 221188
  59.8 13.1 %collective-permute-start.6 = (bf16[8,96,128]{2,1,0:T(8,128)(2,1)S(1)}, bf16[8,96,128]{2,1,0:T(8,128)(2,1)}, u32[]{:S(2)}, u32[]{:S(2)}) collective-permute-start(bf16[8,96,128]{2,1,0:T(8,128)(2,1)S(1)} %collective-permute-done.4.refs_1_), channel_id=1, source_target_pairs={{0,64},{64,128},{128,192},{192,256},{256,320},{320,384},{384,448},... | collective-permute-start | bytes 589832 | tf_op jit(solution)/shard_map/ppermute | solution.py:183
  61.9 14.3 %all-to-all-start.1 = ((bf16[8,4,48,128]{3,2,1,0:T(8,128)(2,1)}), bf16[8,4,48,128]{3,2,1,0:T(8,128)(2,1)S(1)}, u32[]{:S(2)}, u32[]{:S(2)}) async-start(bf16[8,4,48,128]{3,2,1,0:T(8,128)(2,1)} %get-tuple-element.30), calls=%async_computation.1 | async-start | bytes 786432 | tf_op jit(solution)/shard_map/all_to_all | solution.py:207
  68.2 15.8 %collective-permute-start.7 = (bf16[8,96,128]{2,1,0:T(8,128)(2,1)}, bf16[8,96,128]{2,1,0:T(8,128)(2,1)}, u32[]{:S(2)}, u32[]{:S(2)}) collective-permute-start(bf16[8,96,128]{2,1,0:T(8,128)(2,1)} %collective-permute-done.5.refs_2_), channel_id=1, source_target_pairs={{0,448},{64,0},{128,64},{192,128},{256,192},{320,256},{384,320},{4... | collective-permute-start | bytes 589832 | tf_op jit(solution)/shard_map/ppermute | solution.py:183
  72.9 16.3 %collective-permute-start.8 = (bf16[8,96,128]{2,1,0:T(8,128)(2,1)}, bf16[8,96,128]{2,1,0:T(8,128)(2,1)}, u32[]{:S(2)}, u32[]{:S(2)}) collective-permute-start(bf16[8,96,128]{2,1,0:T(8,128)(2,1)} %collective-permute-done.6.refs_3_), channel_id=1, source_target_pairs={{0,64},{64,128},{128,192},{192,256},{256,320},{320,384},{384,448},... | collective-permute-start | bytes 589832 | tf_op jit(solution)/shard_map/ppermute | solution.py:183
  77.0 31.7 %all-to-all-start.2 = ((bf16[8,48,768]{2,1,0:T(8,128)(2,1)}), bf16[8,48,768]{2,1,0:T(8,128)(2,1)S(1)}, u32[]{:S(2)}, u32[]{:S(2)}) async-start(bf16[8,48,768]{2,1,0:T(8,128)(2,1)} %broadcast_in_dim.2), calls=%async_computation.2 | async-start | bytes 1179648 | tf_op jit(solution)/shard_map/all_to_all | solution.py:207
  83.9 14.5 %copy-start.7 = (bf16[8,96,128]{2,1,0:T(8,128)(2,1)S(1)}, bf16[8,96,128]{2,1,0:T(8,128)(2,1)}, u32[]{:S(2)}) copy-start(bf16[8,96,128]{2,1,0:T(8,128)(2,1)} %copy-done.6) | copy-start | bytes 589828
  84.0 9.6 %collective-permute-start.9 = (bf16[8,96,128]{2,1,0:T(8,128)(2,1)}, bf16[8,96,128]{2,1,0:T(8,128)(2,1)S(1)}, u32[]{:S(2)}, u32[]{:S(2)}) collective-permute-start(bf16[8,96,128]{2,1,0:T(8,128)(2,1)} %collective-permute-done.7.refs_4_), channel_id=1, source_target_pairs={{0,448},{64,0},{128,64},{192,128},{256,192},{320,256},{384,320},{4... | collective-permute-start | bytes 589832 | tf_op jit(solution)/shard_map/ppermute | solution.py:183
  89.2 9.2 %collective-permute-start.10 = (bf16[8,96,128]{2,1,0:T(8,128)(2,1)}, bf16[8,96,128]{2,1,0:T(8,128)(2,1)S(1)}, u32[]{:S(2)}, u32[]{:S(2)}) collective-permute-start(bf16[8,96,128]{2,1,0:T(8,128)(2,1)} %collective-permute-done.8.refs_5_), channel_id=1, source_target_pairs={{0,64},{64,128},{128,192},{192,256},{256,320},{320,384},{384,448},... | collective-permute-start | bytes 589832 | tf_op jit(solution)/shard_map/ppermute | solution.py:183
  108.8 14.2 %all-to-all-start.3 = ((bf16[8,4,64,128]{3,2,1,0:T(8,128)(2,1)}), bf16[8,4,64,128]{3,2,1,0:T(8,128)(2,1)S(1)}, u32[]{:S(2)}, u32[]{:S(2)}) async-start(bf16[8,4,64,128]{3,2,1,0:T(8,128)(2,1)} %shard_map.87), calls=%async_computation.3 | async-start | bytes 1048576 | tf_op jit(solution)/shard_map/all_to_all | solution.py:207
  113.6 17.4 %collective-permute-start.11 = (bf16[8,48,768]{2,1,0:T(8,128)(2,1)S(1)}, bf16[8,48,768]{2,1,0:T(8,128)(2,1)S(1)}, u32[]{:S(2)}, u32[]{:S(2)}) collective-permute-start(bf16[8,48,768]{2,1,0:T(8,128)(2,1)S(1)} %all-to-all-done.2.w_near_ref), channel_id=1, source_target_pairs={{0,16},{16,0},{1,17},{17,1},{2,18},{18,2},{3,19},{19,3},{4,20},{20... | collective-permute-start | bytes 1769480 | tf_op jit(solution)/shard_map/ppermute | solution.py:183
  124.4 14.5 %all-to-all-start.4 = ((bf16[8,64,128]{2,1,0:T(8,128)(2,1)}), bf16[8,64,128]{2,1,0:T(8,128)(2,1)S(1)}, u32[]{:S(2)}, u32[]{:S(2)}) async-start(bf16[8,64,128]{2,1,0:T(8,128)(2,1)} %shard_map.88), calls=%async_computation.4 | async-start | bytes 262144 | tf_op jit(solution)/shard_map/all_to_all | solution.py:207

commit v6 on v5

--- a/solution.py
+++ b/solution.py
@@ -112,25 +112,43 @@
             out_ref[2 * p + 1, :, role * 128 : (role + 1) * 128] = odd.astype(BF16)
 
 
-def attend_kernel(shifts, pos_ref, q_ref, keep_ref, recv_ref, far_ref, *refs):
-    kv_refs, out_ref = refs[:-1], refs[-1]
+def attend_kernel(steps, first, last, pos_ref, q_ref, keep_ref, recv_ref, far_ref, *refs):
+    count = sum(len(s) for s in steps)
+    kv_refs, rest = refs[:count], refs[count:]
     me, yy = pos_ref[1] * 2 + pos_ref[2], pos_ref[4]
+    acc = [None, None] if first else [rest[0][i] for i in range(2)]
+    top = [None, None] if first else [rest[1][i, :1] for i in range(2)]
+    at = 0
+    for step in steps:
+        bias = []
+        for sh in step:
+            y = lax.rem(yy + 8 + sh, 8)
+            bias.append(
+                jnp.concatenate([keep_ref[0, y], recv_ref[0, y], far_ref[0, y], far_ref[1, y]], axis=1).astype(F32)
+            )
+        bias = jnp.concatenate(bias, axis=0)
+        blocks = kv_refs[at : at + len(step)]
+        at += len(step)
+        for i in range(2):
+            keys = jnp.concatenate([jnp.transpose(r[i, :HD].astype(F32)).astype(BF16) for r in blocks], axis=0)
+            vals = jnp.concatenate([r[i, HD:] for r in blocks], axis=1)
+            vals = jnp.concatenate([vals, jnp.ones((16, vals.shape[1]), BF16)], axis=0)
+            scores = jnp.dot(keys, q_ref[i], preferred_element_type=F32) + bias
+            best = jnp.max(scores, axis=0, keepdims=True)
+            if top[i] is not None:
+                best = jnp.maximum(best, top[i])
+            probs = jnp.exp(scores - best).astype(BF16)
+            part = jnp.dot(vals, probs, preferred_element_type=F32)
+            if top[i] is not None:
+                part = part + acc[i] * jnp.exp(top[i] - best)
+            acc[i], top[i] = part, best
+    if not last:
+        for i in range(2):
+            rest[-2][i] = acc[i]
+            rest[-1][i] = jnp.broadcast_to(top[i], (8, top[i].shape[1]))
+        return
+    out_ref = rest[-1]
     row = lax.broadcasted_iota(jnp.int32, (16, 128), 0)
-    bias = []
-    for by in shifts:
-        y = lax.rem(yy + 8 + by, 8)
-        bias.append(jnp.concatenate([keep_ref[0, y], recv_ref[0, y], far_ref[0, y], far_ref[1, y]], axis=1).astype(F32))
-    bias = jnp.concatenate(bias, axis=0)
-    acc, top = [], []
-    for i in range(2):
-        keys = jnp.concatenate([jnp.transpose(r[i, :HD].astype(F32)).astype(BF16) for r in kv_refs], axis=0)
-        vals = jnp.concatenate([r[i, HD:] for r in kv_refs], axis=1)
-        vals = jnp.concatenate([vals, jnp.ones((16, vals.shape[1]), BF16)], axis=0)
-        scores = jnp.dot(keys, q_ref[i], preferred_element_type=F32) + bias
-        best = jnp.max(scores, axis=0, keepdims=True)
-        probs = jnp.exp(scores - best).astype(BF16)
-        acc.append(jnp.dot(vals, probs, preferred_element_type=F32))
-        top.append(best)
     for role in range(4):
         d = 2 * jnp.bitwise_xor(me, role)
         tiles = []
@@ -192,7 +210,7 @@
     vm = pl.BlockSpec(memory_space=pltpu.VMEM)
     sm = pl.BlockSpec(memory_space=pltpu.SMEM)
 
-    def call(kernel, specs, out, *args, scratch=()):
+    def call(kernel, specs, out, *args, scratch=(), mib=16):
         shapes = [jax.ShapeDtypeStruct(s, t) for s, t in out]
         return pl.pallas_call(
             kernel,
@@ -200,7 +218,7 @@
             in_specs=specs,
             out_specs=[vm] * len(out),
             scratch_shapes=scratch,
-            compiler_params=params(),
+            compiler_params=params(mib),
         )(*args)
 
     def exchange(x, axes):
@@ -229,6 +247,7 @@
         tokens,
         chain_embed,
         hot_embed,
+        mib=56,
     )
     gathered = exchange(copies, "z")
     weights_other, far_out = lax.optimization_barrier((weights_other, far_out))
@@ -248,44 +267,55 @@
         weights,
         weights_other,
     )
+    w_rows = jnp.where(at["core"] == at["xhi"], w_out, weights_other[4 * HD :])
+    w_near = jnp.broadcast_to(w_rows[None], (peers, HD, width))
+    w_near, kv_own = lax.optimization_barrier((w_near, kv_own))
+    w_near = exchange(w_near, "z")
     kv_other = shift(kv_other, "xhi", 1)
     (kv,) = call(join_kernel, [vm, vm], [((samples, 2 * HD, 128), BF16)], kv_own, kv_other)
 
-    kv, far = lax.optimization_barrier((kv, far))
     right, left, ring, shifts = kv, kv, [kv], [0]
     for step in range(1, 5):
         right = shift(right, "y", 1)
-        if step == 1:
-            right, q_out = lax.optimization_barrier((right, q_out))
         ring.append(right)
         shifts.append(-step)
         if step < 4:
             left = shift(left, "y", -1)
+            if step == 1:
+                left, q_out, w_near = lax.optimization_barrier((left, q_out, w_near))
             ring.append(left)
             shifts.append(step)
     q_in = exchange(q_out, OCT)
     (q_all,) = call(join_q_kernel, [sm, vm], [((samples, HD, 512), BF16)], pos, q_in)
 
-    w_rows = jnp.where(at["core"] == at["xhi"], w_out, weights_other[4 * HD :])
-    w_rows, q_in = lax.optimization_barrier((w_rows, q_in))
-    w_near = exchange(jnp.broadcast_to(w_rows[None], (peers, HD, width)), "z")
-
     def two(*dims):
         return pl.BlockSpec((2,) + dims, lambda s, _: (s,) + (0,) * len(dims))
 
     whole = pl.BlockSpec((2, 8, 128, 128), lambda s, _: (0, 0, 0, 0))
-    parts = pl.pallas_call(
-        functools.partial(attend_kernel, tuple(shifts)),
-        out_shape=jax.ShapeDtypeStruct((8, pairs, 64, 128), BF16),
-        grid_spec=pltpu.PrefetchScalarGridSpec(
-            num_scalar_prefetch=1,
-            grid=(pairs,),
-            in_specs=[two(HD, 512), whole, whole, whole] + [two(2 * HD, 128)] * 8,
-            out_specs=pl.BlockSpec((8, 1, 64, 128), lambda s, _: (0, s, 0, 0)),
-        ),
-        compiler_params=params(32),
-        cost_estimate=pl.CostEstimate(flops=1 << 33, bytes_accessed=4 << 20, transcendentals=1 << 22),
-    )(pos, q_all, keep, recv, far, *ring)
+    state = (((samples, 64, 512), F32), ((samples, 8, 512), F32))
+
+    def attend(blocks, carried, last):
+        out = [((8, pairs, 64, 128), BF16)] if last else state
+        state_specs = [two(64, 512), two(8, 512)]
+        return pl.pallas_call(
+            functools.partial(attend_kernel, (tuple(shifts[i] for i in blocks),), not carried, last),
+            out_shape=[jax.ShapeDtypeStruct(s, t) for s, t in out],
+            grid_spec=pltpu.PrefetchScalarGridSpec(
+                num_scalar_prefetch=1,
+                grid=(pairs,),
+                in_specs=[two(HD, 512), whole, whole, whole]
+                + [two(2 * HD, 128)] * len(blocks)
+                + (state_specs if carried else []),
+                out_specs=[pl.BlockSpec((8, 1, 64, 128), lambda s, _: (0, s, 0, 0))] if last else state_specs,
+            ),
+            compiler_params=params(24),
+            cost_estimate=pl.CostEstimate(
+                flops=len(blocks) << 30, bytes_accessed=4 << 20, transcendentals=len(blocks) << 19
+            ),
+        )(pos, q_all, keep, recv, far, *[ring[i] for i in blocks], *carried)
+
+    carried = attend((0, 1, 2, 3, 4, 5), [], False)
+    (parts,) = attend((6, 7), carried, True)
     parts, w_near = lax.optimization_barrier((parts, w_near))
     w_far = shift(w_near, "core", 1)
     mine = exchange(parts, OCT)

time: 142 us -> 135 us (0.951)
  waiting for transfers between devices: 41 us -> 32.6 us
  Pallas kernels: 19.7 us -> 23.2 us
    ppermute x12, waiting for transfers between devices: 22.5 us -> 12.1 us  [shift(): return lax.ppermute(x, axis, [(i, (i + by) % n) for i in range(n)])]
    pallas_call x1 -> x2, Pallas kernels: 10.3 us -> 13.4 us  [attend(): pl.pallas_call(functools.partial(attend_kernel, (tuple((shifts[i] for i i...]
    all_to_all x5, waiting for transfers between devices: 18.6 us -> 20.5 us  [exchange(): return lax.all_to_all(x, axes, split_axis=0, concat_axis=0, tiled=True)]
    unnamed x22 -> x8, local copies, waits for them, and re-layouts: 1.52 us -> 0.02 us
  transfers between devices with their start and end apart: 17 -> 17, of which waited for: 9 -> 6; matrix products, arithmetic and copies ran while one was open for 1% -> 1% of each run, Pallas kernels for 12% -> 9%
where the time goes in v6:
time: 135 us; the launch traced here: 133 us
  starting transfers between devices  74.6 us (55%)
  waiting for transfers between devices  32.6 us (24%)
  Pallas kernels  23.2 us (17%)
  local copies, waits for them, and re-layouts  1.6 us (1%)
    ppermute x12, starting transfers between devices, shift(): return lax.ppermute(x, axis, [(i, (i + by) % n) for i in range(n)])  39.5 us
    all_to_all x5, starting transfers between devices, exchange(): return lax.all_to_all(x, axes, split_axis=0, concat_axis=0, tiled=True)  35.2 us
    all_to_all x5, waiting for transfers between devices, exchange(): return lax.all_to_all(x, axes, split_axis=0, concat_axis=0, tiled=True)  20.5 us
    pallas_call x2, Pallas kernels, attend(): pl.pallas_call(functools.partial(attend_kernel, (tuple((shifts[i] for i i...  13.4 us
    ppermute x12, waiting for transfers between devices, shift(): return lax.ppermute(x, axis, [(i, (i + by) % n) for i in range(n)])  12.1 us
    pallas_call x7, Pallas kernels, call(): pl.pallas_call(kernel, out_shape=shapes, in_specs=specs, out_specs=[vm] *...  9.85 us
  transfers between devices with their start and end apart: 17, of which 6 were waited for; matrix products, arithmetic and copies ran while one was open for 1% of the time, Pallas kernels for 9%

profile of v6, /device:TPU:1, one launch (start us, length us, event | category | flops | bytes accessed | tf_op | source)
XLA Modules:
  0.0 133.2 jit_solution(15646605578137923671)
XLA Ops:
  0.0 0.7 stack.26.pos_ref
  0.7 0.0 copy-start
  0.7 2.3 %shard_map.83 = bf16[8,64,768]{2,1,0:T(8,128)(2,1)} custom-call(s32[5]{0:T(128)} %stack.26.pos_ref, s32[8]{0:T(128)} %chain_ref.1, s32[16]{0:T(128)} %hot_ref.1, bf16[8,8,768]{2,1,0:T(8,128)(2,1)} %tok_ref.1, bf16[4,768]{1,0:T(4,128)(2,1)} %emb_ref.1, bf16[768]{0:T(1024)(128)(2,1)} %hemb_ref.1), custom_call_target="tpu_custom_call" | custom-call | tf_op jit(solution)/shard_map/pallas_call | solution.py:215
  3.0 0.0 copy-start.1
  3.0 11.0 %all-to-all-start = ((bf16[8,64,768]{2,1,0:T(8,128)(2,1)}), bf16[8,64,768]{2,1,0:T(8,128)(2,1)S(1)}, u32[]{:S(2)}, u32[]{:S(2)}) async-start(bf16[8,64,768]{2,1,0:T(8,128)(2,1)} %shard_map.83), calls=%async_computation | async-start | bytes 1572864 | tf_op jit(solution)/shard_map/all_to_all | solution.py:225
  14.0 0.0 copy-done
  14.0 0.0 copy-done.1
  14.0 0.0 copy-start.2
  14.0 0.0 copy-start.3
  14.1 1.8 %shard_map.82 = (bf16[2,8,128,128]{3,2,1,0:T(8,128)(2,1)S(1)}, bf16[2,8,128,128]{3,2,1,0:T(8,128)(2,1)S(1)}) custom-call(s32[5]{0:T(128)S(1)} %copy-done.1, bf16[1,128,4096]{2,1,0:T(8,128)(2,1)S(1)} %copy-done), custom_call_target="tpu_custom_call" | custom-call | tf_op jit(solution)/shard_map/pallas_call | solution.py:215
  15.9 2.9 %collective-permute-start.1 = (bf16[2,8,128,128]{3,2,1,0:T(8,128)(2,1)S(1)}, bf16[2,8,128,128]{3,2,1,0:T(8,128)(2,1)S(1)}, u32[]{:S(2)}, u32[]{:S(2)}) collective-permute-start(bf16[2,8,128,128]{3,2,1,0:T(8,128)(2,1)S(1)} %get-tuple-element.24), channel_id=1, source_target_pairs={{0,16},{16,0},{1,17},{17,1},{2,18},{18,2},{3,19},{19,3},{4,20},{20... | collective-permute-start | bytes 1572872 | tf_op jit(solution)/shard_map/ppermute | solution.py:201
  18.8 0.0 copy-done.2
  18.8 0.0 copy-done.3
  18.8 4.6 %collective-permute-start = (bf16[240,768]{1,0:T(8,128)(2,1)S(1)}, bf16[240,768]{1,0:T(8,128)(2,1)S(1)}, u32[]{:S(2)}, u32[]{:S(2)}) collective-permute-start(bf16[240,768]{1,0:T(8,128)(2,1)S(1)} %pad_maximum_fusion.1.own_ref), channel_id=1, source_target_pairs={{0,1},{1,0},{2,3},{3,2},{4,5},{5,4},{6,7},{7,6},{8,9},{9,8},{10,11... | collective-permute-start | bytes 1105928 | tf_op jit(solution)/shard_map/ppermute | solution.py:201
  23.5 0.0 collective-permute-done.1.recv_ref
  23.5 0.9 pad_maximum_fusion
  24.4 8.0 %collective-permute-done.other_ref = bf16[240,768]{1,0:T(8,128)(2,1)S(1)} collective-permute-done((bf16[240,768]{1,0:T(8,128)(2,1)S(1)}, bf16[240,768]{1,0:T(8,128)(2,1)S(1)}, u32[]{:S(2)}, u32[]{:S(2)}) %collective-permute-start) | collective-permute-done | bytes 368672 | tf_op jit(solution)/shard_map/ppermute | solution.py:201
  32.4 5.1 %all-to-all-done.x_ref = bf16[8,64,768]{2,1,0:T(8,128)(2,1)S(1)} async-done(((bf16[8,64,768]{2,1,0:T(8,128)(2,1)}), bf16[8,64,768]{2,1,0:T(8,128)(2,1)S(1)}, u32[]{:S(2)}, u32[]{:S(2)}) %all-to-all-start) | async-done | bytes 786464 | tf_op jit(solution)/shard_map/all_to_all | solution.py:225
  37.6 2.2 %shard_map.84 = (bf16[8,4,48,128]{3,2,1,0:T(8,128)(2,1)}, bf16[4,96,128]{2,1,0:T(8,128)(2,1)S(1)}, bf16[4,96,128]{2,1,0:T(8,128)(2,1)S(1)}, f32[2,4,48,128]{3,2,1,0:T(8,128)S(1)}) custom-call(s32[5]{0:T(128)S(1)} %copy-done.1, bf16[8,64,768]{2,1,0:T(8,128)(2,1)S(1)} %all-to-all-done.x_ref, bf16[240,768]{1,0:T(8,128)(2,1)S(1)} %pad_maximum_fusion.1.own_ref, ...), custom_call_target="tpu_custom_call" | custom-call | tf_op jit(solution)/shard_map/pallas_call | solution.py:215
  39.8 0.9 broadcast_in_dim.2
  40.6 3.5 %all-to-all-start.1 = ((bf16[8,48,768]{2,1,0:T(8,128)(2,1)}), bf16[8,48,768]{2,1,0:T(8,128)(2,1)S(1)}, u32[]{:S(2)}, u32[]{:S(2)}) async-start(bf16[8,48,768]{2,1,0:T(8,128)(2,1)} %broadcast_in_dim.2), calls=%async_computation.1 | async-start | bytes 1179648 | tf_op jit(solution)/shard_map/all_to_all | solution.py:225
  44.2 4.7 %collective-permute-start.2 = (bf16[4,96,128]{2,1,0:T(8,128)(2,1)S(1)}, bf16[4,96,128]{2,1,0:T(8,128)(2,1)S(1)}, u32[]{:S(2)}, u32[]{:S(2)}) collective-permute-start(bf16[4,96,128]{2,1,0:T(8,128)(2,1)S(1)} %get-tuple-element.30), channel_id=1, source_target_pairs={{0,1},{1,0},{2,3},{3,2},{4,5},{5,4},{6,7},{7,6},{8,9},{9,8},{10,11... | collective-permute-start | bytes 294920 | tf_op jit(solution)/shard_map/ppermute | solution.py:201
  48.8 2.6 %collective-permute-done.2.other_ref = bf16[4,96,128]{2,1,0:T(8,128)(2,1)S(1)} collective-permute-done((bf16[4,96,128]{2,1,0:T(8,128)(2,1)S(1)}, bf16[4,96,128]{2,1,0:T(8,128)(2,1)S(1)}, u32[]{:S(2)}, u32[]{:S(2)}) %collective-permute-start.2) | collective-permute-done | bytes 98336 | tf_op jit(solution)/shard_map/ppermute | solution.py:201
  51.4 0.1 shard_map.85.refs_0_
  51.6 3.2 %collective-permute-start.7 = (bf16[8,96,128]{2,1,0:T(8,128)(2,1)S(1)}, bf16[8,96,128]{2,1,0:T(8,128)(2,1)S(1)}, u32[]{:S(2)}, u32[]{:S(2)}) collective-permute-start(bf16[8,96,128]{2,1,0:T(8,128)(2,1)S(1)} %shard_map.85.refs_0_), channel_id=1, source_target_pairs={{0,64},{64,128},{128,192},{192,256},{256,320},{320,384},{384,448},... | collective-permute-start | bytes 589832 | tf_op jit(solution)/shard_map/ppermute | solution.py:201
  54.8 3.8 %collective-permute-start.3 = (bf16[8,96,128]{2,1,0:T(8,128)(2,1)S(1)}, bf16[8,96,128]{2,1,0:T(8,128)(2,1)S(1)}, u32[]{:S(2)}, u32[]{:S(2)}) collective-permute-start(bf16[8,96,128]{2,1,0:T(8,128)(2,1)S(1)} %shard_map.85.refs_0_), channel_id=1, source_target_pairs={{0,448},{64,0},{128,64},{192,128},{256,192},{320,256},{384,320},{4... | collective-permute-start | bytes 589832 | tf_op jit(solution)/shard_map/ppermute | solution.py:201
  58.6 3.1 %collective-permute-start.4 = (bf16[2,8,128,128]{3,2,1,0:T(8,128)(2,1)}, bf16[2,8,128,128]{3,2,1,0:T(8,128)(2,1)S(1)}, u32[]{:S(2)}, u32[]{:S(2)}) collective-permute-start(bf16[2,8,128,128]{3,2,1,0:T(8,128)(2,1)} %pad_maximum_fusion), channel_id=1, source_target_pairs={{0,32},{32,0},{1,33},{33,1},{2,34},{34,2},{3,35},{35,3},{4,36},{36... | collective-permute-start | bytes 1572872 | tf_op jit(solution)/shard_map/ppermute | solution.py:201
  61.7 0.0 collective-permute-done.7.refs_1_
  61.7 1.9 %collective-permute-start.8 = (bf16[8,96,128]{2,1,0:T(8,128)(2,1)S(1)}, bf16[8,96,128]{2,1,0:T(8,128)(2,1)S(1)}, u32[]{:S(2)}, u32[]{:S(2)}) collective-permute-start(bf16[8,96,128]{2,1,0:T(8,128)(2,1)S(1)} %collective-permute-done.7.refs_1_), channel_id=1, source_target_pairs={{0,64},{64,128},{128,192},{192,256},{256,320},{320,384},{384,448},... | collective-permute-start | bytes 589832 | tf_op jit(solution)/shard_map/ppermute | solution.py:201
  63.7 0.0 collective-permute-done.3.refs_2_
  63.7 0.0 all-to-all-done.1.w_near_ref
  63.7 6.0 %all-to-all-start.2 = ((bf16[8,4,48,128]{3,2,1,0:T(8,128)(2,1)}), bf16[8,4,48,128]{3,2,1,0:T(8,128)(2,1)S(1)}, u32[]{:S(2)}, u32[]{:S(2)}) async-start(bf16[8,4,48,128]{3,2,1,0:T(8,128)(2,1)} %get-tuple-element.33), calls=%async_computation.2 | async-start | bytes 786432 | tf_op jit(solution)/shard_map/all_to_all | solution.py:225
  69.7 0.0 collective-permute-done.8.refs_3_
  69.7 3.2 %collective-permute-start.9 = (bf16[8,96,128]{2,1,0:T(8,128)(2,1)S(1)}, bf16[8,96,128]{2,1,0:T(8,128)(2,1)}, u32[]{:S(2)}, u32[]{:S(2)}) collective-permute-start(bf16[8,96,128]{2,1,0:T(8,128)(2,1)S(1)} %collective-permute-done.8.refs_3_), channel_id=1, source_target_pairs={{0,64},{64,128},{128,192},{192,256},{256,320},{320,384},{384,448},... | collective-permute-start | bytes 589832 | tf_op jit(solution)/shard_map/ppermute | solution.py:201
  72.9 3.5 %collective-permute-start.5 = (bf16[8,96,128]{2,1,0:T(8,128)(2,1)S(1)}, bf16[8,96,128]{2,1,0:T(8,128)(2,1)}, u32[]{:S(2)}, u32[]{:S(2)}) collective-permute-start(bf16[8,96,128]{2,1,0:T(8,128)(2,1)S(1)} %collective-permute-done.3.refs_2_), channel_id=1, source_target_pairs={{0,448},{64,0},{128,64},{192,128},{256,192},{320,256},{384,320},{4... | collective-permute-start | bytes 589832 | tf_op jit(solution)/shard_map/ppermute | solution.py:201
  76.4 1.4 %collective-permute-done.9.refs_5_ = bf16[8,96,128]{2,1,0:T(8,128)(2,1)} collective-permute-done((bf16[8,96,128]{2,1,0:T(8,128)(2,1)S(1)}, bf16[8,96,128]{2,1,0:T(8,128)(2,1)}, u32[]{:S(2)}, u32[]{:S(2)}) %collective-permute-start.9) | collective-permute-done | bytes 196640 | tf_op jit(solution)/shard_map/ppermute | solution.py:201
  77.8 3.4 %collective-permute-start.10 = (bf16[8,96,128]{2,1,0:T(8,128)(2,1)}, bf16[8,96,128]{2,1,0:T(8,128)(2,1)}, u32[]{:S(2)}, u32[]{:S(2)}) collective-permute-start(bf16[8,96,128]{2,1,0:T(8,128)(2,1)} %collective-permute-done.9.refs_5_), channel_id=1, source_target_pairs={{0,64},{64,128},{128,192},{192,256},{256,320},{320,384},{384,448},... | collective-permute-start | bytes 589832 | tf_op jit(solution)/shard_map/ppermute | solution.py:201
  81.2 0.0 collective-permute-done.5.refs_4_
  81.2 3.3 %collective-permute-start.6 = (bf16[8,96,128]{2,1,0:T(8,128)(2,1)}, bf16[8,96,128]{2,1,0:T(8,128)(2,1)}, u32[]{:S(2)}, u32[]{:S(2)}) collective-permute-start(bf16[8,96,128]{2,1,0:T(8,128)(2,1)} %collective-permute-done.5.refs_4_), channel_id=1, source_target_pairs={{0,448},{64,0},{128,64},{192,128},{256,192},{320,256},{384,320},{4... | collective-permute-start | bytes 589832 | tf_op jit(solution)/shard_map/ppermute | solution.py:201
  84.5 0.0 all-to-all-done.2.q_ref
  84.5 0.7 shard_map.86.q_ref
  85.2 0.0 collective-permute-done.4.far_ref
  85.2 7.6 %shard_map.87 = (f32[8,64,512]{2,1,0:T(8,128)S(1)}, f32[8,8,512]{2,1,0:T(8,128)S(1)}) custom-call(s32[5]{0:T(128)S(1)} %copy-done.1, bf16[8,48,512]{2,1,0:T(8,128)(2,1)S(1)} %shard_map.86.q_ref, bf16[2,8,128,128]{3,2,1,0:T(8,128)(2,1)S(1)} %get-tuple-element.23.keep_ref, bf16[2,8,128,128]{3,2,1,0:T(8,128)(2,1)S(1)} %collective-permute-done.1.recv_ref, ...), custom_call_target="tpu_custom_call" | custom-call | flops 6442450944 | bytes 4194304 | tf_op jit(solution)/shard_map/pallas_call | solution.py:300
  92.9 0.0 collective-permute-done.10.refs_1_
  92.9 0.0 collective-permute-done.6.refs_0_
  92.9 5.7 %shard_map.88 = bf16[8,4,64,128]{3,2,1,0:T(8,128)(2,1)} custom-call(s32[5]{0:T(128)S(1)} %copy-done.1, bf16[8,48,512]{2,1,0:T(8,128)(2,1)S(1)} %shard_map.86.q_ref, bf16[2,8,128,128]{3,2,1,0:T(8,128)(2,1)S(1)} %get-tuple-element.23.keep_ref, bf16[2,8,128,128]{3,2,1,0:T(8,128)(2,1)S(1)} %collective-permute-done.1.recv_ref, ...), custom_call_target="tpu_custom_call" | custom-call | flops 2147483648 | bytes 4194304 | tf_op jit(solution)/shard_map/pallas_call | solution.py:300
  98.7 7.9 %all-to-all-start.3 = ((bf16[8,4,64,128]{3,2,1,0:T(8,128)(2,1)}), bf16[8,4,64,128]{3,2,1,0:T(8,128)(2,1)S(1)}, u32[]{:S(2)}, u32[]{:S(2)}) async-start(bf16[8,4,64,128]{3,2,1,0:T(8,128)(2,1)} %shard_map.88), calls=%async_computation.3 | async-start | bytes 1048576 | tf_op jit(solution)/shard_map/all_to_all | solution.py:225
  106.5 1.9 %collective-permute-start.11 = (bf16[8,48,768]{2,1,0:T(8,128)(2,1)S(1)}, bf16[8,48,768]{2,1,0:T(8,128)(2,1)S(1)}, u32[]{:S(2)}, u32[]{:S(2)}) collective-permute-start(bf16[8,48,768]{2,1,0:T(8,128)(2,1)S(1)} %all-to-all-done.1.w_near_ref), channel_id=1, source_target_pairs={{0,16},{16,0},{1,17},{17,1},{2,18},{18,2},{3,19},{19,3},{4,20},{20... | collective-permute-start | bytes 1769480 | tf_op jit(solution)/shard_map/ppermute | solution.py:201
  108.4 7.5 %all-to-all-done.3.p_ref = bf16[8,4,64,128]{3,2,1,0:T(8,128)(2,1)S(1)} async-done(((bf16[8,4,64,128]{3,2,1,0:T(8,128)(2,1)}), bf16[8,4,64,128]{3,2,1,0:T(8,128)(2,1)S(1)}, u32[]{:S(2)}, u32[]{:S(2)}) %all-to-all-start.3) | async-done | bytes 524320 | tf_op jit(solution)/shard_map/all_to_all | solution.py:225
  115.9 1.4 %shard_map.89 = bf16[8,64,128]{2,1,0:T(8,128)(2,1)} custom-call(s32[5]{0:T(128)S(1)} %copy-done.1, bf16[8,4,64,128]{3,2,1,0:T(8,128)(2,1)S(1)} %all-to-all-done.3.p_ref, f32[2,4,48,128]{3,2,1,0:T(8,128)S(1)} %get-tuple-element.39.gate_ref), custom_call_target="tpu_custom_call" | custom-call | tf_op jit(solution)/shard_map/pallas_call | solution.py:215
  117.3 6.7 %all-to-all-start.4 = ((bf16[8,64,128]{2,1,0:T(8,128)(2,1)}), bf16[8,64,128]{2,1,0:T(8,128)(2,1)S(1)}, u32[]{:S(2)}, u32[]{:S(2)}) async-start(bf16[8,64,128]{2,1,0:T(8,128)(2,1)} %shard_map.89), calls=%async_computation.4 | async-start | bytes 262144 | tf_op jit(solution)/shard_map/all_to_all | solution.py:225
  124.1 0.0 collective-permute-done.11.w_far_ref
  124.1 7.9 %all-to-all-done.4.g_ref = bf16[8,64,128]{2,1,0:T(8,128)(2,1)S(1)} async-done(((bf16[8,64,128]{2,1,0:T(8,128)(2,1)}), bf16[8,64,128]{2,1,0:T(8,128)(2,1)S(1)}, u32[]{:S(2)}, u32[]{:S(2)}) %all-to-all-start.4) | async-done | bytes 131104 | tf_op jit(solution)/shard_map/all_to_all | solution.py:225
  132.0 1.3 shard_map.90
  (4 shorter events, 0.1 us)
Async XLA Ops:
  0.7 13.3 %copy-start = (bf16[1,128,4096]{2,1,0:T(8,128)(2,1)S(1)}, bf16[1,128,4096]{2,1,0:T(8,128)(2,1)}, u32[]{:S(2)}) copy-start(bf16[1,128,4096]{2,1,0:T(8,128)(2,1)} %b_ref.1) | copy-start | bytes 3145732
  3.0 11.0 %copy-start.1 = (s32[5]{0:T(128)S(1)}, s32[5]{0:T(128)}, u32[]{:S(2)}) copy-start(s32[5]{0:T(128)} %stack.26.pos_ref) | copy-start | bytes 64
  3.0 34.6 %all-to-all-start = ((bf16[8,64,768]{2,1,0:T(8,128)(2,1)}), bf16[8,64,768]{2,1,0:T(8,128)(2,1)S(1)}, u32[]{:S(2)}, u32[]{:S(2)}) async-start(bf16[8,64,768]{2,1,0:T(8,128)(2,1)} %shard_map.83), calls=%async_computation | async-start | bytes 1572864 | tf_op jit(solution)/shard_map/all_to_all | solution.py:225
  14.0 4.7 %copy-start.2 = (bf16[48,768]{1,0:T(8,128)(2,1)S(1)}, bf16[48,768]{1,0:T(8,128)(2,1)}, u32[]{:S(2)}) copy-start(bf16[48,768]{1,0:T(8,128)(2,1)} %param.15) | copy-start | bytes 221188
  14.0 4.7 %copy-start.3 = (bf16[768,192]{0,1:T(8,128)(2,1)S(1)}, bf16[768,192]{0,1:T(8,128)(2,1)}, u32[]{:S(2)}) copy-start(bf16[768,192]{0,1:T(8,128)(2,1)} %param.13) | copy-start | bytes 884740
  15.9 7.6 %collective-permute-start.1 = (bf16[2,8,128,128]{3,2,1,0:T(8,128)(2,1)S(1)}, bf16[2,8,128,128]{3,2,1,0:T(8,128)(2,1)S(1)}, u32[]{:S(2)}, u32[]{:S(2)}) collective-permute-start(bf16[2,8,128,128]{3,2,1,0:T(8,128)(2,1)S(1)} %get-tuple-element.24), channel_id=1, source_target_pairs={{0,16},{16,0},{1,17},{17,1},{2,18},{18,2},{3,19},{19,3},{4,20},{20... | collective-permute-start | bytes 1572872 | tf_op jit(solution)/shard_map/ppermute | solution.py:201
  18.8 13.6 %collective-permute-start = (bf16[240,768]{1,0:T(8,128)(2,1)S(1)}, bf16[240,768]{1,0:T(8,128)(2,1)S(1)}, u32[]{:S(2)}, u32[]{:S(2)}) collective-permute-start(bf16[240,768]{1,0:T(8,128)(2,1)S(1)} %pad_maximum_fusion.1.own_ref), channel_id=1, source_target_pairs={{0,1},{1,0},{2,3},{3,2},{4,5},{5,4},{6,7},{7,6},{8,9},{9,8},{10,11... | collective-permute-start | bytes 1105928 | tf_op jit(solution)/shard_map/ppermute | solution.py:201
  40.6 23.1 %all-to-all-start.1 = ((bf16[8,48,768]{2,1,0:T(8,128)(2,1)}), bf16[8,48,768]{2,1,0:T(8,128)(2,1)S(1)}, u32[]{:S(2)}, u32[]{:S(2)}) async-start(bf16[8,48,768]{2,1,0:T(8,128)(2,1)} %broadcast_in_dim.2), calls=%async_computation.1 | async-start | bytes 1179648 | tf_op jit(solution)/shard_map/all_to_all | solution.py:225
  44.2 7.3 %collective-permute-start.2 = (bf16[4,96,128]{2,1,0:T(8,128)(2,1)S(1)}, bf16[4,96,128]{2,1,0:T(8,128)(2,1)S(1)}, u32[]{:S(2)}, u32[]{:S(2)}) collective-permute-start(bf16[4,96,128]{2,1,0:T(8,128)(2,1)S(1)} %get-tuple-element.30), channel_id=1, source_target_pairs={{0,1},{1,0},{2,3},{3,2},{4,5},{5,4},{6,7},{7,6},{8,9},{9,8},{10,11... | collective-permute-start | bytes 294920 | tf_op jit(solution)/shard_map/ppermute | solution.py:201
  51.6 10.2 %collective-permute-start.7 = (bf16[8,96,128]{2,1,0:T(8,128)(2,1)S(1)}, bf16[8,96,128]{2,1,0:T(8,128)(2,1)S(1)}, u32[]{:S(2)}, u32[]{:S(2)}) collective-permute-start(bf16[8,96,128]{2,1,0:T(8,128)(2,1)S(1)} %shard_map.85.refs_0_), channel_id=1, source_target_pairs={{0,64},{64,128},{128,192},{192,256},{256,320},{320,384},{384,448},... | collective-permute-start | bytes 589832 | tf_op jit(solution)/shard_map/ppermute | solution.py:201
  54.8 8.9 %collective-permute-start.3 = (bf16[8,96,128]{2,1,0:T(8,128)(2,1)S(1)}, bf16[8,96,128]{2,1,0:T(8,128)(2,1)S(1)}, u32[]{:S(2)}, u32[]{:S(2)}) collective-permute-start(bf16[8,96,128]{2,1,0:T(8,128)(2,1)S(1)} %shard_map.85.refs_0_), channel_id=1, source_target_pairs={{0,448},{64,0},{128,64},{192,128},{256,192},{320,256},{384,320},{4... | collective-permute-start | bytes 589832 | tf_op jit(solution)/shard_map/ppermute | solution.py:201
  58.6 26.6 %collective-permute-start.4 = (bf16[2,8,128,128]{3,2,1,0:T(8,128)(2,1)}, bf16[2,8,128,128]{3,2,1,0:T(8,128)(2,1)S(1)}, u32[]{:S(2)}, u32[]{:S(2)}) collective-permute-start(bf16[2,8,128,128]{3,2,1,0:T(8,128)(2,1)} %pad_maximum_fusion), channel_id=1, source_target_pairs={{0,32},{32,0},{1,33},{33,1},{2,34},{34,2},{3,35},{35,3},{4,36},{36... | collective-permute-start | bytes 1572872 | tf_op jit(solution)/shard_map/ppermute | solution.py:201
  61.7 8.0 %collective-permute-start.8 = (bf16[8,96,128]{2,1,0:T(8,128)(2,1)S(1)}, bf16[8,96,128]{2,1,0:T(8,128)(2,1)S(1)}, u32[]{:S(2)}, u32[]{:S(2)}) collective-permute-start(bf16[8,96,128]{2,1,0:T(8,128)(2,1)S(1)} %collective-permute-done.7.refs_1_), channel_id=1, source_target_pairs={{0,64},{64,128},{128,192},{192,256},{256,320},{320,384},{384,448},... | collective-permute-start | bytes 589832 | tf_op jit(solution)/shard_map/ppermute | solution.py:201
  63.7 20.8 %all-to-all-start.2 = ((bf16[8,4,48,128]{3,2,1,0:T(8,128)(2,1)}), bf16[8,4,48,128]{3,2,1,0:T(8,128)(2,1)S(1)}, u32[]{:S(2)}, u32[]{:S(2)}) async-start(bf16[8,4,48,128]{3,2,1,0:T(8,128)(2,1)} %get-tuple-element.33), calls=%async_computation.2 | async-start | bytes 786432 | tf_op jit(solution)/shard_map/all_to_all | solution.py:225
  69.7 8.1 %collective-permute-start.9 = (bf16[8,96,128]{2,1,0:T(8,128)(2,1)S(1)}, bf16[8,96,128]{2,1,0:T(8,128)(2,1)}, u32[]{:S(2)}, u32[]{:S(2)}) collective-permute-start(bf16[8,96,128]{2,1,0:T(8,128)(2,1)S(1)} %collective-permute-done.8.refs_3_), channel_id=1, source_target_pairs={{0,64},{64,128},{128,192},{192,256},{256,320},{320,384},{384,448},... | collective-permute-start | bytes 589832 | tf_op jit(solution)/shard_map/ppermute | solution.py:201
  72.9 8.3 %collective-permute-start.5 = (bf16[8,96,128]{2,1,0:T(8,128)(2,1)S(1)}, bf16[8,96,128]{2,1,0:T(8,128)(2,1)}, u32[]{:S(2)}, u32[]{:S(2)}) collective-permute-start(bf16[8,96,128]{2,1,0:T(8,128)(2,1)S(1)} %collective-permute-done.3.refs_2_), channel_id=1, source_target_pairs={{0,448},{64,0},{128,64},{192,128},{256,192},{320,256},{384,320},{4... | collective-permute-start | bytes 589832 | tf_op jit(solution)/shard_map/ppermute | solution.py:201
  77.8 15.1 %collective-permute-start.10 = (bf16[8,96,128]{2,1,0:T(8,128)(2,1)}, bf16[8,96,128]{2,1,0:T(8,128)(2,1)}, u32[]{:S(2)}, u32[]{:S(2)}) collective-permute-start(bf16[8,96,128]{2,1,0:T(8,128)(2,1)} %collective-permute-done.9.refs_5_), channel_id=1, source_target_pairs={{0,64},{64,128},{128,192},{192,256},{256,320},{320,384},{384,448},... | collective-permute-start | bytes 589832 | tf_op jit(solution)/shard_map/ppermute | solution.py:201
  81.2 11.7 %collective-permute-start.6 = (bf16[8,96,128]{2,1,0:T(8,128)(2,1)}, bf16[8,96,128]{2,1,0:T(8,128)(2,1)}, u32[]{:S(2)}, u32[]{:S(2)}) collective-permute-start(bf16[8,96,128]{2,1,0:T(8,128)(2,1)} %collective-permute-done.5.refs_4_), channel_id=1, source_target_pairs={{0,448},{64,0},{128,64},{192,128},{256,192},{320,256},{384,320},{4... | collective-permute-start | bytes 589832 | tf_op jit(solution)/shard_map/ppermute | solution.py:201
  98.7 17.2 %all-to-all-start.3 = ((bf16[8,4,64,128]{3,2,1,0:T(8,128)(2,1)}), bf16[8,4,64,128]{3,2,1,0:T(8,128)(2,1)S(1)}, u32[]{:S(2)}, u32[]{:S(2)}) async-start(bf16[8,4,64,128]{3,2,1,0:T(8,128)(2,1)} %shard_map.88), calls=%async_computation.3 | async-start | bytes 1048576 | tf_op jit(solution)/shard_map/all_to_all | solution.py:225
  106.5 17.5 %collective-permute-start.11 = (bf16[8,48,768]{2,1,0:T(8,128)(2,1)S(1)}, bf16[8,48,768]{2,1,0:T(8,128)(2,1)S(1)}, u32[]{:S(2)}, u32[]{:S(2)}) collective-permute-start(bf16[8,48,768]{2,1,0:T(8,128)(2,1)S(1)} %all-to-all-done.1.w_near_ref), channel_id=1, source_target_pairs={{0,16},{16,0},{1,17},{17,1},{2,18},{18,2},{3,19},{19,3},{4,20},{20... | collective-permute-start | bytes 1769480 | tf_op jit(solution)/shard_map/ppermute | solution.py:201
  117.3 14.6 %all-to-all-start.4 = ((bf16[8,64,128]{2,1,0:T(8,128)(2,1)}), bf16[8,64,128]{2,1,0:T(8,128)(2,1)S(1)}, u32[]{:S(2)}, u32[]{:S(2)}) async-start(bf16[8,64,128]{2,1,0:T(8,128)(2,1)} %shard_map.89), calls=%async_computation.4 | async-start | bytes 262144 | tf_op jit(solution)/shard_map/all_to_all | solution.py:225

commit v7 on v6

--- a/solution.py
+++ b/solution.py
@@ -241,7 +241,7 @@
         norm_kernel,
         [sm, sm, sm, vm, vm, vm],
         [((peers, samples * tok_dev, width), BF16)],
-        pos,
+        first[None],
         chain_id,
         hotspots,
         tokens,
@@ -250,9 +250,10 @@
         mib=56,
     )
     gathered = exchange(copies, "z")
-    weights_other, far_out = lax.optimization_barrier((weights_other, far_out))
+    w_rows = jnp.where(at["core"] == at["xhi"], w_out, weights_other[4 * HD :])
+    w_near = jnp.broadcast_to(w_rows[None], (peers, HD, width))
     far = shift(far_out, "xlo", 1)
-    gathered, far_out = lax.optimization_barrier((gathered, far_out))
+    gathered, far_out, w_near = lax.optimization_barrier((gathered, far_out, w_near))
     q_out, kv_own, kv_other, gate = call(
         proj_kernel,
         [sm, vm, vm, vm],
@@ -267,9 +268,7 @@
         weights,
         weights_other,
     )
-    w_rows = jnp.where(at["core"] == at["xhi"], w_out, weights_other[4 * HD :])
-    w_near = jnp.broadcast_to(w_rows[None], (peers, HD, width))
-    w_near, kv_own = lax.optimization_barrier((w_near, kv_own))
+    w_near, kv_own, kv_other, far = lax.optimization_barrier((w_near, kv_own, kv_other, far))
     w_near = exchange(w_near, "z")
     kv_other = shift(kv_other, "xhi", 1)
     (kv,) = call(join_kernel, [vm, vm], [((samples, 2 * HD, 128), BF16)], kv_own, kv_other)

time: 135 us -> 139 us (1.030)
  waiting for transfers between devices: 32.6 us -> 36.7 us
    all_to_all x5, starting transfers between devices: 35.2 us -> 37.5 us  [exchange(): return lax.all_to_all(x, axes, split_axis=0, concat_axis=0, tiled=True)]
    all_to_all x5, waiting for transfers between devices: 20.5 us -> 22.6 us  [exchange(): return lax.all_to_all(x, axes, split_axis=0, concat_axis=0, tiled=True)]
    ppermute x12, waiting for transfers between devices: 12.1 us -> 14.1 us  [shift(): return lax.ppermute(x, axis, [(i, (i + by) % n) for i in range(n)])]
    ppermute x12, starting transfers between devices: 39.5 us -> 37.4 us  [shift(): return lax.ppermute(x, axis, [(i, (i + by) % n) for i in range(n)])]
  transfers between devices with their start and end apart: 17 -> 17, of which waited for: 6 -> 9; matrix products, arithmetic and copies ran while one was open for 1% -> 1% of each run, Pallas kernels for 9% -> 10%
where the time goes in v7:
time: 139 us; the launch traced here: 138 us
  starting transfers between devices  74.9 us (54%)
  waiting for transfers between devices  36.7 us (26%)
  Pallas kernels  23.2 us (17%)
  local copies, waits for them, and re-layouts  1.64 us (1%)
    all_to_all x5, starting transfers between devices, exchange(): return lax.all_to_all(x, axes, split_axis=0, concat_axis=0, tiled=True)  37.5 us
    ppermute x12, starting transfers between devices, shift(): return lax.ppermute(x, axis, [(i, (i + by) % n) for i in range(n)])  37.4 us
    all_to_all x5, waiting for transfers between devices, exchange(): return lax.all_to_all(x, axes, split_axis=0, concat_axis=0, tiled=True)  22.6 us
    ppermute x12, waiting for transfers between devices, shift(): return lax.ppermute(x, axis, [(i, (i + by) % n) for i in range(n)])  14.1 us
    pallas_call x2, Pallas kernels, attend(): pl.pallas_call(functools.partial(attend_kernel, (tuple((shifts[i] for i i...  13.4 us
    pallas_call x7, Pallas kernels, call(): pl.pallas_call(kernel, out_shape=shapes, in_specs=specs, out_specs=[vm] *...  9.82 us
  transfers between devices with their start and end apart: 17, of which 9 were waited for; matrix products, arithmetic and copies ran while one was open for 1% of the time, Pallas kernels for 10%

profile of v7, /device:TPU:1, one launch (start us, length us, event | category | flops | bytes accessed | tf_op | source)
XLA Modules:
  0.0 137.7 jit_solution(12688849842775036491)
XLA Ops:
  0.0 0.0 copy-start
  0.0 2.3 %shard_map.82 = bf16[8,64,768]{2,1,0:T(8,128)(2,1)} custom-call(s32[1]{0:T(128)} %bitcast.pos_ref, s32[8]{0:T(128)} %chain_ref.1, s32[16]{0:T(128)} %hot_ref.1, bf16[8,8,768]{2,1,0:T(8,128)(2,1)} %tok_ref.1, bf16[4,768]{1,0:T(4,128)(2,1)} %emb_ref.1, bf16[768]{0:T(1024)(128)(2,1)} %hemb_ref.1), custom_call_target="tpu_custom_call" | custom-call | tf_op jit(solution)/shard_map/pallas_call | solution.py:215
  2.3 10.9 %all-to-all-start = ((bf16[8,64,768]{2,1,0:T(8,128)(2,1)}), bf16[8,64,768]{2,1,0:T(8,128)(2,1)S(1)}, u32[]{:S(2)}, u32[]{:S(2)}) async-start(bf16[8,64,768]{2,1,0:T(8,128)(2,1)} %shard_map.82), calls=%async_computation | async-start | bytes 1572864 | tf_op jit(solution)/shard_map/all_to_all | solution.py:225
  13.2 0.1 stack.26.pos_ref
  13.3 0.0 copy-done
  13.3 0.0 copy-start.3
  13.3 0.0 copy-start.4
  13.3 1.8 %shard_map.83 = (bf16[2,8,128,128]{3,2,1,0:T(8,128)(2,1)S(1)}, bf16[2,8,128,128]{3,2,1,0:T(8,128)(2,1)S(1)}) custom-call(s32[5]{0:T(128)S(1)} %stack.26.pos_ref, bf16[1,128,4096]{2,1,0:T(8,128)(2,1)S(1)} %copy-done), custom_call_target="tpu_custom_call" | custom-call | tf_op jit(solution)/shard_map/pallas_call | solution.py:215
  15.1 2.9 %collective-permute-start = (bf16[2,8,128,128]{3,2,1,0:T(8,128)(2,1)S(1)}, bf16[2,8,128,128]{3,2,1,0:T(8,128)(2,1)S(1)}, u32[]{:S(2)}, u32[]{:S(2)}) collective-permute-start(bf16[2,8,128,128]{3,2,1,0:T(8,128)(2,1)S(1)} %get-tuple-element.25), channel_id=1, source_target_pairs={{0,16},{16,0},{1,17},{17,1},{2,18},{18,2},{3,19},{19,3},{4,20},{20... | collective-permute-start | bytes 1572872 | tf_op jit(solution)/shard_map/ppermute | solution.py:201
  18.0 0.0 copy-done.3
  18.0 0.0 copy-done.4
  18.1 4.6 %collective-permute-start.1 = (bf16[240,768]{1,0:T(8,128)(2,1)S(1)}, bf16[240,768]{1,0:T(8,128)(2,1)S(1)}, u32[]{:S(2)}, u32[]{:S(2)}) collective-permute-start(bf16[240,768]{1,0:T(8,128)(2,1)S(1)} %pad_maximum_fusion.1.own_ref), channel_id=1, source_target_pairs={{0,1},{1,0},{2,3},{3,2},{4,5},{5,4},{6,7},{7,6},{8,9},{9,8},{10,11... | collective-permute-start | bytes 1105928 | tf_op jit(solution)/shard_map/ppermute | solution.py:201
  22.7 0.0 collective-permute-done.recv_ref
  22.8 0.9 pad_maximum_fusion
  23.6 2.2 %collective-permute-start.2 = (bf16[2,8,128,128]{3,2,1,0:T(8,128)(2,1)}, bf16[2,8,128,128]{3,2,1,0:T(8,128)(2,1)S(1)}, u32[]{:S(2)}, u32[]{:S(2)}) collective-permute-start(bf16[2,8,128,128]{3,2,1,0:T(8,128)(2,1)} %pad_maximum_fusion), channel_id=1, source_target_pairs={{0,32},{32,0},{1,33},{33,1},{2,34},{34,2},{3,35},{35,3},{4,36},{36... | collective-permute-start | bytes 1572872 | tf_op jit(solution)/shard_map/ppermute | solution.py:201
  25.9 5.8 %collective-permute-done.1.other_ref = bf16[240,768]{1,0:T(8,128)(2,1)S(1)} collective-permute-done((bf16[240,768]{1,0:T(8,128)(2,1)S(1)}, bf16[240,768]{1,0:T(8,128)(2,1)S(1)}, u32[]{:S(2)}, u32[]{:S(2)}) %collective-permute-start.1) | collective-permute-done | bytes 368672 | tf_op jit(solution)/shard_map/ppermute | solution.py:201
  31.7 5.1 %all-to-all-done.x_ref = bf16[8,64,768]{2,1,0:T(8,128)(2,1)S(1)} async-done(((bf16[8,64,768]{2,1,0:T(8,128)(2,1)}), bf16[8,64,768]{2,1,0:T(8,128)(2,1)S(1)}, u32[]{:S(2)}, u32[]{:S(2)}) %all-to-all-start) | async-done | bytes 786464 | tf_op jit(solution)/shard_map/all_to_all | solution.py:225
  36.8 0.9 broadcast_in_dim.2
  37.6 2.2 %shard_map.84 = (bf16[8,4,48,128]{3,2,1,0:T(8,128)(2,1)}, bf16[4,96,128]{2,1,0:T(8,128)(2,1)S(1)}, bf16[4,96,128]{2,1,0:T(8,128)(2,1)S(1)}, f32[2,4,48,128]{3,2,1,0:T(8,128)S(1)}) custom-call(s32[5]{0:T(128)S(1)} %stack.26.pos_ref, bf16[8,64,768]{2,1,0:T(8,128)(2,1)S(1)} %all-to-all-done.x_ref, bf16[240,768]{1,0:T(8,128)(2,1)S(1)} %pad_maximum_fusion.1.own_ref, ...), custom_call_target="tpu_custom_call" | custom-call | tf_op jit(solution)/shard_map/pallas_call | solution.py:215
  39.8 0.0 copy-start.1
  39.8 0.6 copy-done.1
  40.4 2.5 %collective-permute-done.2.far_ref = bf16[2,8,128,128]{3,2,1,0:T(8,128)(2,1)S(1)} collective-permute-done((bf16[2,8,128,128]{3,2,1,0:T(8,128)(2,1)}, bf16[2,8,128,128]{3,2,1,0:T(8,128)(2,1)S(1)}, u32[]{:S(2)}, u32[]{:S(2)}) %collective-permute-start.2) | collective-permute-done | bytes 524320 | tf_op jit(solution)/shard_map/ppermute | solution.py:201
  43.0 0.0 copy-start.2
  43.0 7.1 %all-to-all-start.1 = ((bf16[8,48,768]{2,1,0:T(8,128)(2,1)}), bf16[8,48,768]{2,1,0:T(8,128)(2,1)S(1)}, u32[]{:S(2)}, u32[]{:S(2)}) async-start(bf16[8,48,768]{2,1,0:T(8,128)(2,1)} %broadcast_in_dim.2), calls=%async_computation.1 | async-start | bytes 1179648 | tf_op jit(solution)/shard_map/all_to_all | solution.py:225
  50.0 0.0 copy-done.2
  50.0 3.6 %collective-permute-start.3 = (bf16[4,96,128]{2,1,0:T(8,128)(2,1)S(1)}, bf16[4,96,128]{2,1,0:T(8,128)(2,1)S(1)}, u32[]{:S(2)}, u32[]{:S(2)}) collective-permute-start(bf16[4,96,128]{2,1,0:T(8,128)(2,1)S(1)} %copy-done.2), channel_id=1, source_target_pairs={{0,1},{1,0},{2,3},{3,2},{4,5},{5,4},{6,7},{7,6},{8,9},{9,8},{10,11... | collective-permute-start | bytes 294920 | tf_op jit(solution)/shard_map/ppermute | solution.py:201
  53.7 3.2 %collective-permute-done.3.other_ref = bf16[4,96,128]{2,1,0:T(8,128)(2,1)S(1)} collective-permute-done((bf16[4,96,128]{2,1,0:T(8,128)(2,1)S(1)}, bf16[4,96,128]{2,1,0:T(8,128)(2,1)S(1)}, u32[]{:S(2)}, u32[]{:S(2)}) %collective-permute-start.3) | collective-permute-done | bytes 98336 | tf_op jit(solution)/shard_map/ppermute | solution.py:201
  56.9 0.1 shard_map.85.refs_0_
  57.0 3.2 %collective-permute-start.7 = (bf16[8,96,128]{2,1,0:T(8,128)(2,1)S(1)}, bf16[8,96,128]{2,1,0:T(8,128)(2,1)S(1)}, u32[]{:S(2)}, u32[]{:S(2)}) collective-permute-start(bf16[8,96,128]{2,1,0:T(8,128)(2,1)S(1)} %shard_map.85.refs_0_), channel_id=1, source_target_pairs={{0,64},{64,128},{128,192},{192,256},{256,320},{320,384},{384,448},... | collective-permute-start | bytes 589832 | tf_op jit(solution)/shard_map/ppermute | solution.py:201
  60.2 3.8 %collective-permute-start.4 = (bf16[8,96,128]{2,1,0:T(8,128)(2,1)S(1)}, bf16[8,96,128]{2,1,0:T(8,128)(2,1)S(1)}, u32[]{:S(2)}, u32[]{:S(2)}) collective-permute-start(bf16[8,96,128]{2,1,0:T(8,128)(2,1)S(1)} %shard_map.85.refs_0_), channel_id=1, source_target_pairs={{0,448},{64,0},{128,64},{192,128},{256,192},{320,256},{384,320},{4... | collective-permute-start | bytes 589832 | tf_op jit(solution)/shard_map/ppermute | solution.py:201
  64.1 1.1 collective-permute-done.7.refs_1_
  65.2 1.9 %collective-permute-start.8 = (bf16[8,96,128]{2,1,0:T(8,128)(2,1)S(1)}, bf16[8,96,128]{2,1,0:T(8,128)(2,1)}, u32[]{:S(2)}, u32[]{:S(2)}) collective-permute-start(bf16[8,96,128]{2,1,0:T(8,128)(2,1)S(1)} %collective-permute-done.7.refs_1_), channel_id=1, source_target_pairs={{0,64},{64,128},{128,192},{192,256},{256,320},{320,384},{384,448},... | collective-permute-start | bytes 589832 | tf_op jit(solution)/shard_map/ppermute | solution.py:201
  67.1 0.0 collective-permute-done.4.refs_2_
  67.1 2.3 %all-to-all-done.1.w_near_ref = bf16[8,48,768]{2,1,0:T(8,128)(2,1)S(1)} async-done(((bf16[8,48,768]{2,1,0:T(8,128)(2,1)}), bf16[8,48,768]{2,1,0:T(8,128)(2,1)S(1)}, u32[]{:S(2)}, u32[]{:S(2)}) %all-to-all-start.1) | async-done | bytes 589856 | tf_op jit(solution)/shard_map/all_to_all | solution.py:225
  69.4 4.3 %all-to-all-start.2 = ((bf16[8,4,48,128]{3,2,1,0:T(8,128)(2,1)}), bf16[8,4,48,128]{3,2,1,0:T(8,128)(2,1)S(1)}, u32[]{:S(2)}, u32[]{:S(2)}) async-start(bf16[8,4,48,128]{3,2,1,0:T(8,128)(2,1)} %get-tuple-element.34), calls=%async_computation.2 | async-start | bytes 786432 | tf_op jit(solution)/shard_map/all_to_all | solution.py:225
  73.7 0.0 collective-permute-done.8.refs_3_
  73.7 3.2 %collective-permute-start.9 = (bf16[8,96,128]{2,1,0:T(8,128)(2,1)}, bf16[8,96,128]{2,1,0:T(8,128)(2,1)}, u32[]{:S(2)}, u32[]{:S(2)}) collective-permute-start(bf16[8,96,128]{2,1,0:T(8,128)(2,1)} %collective-permute-done.8.refs_3_), channel_id=1, source_target_pairs={{0,64},{64,128},{128,192},{192,256},{256,320},{320,384},{384,448},... | collective-permute-start | bytes 589832 | tf_op jit(solution)/shard_map/ppermute | solution.py:201
  76.9 3.5 %collective-permute-start.5 = (bf16[8,96,128]{2,1,0:T(8,128)(2,1)S(1)}, bf16[8,96,128]{2,1,0:T(8,128)(2,1)}, u32[]{:S(2)}, u32[]{:S(2)}) collective-permute-start(bf16[8,96,128]{2,1,0:T(8,128)(2,1)S(1)} %collective-permute-done.4.refs_2_), channel_id=1, source_target_pairs={{0,448},{64,0},{128,64},{192,128},{256,192},{320,256},{384,320},{4... | collective-permute-start | bytes 589832 | tf_op jit(solution)/shard_map/ppermute | solution.py:201
  80.4 1.4 %collective-permute-done.9.refs_5_ = bf16[8,96,128]{2,1,0:T(8,128)(2,1)} collective-permute-done((bf16[8,96,128]{2,1,0:T(8,128)(2,1)}, bf16[8,96,128]{2,1,0:T(8,128)(2,1)}, u32[]{:S(2)}, u32[]{:S(2)}) %collective-permute-start.9) | collective-permute-done | bytes 196640 | tf_op jit(solution)/shard_map/ppermute | solution.py:201
  81.8 3.5 %collective-permute-start.10 = (bf16[8,96,128]{2,1,0:T(8,128)(2,1)}, bf16[8,96,128]{2,1,0:T(8,128)(2,1)}, u32[]{:S(2)}, u32[]{:S(2)}) collective-permute-start(bf16[8,96,128]{2,1,0:T(8,128)(2,1)} %collective-permute-done.9.refs_5_), channel_id=1, source_target_pairs={{0,64},{64,128},{128,192},{192,256},{256,320},{320,384},{384,448},... | collective-permute-start | bytes 589832 | tf_op jit(solution)/shard_map/ppermute | solution.py:201
  85.3 0.0 collective-permute-done.5.refs_4_
  85.3 3.0 %collective-permute-start.6 = (bf16[8,96,128]{2,1,0:T(8,128)(2,1)}, bf16[8,96,128]{2,1,0:T(8,128)(2,1)}, u32[]{:S(2)}, u32[]{:S(2)}) collective-permute-start(bf16[8,96,128]{2,1,0:T(8,128)(2,1)} %collective-permute-done.5.refs_4_), channel_id=1, source_target_pairs={{0,448},{64,0},{128,64},{192,128},{256,192},{320,256},{384,320},{4... | collective-permute-start | bytes 589832 | tf_op jit(solution)/shard_map/ppermute | solution.py:201
  88.3 0.0 all-to-all-done.2.q_ref
  88.3 0.7 shard_map.86.q_ref
  89.1 7.6 %shard_map.87 = (f32[8,64,512]{2,1,0:T(8,128)S(1)}, f32[8,8,512]{2,1,0:T(8,128)S(1)}) custom-call(s32[5]{0:T(128)S(1)} %stack.26.pos_ref, bf16[8,48,512]{2,1,0:T(8,128)(2,1)S(1)} %shard_map.86.q_ref, bf16[2,8,128,128]{3,2,1,0:T(8,128)(2,1)S(1)} %get-tuple-element.24.keep_ref, bf16[2,8,128,128]{3,2,1,0:T(8,128)(2,1)S(1)} %collective-permute-done.recv_ref, ...), custom_call_target="tpu_custom_call" | custom-call | flops 6442450944 | bytes 4194304 | tf_op jit(solution)/shard_map/pallas_call | solution.py:299
  96.7 0.0 collective-permute-done.10.refs_1_
  96.7 0.0 collective-permute-done.6.refs_0_
  96.7 5.8 %shard_map.88 = bf16[8,4,64,128]{3,2,1,0:T(8,128)(2,1)} custom-call(s32[5]{0:T(128)S(1)} %stack.26.pos_ref, bf16[8,48,512]{2,1,0:T(8,128)(2,1)S(1)} %shard_map.86.q_ref, bf16[2,8,128,128]{3,2,1,0:T(8,128)(2,1)S(1)} %get-tuple-element.24.keep_ref, bf16[2,8,128,128]{3,2,1,0:T(8,128)(2,1)S(1)} %collective-permute-done.recv_ref, ...), custom_call_target="tpu_custom_call" | custom-call | flops 2147483648 | bytes 4194304 | tf_op jit(solution)/shard_map/pallas_call | solution.py:299
  102.5 8.4 %all-to-all-start.3 = ((bf16[8,4,64,128]{3,2,1,0:T(8,128)(2,1)}), bf16[8,4,64,128]{3,2,1,0:T(8,128)(2,1)S(1)}, u32[]{:S(2)}, u32[]{:S(2)}) async-start(bf16[8,4,64,128]{3,2,1,0:T(8,128)(2,1)} %shard_map.88), calls=%async_computation.3 | async-start | bytes 1048576 | tf_op jit(solution)/shard_map/all_to_all | solution.py:225
  110.9 2.0 %collective-permute-start.11 = (bf16[8,48,768]{2,1,0:T(8,128)(2,1)S(1)}, bf16[8,48,768]{2,1,0:T(8,128)(2,1)S(1)}, u32[]{:S(2)}, u32[]{:S(2)}) collective-permute-start(bf16[8,48,768]{2,1,0:T(8,128)(2,1)S(1)} %all-to-all-done.1.w_near_ref), channel_id=1, source_target_pairs={{0,16},{16,0},{1,17},{17,1},{2,18},{18,2},{3,19},{19,3},{4,20},{20... | collective-permute-start | bytes 1769480 | tf_op jit(solution)/shard_map/ppermute | solution.py:201
  112.9 7.4 %all-to-all-done.3.p_ref = bf16[8,4,64,128]{3,2,1,0:T(8,128)(2,1)S(1)} async-done(((bf16[8,4,64,128]{3,2,1,0:T(8,128)(2,1)}), bf16[8,4,64,128]{3,2,1,0:T(8,128)(2,1)S(1)}, u32[]{:S(2)}, u32[]{:S(2)}) %all-to-all-start.3) | async-done | bytes 524320 | tf_op jit(solution)/shard_map/all_to_all | solution.py:225
  120.3 1.4 %shard_map.89 = bf16[8,64,128]{2,1,0:T(8,128)(2,1)} custom-call(s32[5]{0:T(128)S(1)} %stack.26.pos_ref, bf16[8,4,64,128]{3,2,1,0:T(8,128)(2,1)S(1)} %all-to-all-done.3.p_ref, f32[2,4,48,128]{3,2,1,0:T(8,128)S(1)} %get-tuple-element.41.gate_ref), custom_call_target="tpu_custom_call" | custom-call | tf_op jit(solution)/shard_map/pallas_call | solution.py:215
  121.7 6.9 %all-to-all-start.4 = ((bf16[8,64,128]{2,1,0:T(8,128)(2,1)}), bf16[8,64,128]{2,1,0:T(8,128)(2,1)S(1)}, u32[]{:S(2)}, u32[]{:S(2)}) async-start(bf16[8,64,128]{2,1,0:T(8,128)(2,1)} %shard_map.89), calls=%async_computation.4 | async-start | bytes 262144 | tf_op jit(solution)/shard_map/all_to_all | solution.py:225
  128.6 0.0 collective-permute-done.11.w_far_ref
  128.6 7.9 %all-to-all-done.4.g_ref = bf16[8,64,128]{2,1,0:T(8,128)(2,1)S(1)} async-done(((bf16[8,64,128]{2,1,0:T(8,128)(2,1)}), bf16[8,64,128]{2,1,0:T(8,128)(2,1)S(1)}, u32[]{:S(2)}, u32[]{:S(2)}) %all-to-all-start.4) | async-done | bytes 131104 | tf_op jit(solution)/shard_map/all_to_all | solution.py:225
  136.4 1.3 shard_map.90
  (4 shorter events, 0.1 us)
Async XLA Ops:
  0.0 13.3 %copy-start = (bf16[1,128,4096]{2,1,0:T(8,128)(2,1)S(1)}, bf16[1,128,4096]{2,1,0:T(8,128)(2,1)}, u32[]{:S(2)}) copy-start(bf16[1,128,4096]{2,1,0:T(8,128)(2,1)} %b_ref.1) | copy-start | bytes 3145732
  2.3 34.4 %all-to-all-start = ((bf16[8,64,768]{2,1,0:T(8,128)(2,1)}), bf16[8,64,768]{2,1,0:T(8,128)(2,1)S(1)}, u32[]{:S(2)}, u32[]{:S(2)}) async-start(bf16[8,64,768]{2,1,0:T(8,128)(2,1)} %shard_map.82), calls=%async_computation | async-start | bytes 1572864 | tf_op jit(solution)/shard_map/all_to_all | solution.py:225
  13.3 4.7 %copy-start.3 = (bf16[48,768]{1,0:T(8,128)(2,1)S(1)}, bf16[48,768]{1,0:T(8,128)(2,1)}, u32[]{:S(2)}) copy-start(bf16[48,768]{1,0:T(8,128)(2,1)} %param.15) | copy-start | bytes 221188
  13.3 4.7 %copy-start.4 = (bf16[768,192]{0,1:T(8,128)(2,1)S(1)}, bf16[768,192]{0,1:T(8,128)(2,1)}, u32[]{:S(2)}) copy-start(bf16[768,192]{0,1:T(8,128)(2,1)} %param.13) | copy-start | bytes 884740
  15.1 7.6 %collective-permute-start = (bf16[2,8,128,128]{3,2,1,0:T(8,128)(2,1)S(1)}, bf16[2,8,128,128]{3,2,1,0:T(8,128)(2,1)S(1)}, u32[]{:S(2)}, u32[]{:S(2)}) collective-permute-start(bf16[2,8,128,128]{3,2,1,0:T(8,128)(2,1)S(1)} %get-tuple-element.25), channel_id=1, source_target_pairs={{0,16},{16,0},{1,17},{17,1},{2,18},{18,2},{3,19},{19,3},{4,20},{20... | collective-permute-start | bytes 1572872 | tf_op jit(solution)/shard_map/ppermute | solution.py:201
  18.1 13.6 %collective-permute-start.1 = (bf16[240,768]{1,0:T(8,128)(2,1)S(1)}, bf16[240,768]{1,0:T(8,128)(2,1)S(1)}, u32[]{:S(2)}, u32[]{:S(2)}) collective-permute-start(bf16[240,768]{1,0:T(8,128)(2,1)S(1)} %pad_maximum_fusion.1.own_ref), channel_id=1, source_target_pairs={{0,1},{1,0},{2,3},{3,2},{4,5},{5,4},{6,7},{7,6},{8,9},{9,8},{10,11... | collective-permute-start | bytes 1105928 | tf_op jit(solution)/shard_map/ppermute | solution.py:201
  23.6 19.3 %collective-permute-start.2 = (bf16[2,8,128,128]{3,2,1,0:T(8,128)(2,1)}, bf16[2,8,128,128]{3,2,1,0:T(8,128)(2,1)S(1)}, u32[]{:S(2)}, u32[]{:S(2)}) collective-permute-start(bf16[2,8,128,128]{3,2,1,0:T(8,128)(2,1)} %pad_maximum_fusion), channel_id=1, source_target_pairs={{0,32},{32,0},{1,33},{33,1},{2,34},{34,2},{3,35},{35,3},{4,36},{36... | collective-permute-start | bytes 1572872 | tf_op jit(solution)/shard_map/ppermute | solution.py:201
  39.8 0.6 copy-start.1
  43.0 7.1 %copy-start.2 = (bf16[4,96,128]{2,1,0:T(8,128)(2,1)S(1)}, bf16[4,96,128]{2,1,0:T(8,128)(2,1)}, u32[]{:S(2)}) copy-start(bf16[4,96,128]{2,1,0:T(8,128)(2,1)} %copy-done.1) | copy-start | bytes 294916
  43.0 26.4 %all-to-all-start.1 = ((bf16[8,48,768]{2,1,0:T(8,128)(2,1)}), bf16[8,48,768]{2,1,0:T(8,128)(2,1)S(1)}, u32[]{:S(2)}, u32[]{:S(2)}) async-start(bf16[8,48,768]{2,1,0:T(8,128)(2,1)} %broadcast_in_dim.2), calls=%async_computation.1 | async-start | bytes 1179648 | tf_op jit(solution)/shard_map/all_to_all | solution.py:225
  50.0 6.9 %collective-permute-start.3 = (bf16[4,96,128]{2,1,0:T(8,128)(2,1)S(1)}, bf16[4,96,128]{2,1,0:T(8,128)(2,1)S(1)}, u32[]{:S(2)}, u32[]{:S(2)}) collective-permute-start(bf16[4,96,128]{2,1,0:T(8,128)(2,1)S(1)} %copy-done.2), channel_id=1, source_target_pairs={{0,1},{1,0},{2,3},{3,2},{4,5},{5,4},{6,7},{7,6},{8,9},{9,8},{10,11... | collective-permute-start | bytes 294920 | tf_op jit(solution)/shard_map/ppermute | solution.py:201
  57.0 8.1 %collective-permute-start.7 = (bf16[8,96,128]{2,1,0:T(8,128)(2,1)S(1)}, bf16[8,96,128]{2,1,0:T(8,128)(2,1)S(1)}, u32[]{:S(2)}, u32[]{:S(2)}) collective-permute-start(bf16[8,96,128]{2,1,0:T(8,128)(2,1)S(1)} %shard_map.85.refs_0_), channel_id=1, source_target_pairs={{0,64},{64,128},{128,192},{192,256},{256,320},{320,384},{384,448},... | collective-permute-start | bytes 589832 | tf_op jit(solution)/shard_map/ppermute | solution.py:201
  60.2 6.9 %collective-permute-start.4 = (bf16[8,96,128]{2,1,0:T(8,128)(2,1)S(1)}, bf16[8,96,128]{2,1,0:T(8,128)(2,1)S(1)}, u32[]{:S(2)}, u32[]{:S(2)}) collective-permute-start(bf16[8,96,128]{2,1,0:T(8,128)(2,1)S(1)} %shard_map.85.refs_0_), channel_id=1, source_target_pairs={{0,448},{64,0},{128,64},{192,128},{256,192},{320,256},{384,320},{4... | collective-permute-start | bytes 589832 | tf_op jit(solution)/shard_map/ppermute | solution.py:201
  65.2 8.5 %collective-permute-start.8 = (bf16[8,96,128]{2,1,0:T(8,128)(2,1)S(1)}, bf16[8,96,128]{2,1,0:T(8,128)(2,1)}, u32[]{:S(2)}, u32[]{:S(2)}) collective-permute-start(bf16[8,96,128]{2,1,0:T(8,128)(2,1)S(1)} %collective-permute-done.7.refs_1_), channel_id=1, source_target_pairs={{0,64},{64,128},{128,192},{192,256},{256,320},{320,384},{384,448},... | collective-permute-start | bytes 589832 | tf_op jit(solution)/shard_map/ppermute | solution.py:201
  69.4 18.9 %all-to-all-start.2 = ((bf16[8,4,48,128]{3,2,1,0:T(8,128)(2,1)}), bf16[8,4,48,128]{3,2,1,0:T(8,128)(2,1)S(1)}, u32[]{:S(2)}, u32[]{:S(2)}) async-start(bf16[8,4,48,128]{3,2,1,0:T(8,128)(2,1)} %get-tuple-element.34), calls=%async_computation.2 | async-start | bytes 786432 | tf_op jit(solution)/shard_map/all_to_all | solution.py:225
  73.7 8.1 %collective-permute-start.9 = (bf16[8,96,128]{2,1,0:T(8,128)(2,1)}, bf16[8,96,128]{2,1,0:T(8,128)(2,1)}, u32[]{:S(2)}, u32[]{:S(2)}) collective-permute-start(bf16[8,96,128]{2,1,0:T(8,128)(2,1)} %collective-permute-done.8.refs_3_), channel_id=1, source_target_pairs={{0,64},{64,128},{128,192},{192,256},{256,320},{320,384},{384,448},... | collective-permute-start | bytes 589832 | tf_op jit(solution)/shard_map/ppermute | solution.py:201
  76.9 8.4 %collective-permute-start.5 = (bf16[8,96,128]{2,1,0:T(8,128)(2,1)S(1)}, bf16[8,96,128]{2,1,0:T(8,128)(2,1)}, u32[]{:S(2)}, u32[]{:S(2)}) collective-permute-start(bf16[8,96,128]{2,1,0:T(8,128)(2,1)S(1)} %collective-permute-done.4.refs_2_), channel_id=1, source_target_pairs={{0,448},{64,0},{128,64},{192,128},{256,192},{320,256},{384,320},{4... | collective-permute-start | bytes 589832 | tf_op jit(solution)/shard_map/ppermute | solution.py:201
  81.8 14.9 %collective-permute-start.10 = (bf16[8,96,128]{2,1,0:T(8,128)(2,1)}, bf16[8,96,128]{2,1,0:T(8,128)(2,1)}, u32[]{:S(2)}, u32[]{:S(2)}) collective-permute-start(bf16[8,96,128]{2,1,0:T(8,128)(2,1)} %collective-permute-done.9.refs_5_), channel_id=1, source_target_pairs={{0,64},{64,128},{128,192},{192,256},{256,320},{320,384},{384,448},... | collective-permute-start | bytes 589832 | tf_op jit(solution)/shard_map/ppermute | solution.py:201
  85.3 11.4 %collective-permute-start.6 = (bf16[8,96,128]{2,1,0:T(8,128)(2,1)}, bf16[8,96,128]{2,1,0:T(8,128)(2,1)}, u32[]{:S(2)}, u32[]{:S(2)}) collective-permute-start(bf16[8,96,128]{2,1,0:T(8,128)(2,1)} %collective-permute-done.5.refs_4_), channel_id=1, source_target_pairs={{0,448},{64,0},{128,64},{192,128},{256,192},{320,256},{384,320},{4... | collective-permute-start | bytes 589832 | tf_op jit(solution)/shard_map/ppermute | solution.py:201
  102.5 17.8 %all-to-all-start.3 = ((bf16[8,4,64,128]{3,2,1,0:T(8,128)(2,1)}), bf16[8,4,64,128]{3,2,1,0:T(8,128)(2,1)S(1)}, u32[]{:S(2)}, u32[]{:S(2)}) async-start(bf16[8,4,64,128]{3,2,1,0:T(8,128)(2,1)} %shard_map.88), calls=%async_computation.3 | async-start | bytes 1048576 | tf_op jit(solution)/shard_map/all_to_all | solution.py:225
  110.9 17.7 %collective-permute-start.11 = (bf16[8,48,768]{2,1,0:T(8,128)(2,1)S(1)}, bf16[8,48,768]{2,1,0:T(8,128)(2,1)S(1)}, u32[]{:S(2)}, u32[]{:S(2)}) collective-permute-start(bf16[8,48,768]{2,1,0:T(8,128)(2,1)S(1)} %all-to-all-done.1.w_near_ref), channel_id=1, source_target_pairs={{0,16},{16,0},{1,17},{17,1},{2,18},{18,2},{3,19},{19,3},{4,20},{20... | collective-permute-start | bytes 1769480 | tf_op jit(solution)/shard_map/ppermute | solution.py:201
  121.7 14.8 %all-to-all-start.4 = ((bf16[8,64,128]{2,1,0:T(8,128)(2,1)}), bf16[8,64,128]{2,1,0:T(8,128)(2,1)S(1)}, u32[]{:S(2)}, u32[]{:S(2)}) async-start(bf16[8,64,128]{2,1,0:T(8,128)(2,1)} %shard_map.89), calls=%async_computation.4 | async-start | bytes 262144 | tf_op jit(solution)/shard_map/all_to_all | solution.py:225

commit v8 on v6

--- a/solution.py
+++ b/solution.py
@@ -71,15 +71,21 @@
             away_ref[role, y] = dot(pick_k, rows_ref[at + 1 - core], 1, 1).astype(BF16)
 
 
-def proj_kernel(pos_ref, x_ref, own_ref, other_ref, q_ref, kv_own_ref, kv_other_ref, gate_ref):
+def proj_kernel(pos_ref, x_ref, own_ref, other_ref, q_ref, kv_own_ref, kv_other_ref, gate_ref, w_ref):
     peers, rows, width = x_ref.shape
     pairs = kv_own_ref.shape[0]
     tok = rows // (2 * pairs)
     xhi = pos_ref[3]
     x = x_ref[...].reshape(peers * rows, width)
-    for role, w_ref in enumerate((own_ref, other_ref)):
+    for role, in_ref in enumerate((own_ref, other_ref)):
         kv_ref = (kv_own_ref, kv_other_ref)[role]
-        full = dot(x, w_ref[: 4 * HD], 1, 1).reshape(peers, 2 * pairs, tok, 4 * HD)
+
+        @pl.when(jnp.bitwise_xor(pos_ref[2], xhi) == role)
+        def _():
+            for g in range(peers):
+                w_ref[g] = in_ref[4 * HD :]
+
+        full = dot(x, in_ref[: 4 * HD], 1, 1).reshape(peers, 2 * pairs, tok, 4 * HD)
         for p in range(pairs):
             two = jnp.concatenate([full[:, 2 * p + i].reshape(peers * tok, 4 * HD) for i in range(2)], axis=0)
             turned = jnp.transpose(two)
@@ -241,7 +247,7 @@
         norm_kernel,
         [sm, sm, sm, vm, vm, vm],
         [((peers, samples * tok_dev, width), BF16)],
-        pos,
+        first[None],
         chain_id,
         hotspots,
         tokens,
@@ -253,7 +259,7 @@
     weights_other, far_out = lax.optimization_barrier((weights_other, far_out))
     far = shift(far_out, "xlo", 1)
     gathered, far_out = lax.optimization_barrier((gathered, far_out))
-    q_out, kv_own, kv_other, gate = call(
+    q_out, kv_own, kv_other, gate, w_copies = call(
         proj_kernel,
         [sm, vm, vm, vm],
         [
@@ -261,16 +267,14 @@
             ((pairs, 2 * HD, 128), BF16),
             ((pairs, 2 * HD, 128), BF16),
             ((2, pairs, HD, 128), F32),
+            ((peers, HD, width), BF16),
         ],
         pos,
         gathered,
         weights,
         weights_other,
     )
-    w_rows = jnp.where(at["core"] == at["xhi"], w_out, weights_other[4 * HD :])
-    w_near = jnp.broadcast_to(w_rows[None], (peers, HD, width))
-    w_near, kv_own = lax.optimization_barrier((w_near, kv_own))
-    w_near = exchange(w_near, "z")
+    w_near = exchange(w_copies, "z")
     kv_other = shift(kv_other, "xhi", 1)
     (kv,) = call(join_kernel, [vm, vm], [((samples, 2 * HD, 128), BF16)], kv_own, kv_other)
 

time: 135 us -> 133 us (0.985)
  local copies, waits for them, and re-layouts: 1.6 us -> 0.13 us
where the time goes in v8:
time: 133 us; the launch traced here: 132 us
  starting transfers between devices  74.5 us (56%)
  waiting for transfers between devices  32.5 us (24%)
  Pallas kernels  23.9 us (18%)
    ppermute x12, starting transfers between devices, shift(): return lax.ppermute(x, axis, [(i, (i + by) % n) for i in range(n)])  39.5 us
    all_to_all x5, starting transfers between devices, exchange(): return lax.all_to_all(x, axes, split_axis=0, concat_axis=0, tiled=True)  35 us
    all_to_all x5, waiting for transfers between devices, exchange(): return lax.all_to_all(x, axes, split_axis=0, concat_axis=0, tiled=True)  20.5 us
    pallas_call x2, Pallas kernels, attend(): pl.pallas_call(functools.partial(attend_kernel, (tuple((shifts[i] for i i...  13.4 us
    ppermute x12, waiting for transfers between devices, shift(): return lax.ppermute(x, axis, [(i, (i + by) % n) for i in range(n)])  12 us
    pallas_call x7, Pallas kernels, call(): pl.pallas_call(kernel, out_shape=shapes, in_specs=specs, out_specs=[vm] *...  10.5 us
  transfers between devices with their start and end apart: 17, of which 6 were waited for; matrix products, arithmetic and copies ran while one was open for 1% of the time, Pallas kernels for 9%

profile of v8, /device:TPU:1, one launch (start us, length us, event | category | flops | bytes accessed | tf_op | source)
XLA Modules:
  0.0 132.2 jit_solution(4799453854228376050)
XLA Ops:
  0.0 0.0 copy-start
  0.0 2.3 %shard_map.82 = bf16[8,64,768]{2,1,0:T(8,128)(2,1)} custom-call(s32[1]{0:T(128)} %bitcast.pos_ref, s32[8]{0:T(128)} %chain_ref.1, s32[16]{0:T(128)} %hot_ref.1, bf16[8,8,768]{2,1,0:T(8,128)(2,1)} %tok_ref.1, bf16[4,768]{1,0:T(4,128)(2,1)} %emb_ref.1, bf16[768]{0:T(1024)(128)(2,1)} %hemb_ref.1), custom_call_target="tpu_custom_call" | custom-call | tf_op jit(solution)/shard_map/pallas_call | solution.py:221
  2.3 10.9 %all-to-all-start = ((bf16[8,64,768]{2,1,0:T(8,128)(2,1)}), bf16[8,64,768]{2,1,0:T(8,128)(2,1)S(1)}, u32[]{:S(2)}, u32[]{:S(2)}) async-start(bf16[8,64,768]{2,1,0:T(8,128)(2,1)} %shard_map.82), calls=%async_computation | async-start | bytes 1572864 | tf_op jit(solution)/shard_map/all_to_all | solution.py:231
  13.2 0.1 stack.26.pos_ref
  13.3 0.0 copy-done
  13.3 0.0 copy-start.1
  13.3 0.0 copy-start.2
  13.3 1.8 %shard_map.83 = (bf16[2,8,128,128]{3,2,1,0:T(8,128)(2,1)S(1)}, bf16[2,8,128,128]{3,2,1,0:T(8,128)(2,1)S(1)}) custom-call(s32[5]{0:T(128)S(1)} %stack.26.pos_ref, bf16[1,128,4096]{2,1,0:T(8,128)(2,1)S(1)} %copy-done), custom_call_target="tpu_custom_call" | custom-call | tf_op jit(solution)/shard_map/pallas_call | solution.py:221
  15.1 2.9 %collective-permute-start.1 = (bf16[2,8,128,128]{3,2,1,0:T(8,128)(2,1)S(1)}, bf16[2,8,128,128]{3,2,1,0:T(8,128)(2,1)S(1)}, u32[]{:S(2)}, u32[]{:S(2)}) collective-permute-start(bf16[2,8,128,128]{3,2,1,0:T(8,128)(2,1)S(1)} %get-tuple-element.23), channel_id=1, source_target_pairs={{0,16},{16,0},{1,17},{17,1},{2,18},{18,2},{3,19},{19,3},{4,20},{20... | collective-permute-start | bytes 1572872 | tf_op jit(solution)/shard_map/ppermute | solution.py:207
  18.0 0.0 copy-done.1
  18.0 0.0 copy-done.2
  18.0 4.7 %collective-permute-start = (bf16[240,768]{1,0:T(8,128)(2,1)S(1)}, bf16[240,768]{1,0:T(8,128)(2,1)S(1)}, u32[]{:S(2)}, u32[]{:S(2)}) collective-permute-start(bf16[240,768]{1,0:T(8,128)(2,1)S(1)} %pad_maximum_fusion.1.own_ref), channel_id=1, source_target_pairs={{0,1},{1,0},{2,3},{3,2},{4,5},{5,4},{6,7},{7,6},{8,9},{9,8},{10,11... | collective-permute-start | bytes 1105928 | tf_op jit(solution)/shard_map/ppermute | solution.py:207
  22.7 0.0 collective-permute-done.1.recv_ref
  22.8 0.9 pad_maximum_fusion
  23.6 8.0 %collective-permute-done.other_ref = bf16[240,768]{1,0:T(8,128)(2,1)S(1)} collective-permute-done((bf16[240,768]{1,0:T(8,128)(2,1)S(1)}, bf16[240,768]{1,0:T(8,128)(2,1)S(1)}, u32[]{:S(2)}, u32[]{:S(2)}) %collective-permute-start) | collective-permute-done | bytes 368672 | tf_op jit(solution)/shard_map/ppermute | solution.py:207
  31.6 5.1 %all-to-all-done.x_ref = bf16[8,64,768]{2,1,0:T(8,128)(2,1)S(1)} async-done(((bf16[8,64,768]{2,1,0:T(8,128)(2,1)}), bf16[8,64,768]{2,1,0:T(8,128)(2,1)S(1)}, u32[]{:S(2)}, u32[]{:S(2)}) %all-to-all-start) | async-done | bytes 786464 | tf_op jit(solution)/shard_map/all_to_all | solution.py:231
  36.8 2.8 %shard_map.84 = (bf16[8,4,48,128]{3,2,1,0:T(8,128)(2,1)}, bf16[4,96,128]{2,1,0:T(8,128)(2,1)S(1)}, bf16[4,96,128]{2,1,0:T(8,128)(2,1)S(1)}, f32[2,4,48,128]{3,2,1,0:T(8,128)S(1)}, bf16[8,48,768]{2,1,0:T(8,128)(2,1)}) custom-call(s32[5]{0:T(128)S(1)} %stack.26.pos_ref, bf16[8,64,768]{2,1,0:T(8,128)(2,1)S(1)} %all-to-all-done.x_ref, ...), custom_call_target="tpu_custom_call" | custom-call | tf_op jit(solution)/shard_map/pallas_call | solution.py:221
  39.6 3.5 %all-to-all-start.1 = ((bf16[8,48,768]{2,1,0:T(8,128)(2,1)}), bf16[8,48,768]{2,1,0:T(8,128)(2,1)S(1)}, u32[]{:S(2)}, u32[]{:S(2)}) async-start(bf16[8,48,768]{2,1,0:T(8,128)(2,1)} %get-tuple-element.30), calls=%async_computation.1 | async-start | bytes 1179648 | tf_op jit(solution)/shard_map/all_to_all | solution.py:231
  43.1 4.7 %collective-permute-start.2 = (bf16[4,96,128]{2,1,0:T(8,128)(2,1)S(1)}, bf16[4,96,128]{2,1,0:T(8,128)(2,1)S(1)}, u32[]{:S(2)}, u32[]{:S(2)}) collective-permute-start(bf16[4,96,128]{2,1,0:T(8,128)(2,1)S(1)} %get-tuple-element.28), channel_id=1, source_target_pairs={{0,1},{1,0},{2,3},{3,2},{4,5},{5,4},{6,7},{7,6},{8,9},{9,8},{10,11... | collective-permute-start | bytes 294920 | tf_op jit(solution)/shard_map/ppermute | solution.py:207
  47.8 2.5 %collective-permute-done.2.other_ref = bf16[4,96,128]{2,1,0:T(8,128)(2,1)S(1)} collective-permute-done((bf16[4,96,128]{2,1,0:T(8,128)(2,1)S(1)}, bf16[4,96,128]{2,1,0:T(8,128)(2,1)S(1)}, u32[]{:S(2)}, u32[]{:S(2)}) %collective-permute-start.2) | collective-permute-done | bytes 98336 | tf_op jit(solution)/shard_map/ppermute | solution.py:207
  50.3 0.1 shard_map.85.refs_0_
  50.5 3.2 %collective-permute-start.7 = (bf16[8,96,128]{2,1,0:T(8,128)(2,1)S(1)}, bf16[8,96,128]{2,1,0:T(8,128)(2,1)S(1)}, u32[]{:S(2)}, u32[]{:S(2)}) collective-permute-start(bf16[8,96,128]{2,1,0:T(8,128)(2,1)S(1)} %shard_map.85.refs_0_), channel_id=1, source_target_pairs={{0,64},{64,128},{128,192},{192,256},{256,320},{320,384},{384,448},... | collective-permute-start | bytes 589832 | tf_op jit(solution)/shard_map/ppermute | solution.py:207
  53.7 3.8 %collective-permute-start.3 = (bf16[8,96,128]{2,1,0:T(8,128)(2,1)S(1)}, bf16[8,96,128]{2,1,0:T(8,128)(2,1)S(1)}, u32[]{:S(2)}, u32[]{:S(2)}) collective-permute-start(bf16[8,96,128]{2,1,0:T(8,128)(2,1)S(1)} %shard_map.85.refs_0_), channel_id=1, source_target_pairs={{0,448},{64,0},{128,64},{192,128},{256,192},{320,256},{384,320},{4... | collective-permute-start | bytes 589832 | tf_op jit(solution)/shard_map/ppermute | solution.py:207
  57.5 3.1 %collective-permute-start.4 = (bf16[2,8,128,128]{3,2,1,0:T(8,128)(2,1)}, bf16[2,8,128,128]{3,2,1,0:T(8,128)(2,1)S(1)}, u32[]{:S(2)}, u32[]{:S(2)}) collective-permute-start(bf16[2,8,128,128]{3,2,1,0:T(8,128)(2,1)} %pad_maximum_fusion), channel_id=1, source_target_pairs={{0,32},{32,0},{1,33},{33,1},{2,34},{34,2},{3,35},{35,3},{4,36},{36... | collective-permute-start | bytes 1572872 | tf_op jit(solution)/shard_map/ppermute | solution.py:207
  60.6 0.0 collective-permute-done.7.refs_1_
  60.6 1.9 %collective-permute-start.8 = (bf16[8,96,128]{2,1,0:T(8,128)(2,1)S(1)}, bf16[8,96,128]{2,1,0:T(8,128)(2,1)S(1)}, u32[]{:S(2)}, u32[]{:S(2)}) collective-permute-start(bf16[8,96,128]{2,1,0:T(8,128)(2,1)S(1)} %collective-permute-done.7.refs_1_), channel_id=1, source_target_pairs={{0,64},{64,128},{128,192},{192,256},{256,320},{320,384},{384,448},... | collective-permute-start | bytes 589832 | tf_op jit(solution)/shard_map/ppermute | solution.py:207
  62.6 0.0 collective-permute-done.3.refs_2_
  62.6 0.0 all-to-all-done.1.w_near_ref
  62.6 6.1 %all-to-all-start.2 = ((bf16[8,4,48,128]{3,2,1,0:T(8,128)(2,1)}), bf16[8,4,48,128]{3,2,1,0:T(8,128)(2,1)S(1)}, u32[]{:S(2)}, u32[]{:S(2)}) async-start(bf16[8,4,48,128]{3,2,1,0:T(8,128)(2,1)} %get-tuple-element.31), calls=%async_computation.2 | async-start | bytes 786432 | tf_op jit(solution)/shard_map/all_to_all | solution.py:231
  68.7 0.0 collective-permute-done.8.refs_3_
  68.7 3.2 %collective-permute-start.9 = (bf16[8,96,128]{2,1,0:T(8,128)(2,1)S(1)}, bf16[8,96,128]{2,1,0:T(8,128)(2,1)}, u32[]{:S(2)}, u32[]{:S(2)}) collective-permute-start(bf16[8,96,128]{2,1,0:T(8,128)(2,1)S(1)} %collective-permute-done.8.refs_3_), channel_id=1, source_target_pairs={{0,64},{64,128},{128,192},{192,256},{256,320},{320,384},{384,448},... | collective-permute-start | bytes 589832 | tf_op jit(solution)/shard_map/ppermute | solution.py:207
  71.9 3.5 %collective-permute-start.5 = (bf16[8,96,128]{2,1,0:T(8,128)(2,1)S(1)}, bf16[8,96,128]{2,1,0:T(8,128)(2,1)}, u32[]{:S(2)}, u32[]{:S(2)}) collective-permute-start(bf16[8,96,128]{2,1,0:T(8,128)(2,1)S(1)} %collective-permute-done.3.refs_2_), channel_id=1, source_target_pairs={{0,448},{64,0},{128,64},{192,128},{256,192},{320,256},{384,320},{4... | collective-permute-start | bytes 589832 | tf_op jit(solution)/shard_map/ppermute | solution.py:207
  75.4 1.4 %collective-permute-done.9.refs_5_ = bf16[8,96,128]{2,1,0:T(8,128)(2,1)} collective-permute-done((bf16[8,96,128]{2,1,0:T(8,128)(2,1)S(1)}, bf16[8,96,128]{2,1,0:T(8,128)(2,1)}, u32[]{:S(2)}, u32[]{:S(2)}) %collective-permute-start.9) | collective-permute-done | bytes 196640 | tf_op jit(solution)/shard_map/ppermute | solution.py:207
  76.8 3.4 %collective-permute-start.10 = (bf16[8,96,128]{2,1,0:T(8,128)(2,1)}, bf16[8,96,128]{2,1,0:T(8,128)(2,1)}, u32[]{:S(2)}, u32[]{:S(2)}) collective-permute-start(bf16[8,96,128]{2,1,0:T(8,128)(2,1)} %collective-permute-done.9.refs_5_), channel_id=1, source_target_pairs={{0,64},{64,128},{128,192},{192,256},{256,320},{320,384},{384,448},... | collective-permute-start | bytes 589832 | tf_op jit(solution)/shard_map/ppermute | solution.py:207
  80.2 0.0 collective-permute-done.5.refs_4_
  80.2 3.3 %collective-permute-start.6 = (bf16[8,96,128]{2,1,0:T(8,128)(2,1)}, bf16[8,96,128]{2,1,0:T(8,128)(2,1)}, u32[]{:S(2)}, u32[]{:S(2)}) collective-permute-start(bf16[8,96,128]{2,1,0:T(8,128)(2,1)} %collective-permute-done.5.refs_4_), channel_id=1, source_target_pairs={{0,448},{64,0},{128,64},{192,128},{256,192},{320,256},{384,320},{4... | collective-permute-start | bytes 589832 | tf_op jit(solution)/shard_map/ppermute | solution.py:207
  83.5 0.0 all-to-all-done.2.q_ref
  83.5 0.7 shard_map.86.q_ref
  84.2 0.0 collective-permute-done.4.far_ref
  84.2 7.6 %shard_map.87 = (f32[8,64,512]{2,1,0:T(8,128)S(1)}, f32[8,8,512]{2,1,0:T(8,128)S(1)}) custom-call(s32[5]{0:T(128)S(1)} %stack.26.pos_ref, bf16[8,48,512]{2,1,0:T(8,128)(2,1)S(1)} %shard_map.86.q_ref, bf16[2,8,128,128]{3,2,1,0:T(8,128)(2,1)S(1)} %get-tuple-element.22.keep_ref, bf16[2,8,128,128]{3,2,1,0:T(8,128)(2,1)S(1)} %collective-permute-done.1.recv_ref, ...), custom_call_target="tpu_custom_call" | custom-call | flops 6442450944 | bytes 4194304 | tf_op jit(solution)/shard_map/pallas_call | solution.py:304
  91.9 0.0 collective-permute-done.10.refs_1_
  91.9 0.0 collective-permute-done.6.refs_0_
  91.9 5.7 %shard_map.88 = bf16[8,4,64,128]{3,2,1,0:T(8,128)(2,1)} custom-call(s32[5]{0:T(128)S(1)} %stack.26.pos_ref, bf16[8,48,512]{2,1,0:T(8,128)(2,1)S(1)} %shard_map.86.q_ref, bf16[2,8,128,128]{3,2,1,0:T(8,128)(2,1)S(1)} %get-tuple-element.22.keep_ref, bf16[2,8,128,128]{3,2,1,0:T(8,128)(2,1)S(1)} %collective-permute-done.1.recv_ref, ...), custom_call_target="tpu_custom_call" | custom-call | flops 2147483648 | bytes 4194304 | tf_op jit(solution)/shard_map/pallas_call | solution.py:304
  97.7 7.8 %all-to-all-start.3 = ((bf16[8,4,64,128]{3,2,1,0:T(8,128)(2,1)}), bf16[8,4,64,128]{3,2,1,0:T(8,128)(2,1)S(1)}, u32[]{:S(2)}, u32[]{:S(2)}) async-start(bf16[8,4,64,128]{3,2,1,0:T(8,128)(2,1)} %shard_map.88), calls=%async_computation.3 | async-start | bytes 1048576 | tf_op jit(solution)/shard_map/all_to_all | solution.py:231
  105.5 1.9 %collective-permute-start.11 = (bf16[8,48,768]{2,1,0:T(8,128)(2,1)S(1)}, bf16[8,48,768]{2,1,0:T(8,128)(2,1)S(1)}, u32[]{:S(2)}, u32[]{:S(2)}) collective-permute-start(bf16[8,48,768]{2,1,0:T(8,128)(2,1)S(1)} %all-to-all-done.1.w_near_ref), channel_id=1, source_target_pairs={{0,16},{16,0},{1,17},{17,1},{2,18},{18,2},{3,19},{19,3},{4,20},{20... | collective-permute-start | bytes 1769480 | tf_op jit(solution)/shard_map/ppermute | solution.py:207
  107.4 7.5 %all-to-all-done.3.p_ref = bf16[8,4,64,128]{3,2,1,0:T(8,128)(2,1)S(1)} async-done(((bf16[8,4,64,128]{3,2,1,0:T(8,128)(2,1)}), bf16[8,4,64,128]{3,2,1,0:T(8,128)(2,1)S(1)}, u32[]{:S(2)}, u32[]{:S(2)}) %all-to-all-start.3) | async-done | bytes 524320 | tf_op jit(solution)/shard_map/all_to_all | solution.py:231
  114.9 1.4 %shard_map.89 = bf16[8,64,128]{2,1,0:T(8,128)(2,1)} custom-call(s32[5]{0:T(128)S(1)} %stack.26.pos_ref, bf16[8,4,64,128]{3,2,1,0:T(8,128)(2,1)S(1)} %all-to-all-done.3.p_ref, f32[2,4,48,128]{3,2,1,0:T(8,128)S(1)} %get-tuple-element.37.gate_ref), custom_call_target="tpu_custom_call" | custom-call | tf_op jit(solution)/shard_map/pallas_call | solution.py:221
  116.3 6.7 %all-to-all-start.4 = ((bf16[8,64,128]{2,1,0:T(8,128)(2,1)}), bf16[8,64,128]{2,1,0:T(8,128)(2,1)S(1)}, u32[]{:S(2)}, u32[]{:S(2)}) async-start(bf16[8,64,128]{2,1,0:T(8,128)(2,1)} %shard_map.89), calls=%async_computation.4 | async-start | bytes 262144 | tf_op jit(solution)/shard_map/all_to_all | solution.py:231
  123.0 0.0 collective-permute-done.11.w_far_ref
  123.0 7.9 %all-to-all-done.4.g_ref = bf16[8,64,128]{2,1,0:T(8,128)(2,1)S(1)} async-done(((bf16[8,64,128]{2,1,0:T(8,128)(2,1)}), bf16[8,64,128]{2,1,0:T(8,128)(2,1)S(1)}, u32[]{:S(2)}, u32[]{:S(2)}) %all-to-all-start.4) | async-done | bytes 131104 | tf_op jit(solution)/shard_map/all_to_all | solution.py:231
  130.9 1.3 shard_map.90
  (3 shorter events, 0.1 us)
Async XLA Ops:
  0.0 13.3 %copy-start = (bf16[1,128,4096]{2,1,0:T(8,128)(2,1)S(1)}, bf16[1,128,4096]{2,1,0:T(8,128)(2,1)}, u32[]{:S(2)}) copy-start(bf16[1,128,4096]{2,1,0:T(8,128)(2,1)} %b_ref.1) | copy-start | bytes 3145732
  2.3 34.4 %all-to-all-start = ((bf16[8,64,768]{2,1,0:T(8,128)(2,1)}), bf16[8,64,768]{2,1,0:T(8,128)(2,1)S(1)}, u32[]{:S(2)}, u32[]{:S(2)}) async-start(bf16[8,64,768]{2,1,0:T(8,128)(2,1)} %shard_map.82), calls=%async_computation | async-start | bytes 1572864 | tf_op jit(solution)/shard_map/all_to_all | solution.py:231
  13.3 4.7 %copy-start.1 = (bf16[768,192]{0,1:T(8,128)(2,1)S(1)}, bf16[768,192]{0,1:T(8,128)(2,1)}, u32[]{:S(2)}) copy-start(bf16[768,192]{0,1:T(8,128)(2,1)} %param.13) | copy-start | bytes 884740
  13.3 4.7 %copy-start.2 = (bf16[48,768]{1,0:T(8,128)(2,1)S(1)}, bf16[48,768]{1,0:T(8,128)(2,1)}, u32[]{:S(2)}) copy-start(bf16[48,768]{1,0:T(8,128)(2,1)} %param.15) | copy-start | bytes 221188
  15.1 7.6 %collective-permute-start.1 = (bf16[2,8,128,128]{3,2,1,0:T(8,128)(2,1)S(1)}, bf16[2,8,128,128]{3,2,1,0:T(8,128)(2,1)S(1)}, u32[]{:S(2)}, u32[]{:S(2)}) collective-permute-start(bf16[2,8,128,128]{3,2,1,0:T(8,128)(2,1)S(1)} %get-tuple-element.23), channel_id=1, source_target_pairs={{0,16},{16,0},{1,17},{17,1},{2,18},{18,2},{3,19},{19,3},{4,20},{20... | collective-permute-start | bytes 1572872 | tf_op jit(solution)/shard_map/ppermute | solution.py:207
  18.0 13.6 %collective-permute-start = (bf16[240,768]{1,0:T(8,128)(2,1)S(1)}, bf16[240,768]{1,0:T(8,128)(2,1)S(1)}, u32[]{:S(2)}, u32[]{:S(2)}) collective-permute-start(bf16[240,768]{1,0:T(8,128)(2,1)S(1)} %pad_maximum_fusion.1.own_ref), channel_id=1, source_target_pairs={{0,1},{1,0},{2,3},{3,2},{4,5},{5,4},{6,7},{7,6},{8,9},{9,8},{10,11... | collective-permute-start | bytes 1105928 | tf_op jit(solution)/shard_map/ppermute | solution.py:207
  39.6 23.0 %all-to-all-start.1 = ((bf16[8,48,768]{2,1,0:T(8,128)(2,1)}), bf16[8,48,768]{2,1,0:T(8,128)(2,1)S(1)}, u32[]{:S(2)}, u32[]{:S(2)}) async-start(bf16[8,48,768]{2,1,0:T(8,128)(2,1)} %get-tuple-element.30), calls=%async_computation.1 | async-start | bytes 1179648 | tf_op jit(solution)/shard_map/all_to_all | solution.py:231
  43.1 7.2 %collective-permute-start.2 = (bf16[4,96,128]{2,1,0:T(8,128)(2,1)S(1)}, bf16[4,96,128]{2,1,0:T(8,128)(2,1)S(1)}, u32[]{:S(2)}, u32[]{:S(2)}) collective-permute-start(bf16[4,96,128]{2,1,0:T(8,128)(2,1)S(1)} %get-tuple-element.28), channel_id=1, source_target_pairs={{0,1},{1,0},{2,3},{3,2},{4,5},{5,4},{6,7},{7,6},{8,9},{9,8},{10,11... | collective-permute-start | bytes 294920 | tf_op jit(solution)/shard_map/ppermute | solution.py:207
  50.5 10.2 %collective-permute-start.7 = (bf16[8,96,128]{2,1,0:T(8,128)(2,1)S(1)}, bf16[8,96,128]{2,1,0:T(8,128)(2,1)S(1)}, u32[]{:S(2)}, u32[]{:S(2)}) collective-permute-start(bf16[8,96,128]{2,1,0:T(8,128)(2,1)S(1)} %shard_map.85.refs_0_), channel_id=1, source_target_pairs={{0,64},{64,128},{128,192},{192,256},{256,320},{320,384},{384,448},... | collective-permute-start | bytes 589832 | tf_op jit(solution)/shard_map/ppermute | solution.py:207
  53.7 8.9 %collective-permute-start.3 = (bf16[8,96,128]{2,1,0:T(8,128)(2,1)S(1)}, bf16[8,96,128]{2,1,0:T(8,128)(2,1)S(1)}, u32[]{:S(2)}, u32[]{:S(2)}) collective-permute-start(bf16[8,96,128]{2,1,0:T(8,128)(2,1)S(1)} %shard_map.85.refs_0_), channel_id=1, source_target_pairs={{0,448},{64,0},{128,64},{192,128},{256,192},{320,256},{384,320},{4... | collective-permute-start | bytes 589832 | tf_op jit(solution)/shard_map/ppermute | solution.py:207
  57.5 26.7 %collective-permute-start.4 = (bf16[2,8,128,128]{3,2,1,0:T(8,128)(2,1)}, bf16[2,8,128,128]{3,2,1,0:T(8,128)(2,1)S(1)}, u32[]{:S(2)}, u32[]{:S(2)}) collective-permute-start(bf16[2,8,128,128]{3,2,1,0:T(8,128)(2,1)} %pad_maximum_fusion), channel_id=1, source_target_pairs={{0,32},{32,0},{1,33},{33,1},{2,34},{34,2},{3,35},{35,3},{4,36},{36... | collective-permute-start | bytes 1572872 | tf_op jit(solution)/shard_map/ppermute | solution.py:207
  60.6 8.1 %collective-permute-start.8 = (bf16[8,96,128]{2,1,0:T(8,128)(2,1)S(1)}, bf16[8,96,128]{2,1,0:T(8,128)(2,1)S(1)}, u32[]{:S(2)}, u32[]{:S(2)}) collective-permute-start(bf16[8,96,128]{2,1,0:T(8,128)(2,1)S(1)} %collective-permute-done.7.refs_1_), channel_id=1, source_target_pairs={{0,64},{64,128},{128,192},{192,256},{256,320},{320,384},{384,448},... | collective-permute-start | bytes 589832 | tf_op jit(solution)/shard_map/ppermute | solution.py:207
  62.6 20.9 %all-to-all-start.2 = ((bf16[8,4,48,128]{3,2,1,0:T(8,128)(2,1)}), bf16[8,4,48,128]{3,2,1,0:T(8,128)(2,1)S(1)}, u32[]{:S(2)}, u32[]{:S(2)}) async-start(bf16[8,4,48,128]{3,2,1,0:T(8,128)(2,1)} %get-tuple-element.31), calls=%async_computation.2 | async-start | bytes 786432 | tf_op jit(solution)/shard_map/all_to_all | solution.py:231
  68.7 8.1 %collective-permute-start.9 = (bf16[8,96,128]{2,1,0:T(8,128)(2,1)S(1)}, bf16[8,96,128]{2,1,0:T(8,128)(2,1)}, u32[]{:S(2)}, u32[]{:S(2)}) collective-permute-start(bf16[8,96,128]{2,1,0:T(8,128)(2,1)S(1)} %collective-permute-done.8.refs_3_), channel_id=1, source_target_pairs={{0,64},{64,128},{128,192},{192,256},{256,320},{320,384},{384,448},... | collective-permute-start | bytes 589832 | tf_op jit(solution)/shard_map/ppermute | solution.py:207
  71.9 8.3 %collective-permute-start.5 = (bf16[8,96,128]{2,1,0:T(8,128)(2,1)S(1)}, bf16[8,96,128]{2,1,0:T(8,128)(2,1)}, u32[]{:S(2)}, u32[]{:S(2)}) collective-permute-start(bf16[8,96,128]{2,1,0:T(8,128)(2,1)S(1)} %collective-permute-done.3.refs_2_), channel_id=1, source_target_pairs={{0,448},{64,0},{128,64},{192,128},{256,192},{320,256},{384,320},{4... | collective-permute-start | bytes 589832 | tf_op jit(solution)/shard_map/ppermute | solution.py:207
  76.8 15.1 %collective-permute-start.10 = (bf16[8,96,128]{2,1,0:T(8,128)(2,1)}, bf16[8,96,128]{2,1,0:T(8,128)(2,1)}, u32[]{:S(2)}, u32[]{:S(2)}) collective-permute-start(bf16[8,96,128]{2,1,0:T(8,128)(2,1)} %collective-permute-done.9.refs_5_), channel_id=1, source_target_pairs={{0,64},{64,128},{128,192},{192,256},{256,320},{320,384},{384,448},... | collective-permute-start | bytes 589832 | tf_op jit(solution)/shard_map/ppermute | solution.py:207
  80.2 11.7 %collective-permute-start.6 = (bf16[8,96,128]{2,1,0:T(8,128)(2,1)}, bf16[8,96,128]{2,1,0:T(8,128)(2,1)}, u32[]{:S(2)}, u32[]{:S(2)}) collective-permute-start(bf16[8,96,128]{2,1,0:T(8,128)(2,1)} %collective-permute-done.5.refs_4_), channel_id=1, source_target_pairs={{0,448},{64,0},{128,64},{192,128},{256,192},{320,256},{384,320},{4... | collective-permute-start | bytes 589832 | tf_op jit(solution)/shard_map/ppermute | solution.py:207
  97.7 17.2 %all-to-all-start.3 = ((bf16[8,4,64,128]{3,2,1,0:T(8,128)(2,1)}), bf16[8,4,64,128]{3,2,1,0:T(8,128)(2,1)S(1)}, u32[]{:S(2)}, u32[]{:S(2)}) async-start(bf16[8,4,64,128]{3,2,1,0:T(8,128)(2,1)} %shard_map.88), calls=%async_computation.3 | async-start | bytes 1048576 | tf_op jit(solution)/shard_map/all_to_all | solution.py:231
  105.5 17.5 %collective-permute-start.11 = (bf16[8,48,768]{2,1,0:T(8,128)(2,1)S(1)}, bf16[8,48,768]{2,1,0:T(8,128)(2,1)S(1)}, u32[]{:S(2)}, u32[]{:S(2)}) collective-permute-start(bf16[8,48,768]{2,1,0:T(8,128)(2,1)S(1)} %all-to-all-done.1.w_near_ref), channel_id=1, source_target_pairs={{0,16},{16,0},{1,17},{17,1},{2,18},{18,2},{3,19},{19,3},{4,20},{20... | collective-permute-start | bytes 1769480 | tf_op jit(solution)/shard_map/ppermute | solution.py:207
  116.3 14.6 %all-to-all-start.4 = ((bf16[8,64,128]{2,1,0:T(8,128)(2,1)}), bf16[8,64,128]{2,1,0:T(8,128)(2,1)S(1)}, u32[]{:S(2)}, u32[]{:S(2)}) async-start(bf16[8,64,128]{2,1,0:T(8,128)(2,1)} %shard_map.89), calls=%async_computation.4 | async-start | bytes 262144 | tf_op jit(solution)/shard_map/all_to_all | solution.py:231

commit v9 on v8

--- a/solution.py
+++ b/solution.py
@@ -274,7 +274,6 @@
         weights,
         weights_other,
     )
-    w_near = exchange(w_copies, "z")
     kv_other = shift(kv_other, "xhi", 1)
     (kv,) = call(join_kernel, [vm, vm], [((samples, 2 * HD, 128), BF16)], kv_own, kv_other)
 
@@ -286,10 +285,12 @@
         if step < 4:
             left = shift(left, "y", -1)
             if step == 1:
-                left, q_out, w_near = lax.optimization_barrier((left, q_out, w_near))
+                left, q_out = lax.optimization_barrier((left, q_out))
             ring.append(left)
             shifts.append(step)
     q_in = exchange(q_out, OCT)
+    w_copies, q_in = lax.optimization_barrier((w_copies, q_in))
+    w_near = exchange(w_copies, "z")
     (q_all,) = call(join_q_kernel, [sm, vm], [((samples, HD, 512), BF16)], pos, q_in)
 
     def two(*dims):

time: 133 us -> 135 us (1.015)
  waiting for transfers between devices: 32.5 us -> 36 us
  Pallas kernels: 23.9 us -> 22.2 us
    all_to_all x5, starting transfers between devices: 35 us -> 32.7 us  [exchange(): return lax.all_to_all(x, axes, split_axis=0, concat_axis=0, tiled=True)]
    all_to_all x5, waiting for transfers between devices: 20.5 us -> 22.8 us  [exchange(): return lax.all_to_all(x, axes, split_axis=0, concat_axis=0, tiled=True)]
    ppermute x12, starting transfers between devices: 39.5 us -> 41.2 us  [shift(): return lax.ppermute(x, axis, [(i, (i + by) % n) for i in range(n)])]
    pallas_call x2, Pallas kernels: 13.4 us -> 11.8 us  [attend(): pl.pallas_call(functools.partial(attend_kernel, (tuple((shifts[i] for i i...]
  transfers between devices with their start and end apart: 17 -> 17, of which waited for: 6 -> 8; matrix products, arithmetic and copies ran while one was open for 1% -> 1% of each run, Pallas kernels for 9% -> 12%
where the time goes in v9:
time: 135 us; the launch traced here: 133 us
  starting transfers between devices  73.9 us (55%)
  waiting for transfers between devices  36 us (27%)
  Pallas kernels  22.2 us (16%)
    ppermute x12, starting transfers between devices, shift(): return lax.ppermute(x, axis, [(i, (i + by) % n) for i in range(n)])  41.2 us
    all_to_all x5, starting transfers between devices, exchange(): return lax.all_to_all(x, axes, split_axis=0, concat_axis=0, tiled=True)  32.7 us
    all_to_all x5, waiting for transfers between devices, exchange(): return lax.all_to_all(x, axes, split_axis=0, concat_axis=0, tiled=True)  22.8 us
    ppermute x12, waiting for transfers between devices, shift(): return lax.ppermute(x, axis, [(i, (i + by) % n) for i in range(n)])  13.2 us
    pallas_call x2, Pallas kernels, attend(): pl.pallas_call(functools.partial(attend_kernel, (tuple((shifts[i] for i i...  11.8 us
    pallas_call x7, Pallas kernels, call(): pl.pallas_call(kernel, out_shape=shapes, in_specs=specs, out_specs=[vm] *...  10.5 us
  transfers between devices with their start and end apart: 17, of which 8 were waited for; matrix products, arithmetic and copies ran while one was open for 1% of the time, Pallas kernels for 12%

profile of v9, /device:TPU:1, one launch (start us, length us, event | category | flops | bytes accessed | tf_op | source)
XLA Modules:
  0.0 133.4 jit_solution(5530956286832519644)
XLA Ops:
  0.0 0.0 copy-start
  0.0 2.3 %shard_map.82 = bf16[8,64,768]{2,1,0:T(8,128)(2,1)} custom-call(s32[1]{0:T(128)} %bitcast.pos_ref, s32[8]{0:T(128)} %chain_ref.1, s32[16]{0:T(128)} %hot_ref.1, bf16[8,8,768]{2,1,0:T(8,128)(2,1)} %tok_ref.1, bf16[4,768]{1,0:T(4,128)(2,1)} %emb_ref.1, bf16[768]{0:T(1024)(128)(2,1)} %hemb_ref.1), custom_call_target="tpu_custom_call" | custom-call | tf_op jit(solution)/shard_map/pallas_call | solution.py:221
  2.3 10.9 %all-to-all-start = ((bf16[8,64,768]{2,1,0:T(8,128)(2,1)}), bf16[8,64,768]{2,1,0:T(8,128)(2,1)S(1)}, u32[]{:S(2)}, u32[]{:S(2)}) async-start(bf16[8,64,768]{2,1,0:T(8,128)(2,1)} %shard_map.82), calls=%async_computation | async-start | bytes 1572864 | tf_op jit(solution)/shard_map/all_to_all | solution.py:231
  13.2 0.1 stack.26.pos_ref
  13.3 0.0 copy-done
  13.3 0.0 copy-start.1
  13.3 0.0 copy-start.2
  13.3 1.8 %shard_map.83 = (bf16[2,8,128,128]{3,2,1,0:T(8,128)(2,1)S(1)}, bf16[2,8,128,128]{3,2,1,0:T(8,128)(2,1)S(1)}) custom-call(s32[5]{0:T(128)S(1)} %stack.26.pos_ref, bf16[1,128,4096]{2,1,0:T(8,128)(2,1)S(1)} %copy-done), custom_call_target="tpu_custom_call" | custom-call | tf_op jit(solution)/shard_map/pallas_call | solution.py:221
  15.1 2.9 %collective-permute-start.1 = (bf16[2,8,128,128]{3,2,1,0:T(8,128)(2,1)S(1)}, bf16[2,8,128,128]{3,2,1,0:T(8,128)(2,1)S(1)}, u32[]{:S(2)}, u32[]{:S(2)}) collective-permute-start(bf16[2,8,128,128]{3,2,1,0:T(8,128)(2,1)S(1)} %get-tuple-element.24), channel_id=1, source_target_pairs={{0,16},{16,0},{1,17},{17,1},{2,18},{18,2},{3,19},{19,3},{4,20},{20... | collective-permute-start | bytes 1572872 | tf_op jit(solution)/shard_map/ppermute | solution.py:207
  18.0 0.0 copy-done.1
  18.0 0.0 copy-done.2
  18.0 4.7 %collective-permute-start = (bf16[240,768]{1,0:T(8,128)(2,1)S(1)}, bf16[240,768]{1,0:T(8,128)(2,1)S(1)}, u32[]{:S(2)}, u32[]{:S(2)}) collective-permute-start(bf16[240,768]{1,0:T(8,128)(2,1)S(1)} %pad_maximum_fusion.1.own_ref), channel_id=1, source_target_pairs={{0,1},{1,0},{2,3},{3,2},{4,5},{5,4},{6,7},{7,6},{8,9},{9,8},{10,11... | collective-permute-start | bytes 1105928 | tf_op jit(solution)/shard_map/ppermute | solution.py:207
  22.7 0.0 collective-permute-done.1.recv_ref
  22.8 0.9 pad_maximum_fusion
  23.6 8.0 %collective-permute-done.other_ref = bf16[240,768]{1,0:T(8,128)(2,1)S(1)} collective-permute-done((bf16[240,768]{1,0:T(8,128)(2,1)S(1)}, bf16[240,768]{1,0:T(8,128)(2,1)S(1)}, u32[]{:S(2)}, u32[]{:S(2)}) %collective-permute-start) | collective-permute-done | bytes 368672 | tf_op jit(solution)/shard_map/ppermute | solution.py:207
  31.6 5.1 %all-to-all-done.x_ref = bf16[8,64,768]{2,1,0:T(8,128)(2,1)S(1)} async-done(((bf16[8,64,768]{2,1,0:T(8,128)(2,1)}), bf16[8,64,768]{2,1,0:T(8,128)(2,1)S(1)}, u32[]{:S(2)}, u32[]{:S(2)}) %all-to-all-start) | async-done | bytes 786464 | tf_op jit(solution)/shard_map/all_to_all | solution.py:231
  36.8 2.8 %shard_map.84 = (bf16[8,4,48,128]{3,2,1,0:T(8,128)(2,1)}, bf16[4,96,128]{2,1,0:T(8,128)(2,1)S(1)}, bf16[4,96,128]{2,1,0:T(8,128)(2,1)S(1)}, f32[2,4,48,128]{3,2,1,0:T(8,128)S(1)}, bf16[8,48,768]{2,1,0:T(8,128)(2,1)}) custom-call(s32[5]{0:T(128)S(1)} %stack.26.pos_ref, bf16[8,64,768]{2,1,0:T(8,128)(2,1)S(1)} %all-to-all-done.x_ref, ...), custom_call_target="tpu_custom_call" | custom-call | tf_op jit(solution)/shard_map/pallas_call | solution.py:221
  39.6 4.7 %collective-permute-start.2 = (bf16[4,96,128]{2,1,0:T(8,128)(2,1)S(1)}, bf16[4,96,128]{2,1,0:T(8,128)(2,1)S(1)}, u32[]{:S(2)}, u32[]{:S(2)}) collective-permute-start(bf16[4,96,128]{2,1,0:T(8,128)(2,1)S(1)} %get-tuple-element.30), channel_id=1, source_target_pairs={{0,1},{1,0},{2,3},{3,2},{4,5},{5,4},{6,7},{7,6},{8,9},{9,8},{10,11... | collective-permute-start | bytes 294920 | tf_op jit(solution)/shard_map/ppermute | solution.py:207
  44.3 2.5 %collective-permute-done.2.other_ref = bf16[4,96,128]{2,1,0:T(8,128)(2,1)S(1)} collective-permute-done((bf16[4,96,128]{2,1,0:T(8,128)(2,1)S(1)}, bf16[4,96,128]{2,1,0:T(8,128)(2,1)S(1)}, u32[]{:S(2)}, u32[]{:S(2)}) %collective-permute-start.2) | collective-permute-done | bytes 98336 | tf_op jit(solution)/shard_map/ppermute | solution.py:207
  46.8 0.1 shard_map.85.refs_0_
  46.9 5.1 %collective-permute-start.3 = (bf16[8,96,128]{2,1,0:T(8,128)(2,1)S(1)}, bf16[8,96,128]{2,1,0:T(8,128)(2,1)S(1)}, u32[]{:S(2)}, u32[]{:S(2)}) collective-permute-start(bf16[8,96,128]{2,1,0:T(8,128)(2,1)S(1)} %shard_map.85.refs_0_), channel_id=1, source_target_pairs={{0,448},{64,0},{128,64},{192,128},{256,192},{320,256},{384,320},{4... | collective-permute-start | bytes 589832 | tf_op jit(solution)/shard_map/ppermute | solution.py:207
  52.0 1.9 %collective-permute-start.7 = (bf16[8,96,128]{2,1,0:T(8,128)(2,1)S(1)}, bf16[8,96,128]{2,1,0:T(8,128)(2,1)S(1)}, u32[]{:S(2)}, u32[]{:S(2)}) collective-permute-start(bf16[8,96,128]{2,1,0:T(8,128)(2,1)S(1)} %shard_map.85.refs_0_), channel_id=1, source_target_pairs={{0,64},{64,128},{128,192},{192,256},{256,320},{320,384},{384,448},... | collective-permute-start | bytes 589832 | tf_op jit(solution)/shard_map/ppermute | solution.py:207
  53.9 0.7 collective-permute-done.3.refs_2_
  54.6 6.9 %all-to-all-start.1 = ((bf16[8,4,48,128]{3,2,1,0:T(8,128)(2,1)}), bf16[8,4,48,128]{3,2,1,0:T(8,128)(2,1)S(1)}, u32[]{:S(2)}, u32[]{:S(2)}) async-start(bf16[8,4,48,128]{3,2,1,0:T(8,128)(2,1)} %get-tuple-element.32), calls=%async_computation.1 | async-start | bytes 786432 | tf_op jit(solution)/shard_map/all_to_all | solution.py:231
  61.5 3.3 %collective-permute-start.4 = (bf16[2,8,128,128]{3,2,1,0:T(8,128)(2,1)}, bf16[2,8,128,128]{3,2,1,0:T(8,128)(2,1)S(1)}, u32[]{:S(2)}, u32[]{:S(2)}) collective-permute-start(bf16[2,8,128,128]{3,2,1,0:T(8,128)(2,1)} %pad_maximum_fusion), channel_id=1, source_target_pairs={{0,32},{32,0},{1,33},{33,1},{2,34},{34,2},{3,35},{35,3},{4,36},{36... | collective-permute-start | bytes 1572872 | tf_op jit(solution)/shard_map/ppermute | solution.py:207
  64.8 0.0 collective-permute-done.7.refs_1_
  64.8 2.2 %collective-permute-start.8 = (bf16[8,96,128]{2,1,0:T(8,128)(2,1)S(1)}, bf16[8,96,128]{2,1,0:T(8,128)(2,1)S(1)}, u32[]{:S(2)}, u32[]{:S(2)}) collective-permute-start(bf16[8,96,128]{2,1,0:T(8,128)(2,1)S(1)} %collective-permute-done.7.refs_1_), channel_id=1, source_target_pairs={{0,64},{64,128},{128,192},{192,256},{256,320},{320,384},{384,448},... | collective-permute-start | bytes 589832 | tf_op jit(solution)/shard_map/ppermute | solution.py:207
  67.0 2.4 %all-to-all-done.1.q_ref = bf16[8,4,48,128]{3,2,1,0:T(8,128)(2,1)S(1)} async-done(((bf16[8,4,48,128]{3,2,1,0:T(8,128)(2,1)}), bf16[8,4,48,128]{3,2,1,0:T(8,128)(2,1)S(1)}, u32[]{:S(2)}, u32[]{:S(2)}) %all-to-all-start.1) | async-done | bytes 393248 | tf_op jit(solution)/shard_map/all_to_all | solution.py:231
  69.5 3.5 %all-to-all-start.2 = ((bf16[8,48,768]{2,1,0:T(8,128)(2,1)}), bf16[8,48,768]{2,1,0:T(8,128)(2,1)S(1)}, u32[]{:S(2)}, u32[]{:S(2)}) async-start(bf16[8,48,768]{2,1,0:T(8,128)(2,1)} %get-tuple-element.37), calls=%async_computation.2 | async-start | bytes 1179648 | tf_op jit(solution)/shard_map/all_to_all | solution.py:231
  73.0 5.3 %collective-permute-start.5 = (bf16[8,96,128]{2,1,0:T(8,128)(2,1)S(1)}, bf16[8,96,128]{2,1,0:T(8,128)(2,1)S(1)}, u32[]{:S(2)}, u32[]{:S(2)}) collective-permute-start(bf16[8,96,128]{2,1,0:T(8,128)(2,1)S(1)} %collective-permute-done.3.refs_2_), channel_id=1, source_target_pairs={{0,448},{64,0},{128,64},{192,128},{256,192},{320,256},{384,320},{4... | collective-permute-start | bytes 589832 | tf_op jit(solution)/shard_map/ppermute | solution.py:207
  78.4 0.0 collective-permute-done.8.refs_3_
  78.4 1.9 %collective-permute-start.9 = (bf16[8,96,128]{2,1,0:T(8,128)(2,1)S(1)}, bf16[8,96,128]{2,1,0:T(8,128)(2,1)S(1)}, u32[]{:S(2)}, u32[]{:S(2)}) collective-permute-start(bf16[8,96,128]{2,1,0:T(8,128)(2,1)S(1)} %collective-permute-done.8.refs_3_), channel_id=1, source_target_pairs={{0,64},{64,128},{128,192},{192,256},{256,320},{320,384},{384,448},... | collective-permute-start | bytes 589832 | tf_op jit(solution)/shard_map/ppermute | solution.py:207
  80.3 2.0 %collective-permute-done.5.refs_4_ = bf16[8,96,128]{2,1,0:T(8,128)(2,1)S(1)} collective-permute-done((bf16[8,96,128]{2,1,0:T(8,128)(2,1)S(1)}, bf16[8,96,128]{2,1,0:T(8,128)(2,1)S(1)}, u32[]{:S(2)}, u32[]{:S(2)}) %collective-permute-start.5) | collective-permute-done | bytes 196640 | tf_op jit(solution)/shard_map/ppermute | solution.py:207
  82.3 5.3 %collective-permute-start.6 = (bf16[8,96,128]{2,1,0:T(8,128)(2,1)S(1)}, bf16[8,96,128]{2,1,0:T(8,128)(2,1)S(1)}, u32[]{:S(2)}, u32[]{:S(2)}) collective-permute-start(bf16[8,96,128]{2,1,0:T(8,128)(2,1)S(1)} %collective-permute-done.5.refs_4_), channel_id=1, source_target_pairs={{0,448},{64,0},{128,64},{192,128},{256,192},{320,256},{384,320},{4... | collective-permute-start | bytes 589832 | tf_op jit(solution)/shard_map/ppermute | solution.py:207
  87.6 0.7 shard_map.86.q_ref
  88.4 0.0 collective-permute-done.9.refs_5_
  88.4 1.9 %collective-permute-start.10 = (bf16[8,96,128]{2,1,0:T(8,128)(2,1)S(1)}, bf16[8,96,128]{2,1,0:T(8,128)(2,1)S(1)}, u32[]{:S(2)}, u32[]{:S(2)}) collective-permute-start(bf16[8,96,128]{2,1,0:T(8,128)(2,1)S(1)} %collective-permute-done.9.refs_5_), channel_id=1, source_target_pairs={{0,64},{64,128},{128,192},{192,256},{256,320},{320,384},{384,448},... | collective-permute-start | bytes 589832 | tf_op jit(solution)/shard_map/ppermute | solution.py:207
  90.3 0.0 collective-permute-done.4.far_ref
  90.3 6.8 %shard_map.87 = (f32[8,64,512]{2,1,0:T(8,128)S(1)}, f32[8,8,512]{2,1,0:T(8,128)S(1)}) custom-call(s32[5]{0:T(128)S(1)} %stack.26.pos_ref, bf16[8,48,512]{2,1,0:T(8,128)(2,1)S(1)} %shard_map.86.q_ref, bf16[2,8,128,128]{3,2,1,0:T(8,128)(2,1)S(1)} %get-tuple-element.23.keep_ref, bf16[2,8,128,128]{3,2,1,0:T(8,128)(2,1)S(1)} %collective-permute-done.1.recv_ref, ...), custom_call_target="tpu_custom_call" | custom-call | flops 6442450944 | bytes 4194304 | tf_op jit(solution)/shard_map/pallas_call | solution.py:305
  97.1 0.0 collective-permute-done.6.refs_0_
  97.1 0.0 collective-permute-done.10.refs_1_
  97.1 5.0 %shard_map.88 = bf16[8,4,64,128]{3,2,1,0:T(8,128)(2,1)} custom-call(s32[5]{0:T(128)S(1)} %stack.26.pos_ref, bf16[8,48,512]{2,1,0:T(8,128)(2,1)S(1)} %shard_map.86.q_ref, bf16[2,8,128,128]{3,2,1,0:T(8,128)(2,1)S(1)} %get-tuple-element.23.keep_ref, bf16[2,8,128,128]{3,2,1,0:T(8,128)(2,1)S(1)} %collective-permute-done.1.recv_ref, ...), custom_call_target="tpu_custom_call" | custom-call | flops 2147483648 | bytes 4194304 | tf_op jit(solution)/shard_map/pallas_call | solution.py:305
  102.1 0.0 all-to-all-done.2.w_near_ref
  102.1 5.1 %all-to-all-start.3 = ((bf16[8,4,64,128]{3,2,1,0:T(8,128)(2,1)}), bf16[8,4,64,128]{3,2,1,0:T(8,128)(2,1)S(1)}, u32[]{:S(2)}, u32[]{:S(2)}) async-start(bf16[8,4,64,128]{3,2,1,0:T(8,128)(2,1)} %shard_map.88), calls=%async_computation.3 | async-start | bytes 1048576 | tf_op jit(solution)/shard_map/all_to_all | solution.py:231
  107.2 2.0 %collective-permute-start.11 = (bf16[8,48,768]{2,1,0:T(8,128)(2,1)S(1)}, bf16[8,48,768]{2,1,0:T(8,128)(2,1)S(1)}, u32[]{:S(2)}, u32[]{:S(2)}) collective-permute-start(bf16[8,48,768]{2,1,0:T(8,128)(2,1)S(1)} %all-to-all-done.2.w_near_ref), channel_id=1, source_target_pairs={{0,16},{16,0},{1,17},{17,1},{2,18},{18,2},{3,19},{19,3},{4,20},{20... | collective-permute-start | bytes 1769480 | tf_op jit(solution)/shard_map/ppermute | solution.py:207
  109.2 7.4 %all-to-all-done.3.p_ref = bf16[8,4,64,128]{3,2,1,0:T(8,128)(2,1)S(1)} async-done(((bf16[8,4,64,128]{3,2,1,0:T(8,128)(2,1)}), bf16[8,4,64,128]{3,2,1,0:T(8,128)(2,1)S(1)}, u32[]{:S(2)}, u32[]{:S(2)}) %all-to-all-start.3) | async-done | bytes 524320 | tf_op jit(solution)/shard_map/all_to_all | solution.py:231
  116.6 1.4 %shard_map.89 = bf16[8,64,128]{2,1,0:T(8,128)(2,1)} custom-call(s32[5]{0:T(128)S(1)} %stack.26.pos_ref, bf16[8,4,64,128]{3,2,1,0:T(8,128)(2,1)S(1)} %all-to-all-done.3.p_ref, f32[2,4,48,128]{3,2,1,0:T(8,128)S(1)} %get-tuple-element.39.gate_ref), custom_call_target="tpu_custom_call" | custom-call | tf_op jit(solution)/shard_map/pallas_call | solution.py:221
  118.0 6.3 %all-to-all-start.4 = ((bf16[8,64,128]{2,1,0:T(8,128)(2,1)}), bf16[8,64,128]{2,1,0:T(8,128)(2,1)S(1)}, u32[]{:S(2)}, u32[]{:S(2)}) async-start(bf16[8,64,128]{2,1,0:T(8,128)(2,1)} %shard_map.89), calls=%async_computation.4 | async-start | bytes 262144 | tf_op jit(solution)/shard_map/all_to_all | solution.py:231
  124.3 0.0 collective-permute-done.11.w_far_ref
  124.3 7.9 %all-to-all-done.4.g_ref = bf16[8,64,128]{2,1,0:T(8,128)(2,1)S(1)} async-done(((bf16[8,64,128]{2,1,0:T(8,128)(2,1)}), bf16[8,64,128]{2,1,0:T(8,128)(2,1)S(1)}, u32[]{:S(2)}, u32[]{:S(2)}) %all-to-all-start.4) | async-done | bytes 131104 | tf_op jit(solution)/shard_map/all_to_all | solution.py:231
  132.2 1.3 shard_map.90
  (3 shorter events, 0.1 us)
Async XLA Ops:
  0.0 13.3 %copy-start = (bf16[1,128,4096]{2,1,0:T(8,128)(2,1)S(1)}, bf16[1,128,4096]{2,1,0:T(8,128)(2,1)}, u32[]{:S(2)}) copy-start(bf16[1,128,4096]{2,1,0:T(8,128)(2,1)} %b_ref.1) | copy-start | bytes 3145732
  2.3 34.4 %all-to-all-start = ((bf16[8,64,768]{2,1,0:T(8,128)(2,1)}), bf16[8,64,768]{2,1,0:T(8,128)(2,1)S(1)}, u32[]{:S(2)}, u32[]{:S(2)}) async-start(bf16[8,64,768]{2,1,0:T(8,128)(2,1)} %shard_map.82), calls=%async_computation | async-start | bytes 1572864 | tf_op jit(solution)/shard_map/all_to_all | solution.py:231
  13.3 4.7 %copy-start.1 = (bf16[768,192]{0,1:T(8,128)(2,1)S(1)}, bf16[768,192]{0,1:T(8,128)(2,1)}, u32[]{:S(2)}) copy-start(bf16[768,192]{0,1:T(8,128)(2,1)} %param.13) | copy-start | bytes 884740
  13.3 4.7 %copy-start.2 = (bf16[48,768]{1,0:T(8,128)(2,1)S(1)}, bf16[48,768]{1,0:T(8,128)(2,1)}, u32[]{:S(2)}) copy-start(bf16[48,768]{1,0:T(8,128)(2,1)} %param.15) | copy-start | bytes 221188
  15.1 7.6 %collective-permute-start.1 = (bf16[2,8,128,128]{3,2,1,0:T(8,128)(2,1)S(1)}, bf16[2,8,128,128]{3,2,1,0:T(8,128)(2,1)S(1)}, u32[]{:S(2)}, u32[]{:S(2)}) collective-permute-start(bf16[2,8,128,128]{3,2,1,0:T(8,128)(2,1)S(1)} %get-tuple-element.24), channel_id=1, source_target_pairs={{0,16},{16,0},{1,17},{17,1},{2,18},{18,2},{3,19},{19,3},{4,20},{20... | collective-permute-start | bytes 1572872 | tf_op jit(solution)/shard_map/ppermute | solution.py:207
  18.0 13.6 %collective-permute-start = (bf16[240,768]{1,0:T(8,128)(2,1)S(1)}, bf16[240,768]{1,0:T(8,128)(2,1)S(1)}, u32[]{:S(2)}, u32[]{:S(2)}) collective-permute-start(bf16[240,768]{1,0:T(8,128)(2,1)S(1)} %pad_maximum_fusion.1.own_ref), channel_id=1, source_target_pairs={{0,1},{1,0},{2,3},{3,2},{4,5},{5,4},{6,7},{7,6},{8,9},{9,8},{10,11... | collective-permute-start | bytes 1105928 | tf_op jit(solution)/shard_map/ppermute | solution.py:207
  39.6 7.2 %collective-permute-start.2 = (bf16[4,96,128]{2,1,0:T(8,128)(2,1)S(1)}, bf16[4,96,128]{2,1,0:T(8,128)(2,1)S(1)}, u32[]{:S(2)}, u32[]{:S(2)}) collective-permute-start(bf16[4,96,128]{2,1,0:T(8,128)(2,1)S(1)} %get-tuple-element.30), channel_id=1, source_target_pairs={{0,1},{1,0},{2,3},{3,2},{4,5},{5,4},{6,7},{7,6},{8,9},{9,8},{10,11... | collective-permute-start | bytes 294920 | tf_op jit(solution)/shard_map/ppermute | solution.py:207
  46.9 7.7 %collective-permute-start.3 = (bf16[8,96,128]{2,1,0:T(8,128)(2,1)S(1)}, bf16[8,96,128]{2,1,0:T(8,128)(2,1)S(1)}, u32[]{:S(2)}, u32[]{:S(2)}) collective-permute-start(bf16[8,96,128]{2,1,0:T(8,128)(2,1)S(1)} %shard_map.85.refs_0_), channel_id=1, source_target_pairs={{0,448},{64,0},{128,64},{192,128},{256,192},{320,256},{384,320},{4... | collective-permute-start | bytes 589832 | tf_op jit(solution)/shard_map/ppermute | solution.py:207
  52.0 12.8 %collective-permute-start.7 = (bf16[8,96,128]{2,1,0:T(8,128)(2,1)S(1)}, bf16[8,96,128]{2,1,0:T(8,128)(2,1)S(1)}, u32[]{:S(2)}, u32[]{:S(2)}) collective-permute-start(bf16[8,96,128]{2,1,0:T(8,128)(2,1)S(1)} %shard_map.85.refs_0_), channel_id=1, source_target_pairs={{0,64},{64,128},{128,192},{192,256},{256,320},{320,384},{384,448},... | collective-permute-start | bytes 589832 | tf_op jit(solution)/shard_map/ppermute | solution.py:207
  54.6 14.9 %all-to-all-start.1 = ((bf16[8,4,48,128]{3,2,1,0:T(8,128)(2,1)}), bf16[8,4,48,128]{3,2,1,0:T(8,128)(2,1)S(1)}, u32[]{:S(2)}, u32[]{:S(2)}) async-start(bf16[8,4,48,128]{3,2,1,0:T(8,128)(2,1)} %get-tuple-element.32), calls=%async_computation.1 | async-start | bytes 786432 | tf_op jit(solution)/shard_map/all_to_all | solution.py:231
  61.5 28.8 %collective-permute-start.4 = (bf16[2,8,128,128]{3,2,1,0:T(8,128)(2,1)}, bf16[2,8,128,128]{3,2,1,0:T(8,128)(2,1)S(1)}, u32[]{:S(2)}, u32[]{:S(2)}) collective-permute-start(bf16[2,8,128,128]{3,2,1,0:T(8,128)(2,1)} %pad_maximum_fusion), channel_id=1, source_target_pairs={{0,32},{32,0},{1,33},{33,1},{2,34},{34,2},{3,35},{35,3},{4,36},{36... | collective-permute-start | bytes 1572872 | tf_op jit(solution)/shard_map/ppermute | solution.py:207
  64.8 13.5 %collective-permute-start.8 = (bf16[8,96,128]{2,1,0:T(8,128)(2,1)S(1)}, bf16[8,96,128]{2,1,0:T(8,128)(2,1)S(1)}, u32[]{:S(2)}, u32[]{:S(2)}) collective-permute-start(bf16[8,96,128]{2,1,0:T(8,128)(2,1)S(1)} %collective-permute-done.7.refs_1_), channel_id=1, source_target_pairs={{0,64},{64,128},{128,192},{192,256},{256,320},{320,384},{384,448},... | collective-permute-start | bytes 589832 | tf_op jit(solution)/shard_map/ppermute | solution.py:207
  69.5 32.6 %all-to-all-start.2 = ((bf16[8,48,768]{2,1,0:T(8,128)(2,1)}), bf16[8,48,768]{2,1,0:T(8,128)(2,1)S(1)}, u32[]{:S(2)}, u32[]{:S(2)}) async-start(bf16[8,48,768]{2,1,0:T(8,128)(2,1)} %get-tuple-element.37), calls=%async_computation.2 | async-start | bytes 1179648 | tf_op jit(solution)/shard_map/all_to_all | solution.py:231
  73.0 9.3 %collective-permute-start.5 = (bf16[8,96,128]{2,1,0:T(8,128)(2,1)S(1)}, bf16[8,96,128]{2,1,0:T(8,128)(2,1)S(1)}, u32[]{:S(2)}, u32[]{:S(2)}) collective-permute-start(bf16[8,96,128]{2,1,0:T(8,128)(2,1)S(1)} %collective-permute-done.3.refs_2_), channel_id=1, source_target_pairs={{0,448},{64,0},{128,64},{192,128},{256,192},{320,256},{384,320},{4... | collective-permute-start | bytes 589832 | tf_op jit(solution)/shard_map/ppermute | solution.py:207
  78.4 10.0 %collective-permute-start.9 = (bf16[8,96,128]{2,1,0:T(8,128)(2,1)S(1)}, bf16[8,96,128]{2,1,0:T(8,128)(2,1)S(1)}, u32[]{:S(2)}, u32[]{:S(2)}) collective-permute-start(bf16[8,96,128]{2,1,0:T(8,128)(2,1)S(1)} %collective-permute-done.8.refs_3_), channel_id=1, source_target_pairs={{0,64},{64,128},{128,192},{192,256},{256,320},{320,384},{384,448},... | collective-permute-start | bytes 589832 | tf_op jit(solution)/shard_map/ppermute | solution.py:207
  82.3 14.8 %collective-permute-start.6 = (bf16[8,96,128]{2,1,0:T(8,128)(2,1)S(1)}, bf16[8,96,128]{2,1,0:T(8,128)(2,1)S(1)}, u32[]{:S(2)}, u32[]{:S(2)}) collective-permute-start(bf16[8,96,128]{2,1,0:T(8,128)(2,1)S(1)} %collective-permute-done.5.refs_4_), channel_id=1, source_target_pairs={{0,448},{64,0},{128,64},{192,128},{256,192},{320,256},{384,320},{4... | collective-permute-start | bytes 589832 | tf_op jit(solution)/shard_map/ppermute | solution.py:207
  88.4 8.8 %collective-permute-start.10 = (bf16[8,96,128]{2,1,0:T(8,128)(2,1)S(1)}, bf16[8,96,128]{2,1,0:T(8,128)(2,1)S(1)}, u32[]{:S(2)}, u32[]{:S(2)}) collective-permute-start(bf16[8,96,128]{2,1,0:T(8,128)(2,1)S(1)} %collective-permute-done.9.refs_5_), channel_id=1, source_target_pairs={{0,64},{64,128},{128,192},{192,256},{256,320},{320,384},{384,448},... | collective-permute-start | bytes 589832 | tf_op jit(solution)/shard_map/ppermute | solution.py:207
  102.1 14.4 %all-to-all-start.3 = ((bf16[8,4,64,128]{3,2,1,0:T(8,128)(2,1)}), bf16[8,4,64,128]{3,2,1,0:T(8,128)(2,1)S(1)}, u32[]{:S(2)}, u32[]{:S(2)}) async-start(bf16[8,4,64,128]{3,2,1,0:T(8,128)(2,1)} %shard_map.88), calls=%async_computation.3 | async-start | bytes 1048576 | tf_op jit(solution)/shard_map/all_to_all | solution.py:231
  107.2 17.1 %collective-permute-start.11 = (bf16[8,48,768]{2,1,0:T(8,128)(2,1)S(1)}, bf16[8,48,768]{2,1,0:T(8,128)(2,1)S(1)}, u32[]{:S(2)}, u32[]{:S(2)}) collective-permute-start(bf16[8,48,768]{2,1,0:T(8,128)(2,1)S(1)} %all-to-all-done.2.w_near_ref), channel_id=1, source_target_pairs={{0,16},{16,0},{1,17},{17,1},{2,18},{18,2},{3,19},{19,3},{4,20},{20... | collective-permute-start | bytes 1769480 | tf_op jit(solution)/shard_map/ppermute | solution.py:207
  118.0 14.2 %all-to-all-start.4 = ((bf16[8,64,128]{2,1,0:T(8,128)(2,1)}), bf16[8,64,128]{2,1,0:T(8,128)(2,1)S(1)}, u32[]{:S(2)}, u32[]{:S(2)}) async-start(bf16[8,64,128]{2,1,0:T(8,128)(2,1)} %shard_map.89), calls=%async_computation.4 | async-start | bytes 262144 | tf_op jit(solution)/shard_map/all_to_all | solution.py:231
